TPU v7x, 32 devices: a whole 2x2x4 slice. The times are simulated.
32 devices in a mesh: row: 8 (over z, y), col: 4 (over x, core).
Axes of the slice: x: 2, y: 2, z: 4, core: 2. Of those that a mesh axis runs over, the one named last changes fastest.
Arguments:
- blocks: float32 [8, 4, 8, 128, 128], P('row', 'col'), may hold values from -1.2 to 1.2
- block_rows: int32 [8, 4, 8], P('row', 'col'), may hold values from -1 to 63, as said below
- block_cols: int32 [8, 4, 8], P('row', 'col'), may hold values from -1 to 127, as said below
Outputs:
- square_part: float32 [8, 4, 8, 128, 128], P('row', 'col')
Inputs may be any that keep to these rules, and one draw needn't show every extreme that they name: Empty slots have -1 in block_rows and block_cols alike; a used slot has a block row below 64; no block is listed twice in one tile. At most 4 used slots of one tile share a block row, and some tile has a block row with exactly 4. Some tile uses all 8 slots, and some tile has empty slots. `block_cols`: the two lists describe the same slots; a used slot has a block column below 128.
All inputs are finite; a program needn't handle non-finite values.
Results may differ from a plain program's by a relative error of at most 0.0003.
Values sent between devices are 32-bit elements; how exact they have to be, the bound alone decides.
No kernel may reach another device: no remote copies, remote signals or barrier semaphores. Data moves between devices by JAX's collectives and lax.ppermute only.
A program may use at most 64 MiB of HBM per device.

v0:
```python
import jax
import jax.numpy as jnp
from jax import lax
from jax.sharding import PartitionSpec as P

NBLK = 512
ACT = 2
SECTIONS = 4


def from_root(x, axis, root):
    mine = lax.axis_index(axis) == root
    return lax.psum(jnp.where(mine, x, jnp.zeros_like(x)), axis)


def from_partner(x, axis, bit):
    return lax.ppermute(x, axis, [(i, i ^ 1 << bit) for i in range(lax.axis_size(axis))])


def shifted(value, axis, steps):
    count = lax.axis_size(axis)
    pairs = [(source, (source + steps) % count) for source in range(count)]
    return lax.ppermute(value, axis, pairs)


def section_product(panel, pair, out_rows, out_cols, depth):
    panel_vals, panel_rows, panel_cols = panel
    pair_vals, pair_inner, pair_cols = pair
    panel_iota = jnp.arange(panel_rows.shape[0], dtype=jnp.int32)
    pair_iota = jnp.arange(pair_inner.shape[0], dtype=jnp.int32)
    depth_iota = jnp.arange(depth, dtype=jnp.int32)
    panel_live = panel_rows >= 0
    earlier = (
        (panel_rows[None, :] == panel_rows[:, None])
        & panel_live[None, :]
        & (panel_iota[None, :] < panel_iota[:, None])
    )
    within = jnp.sum(earlier.astype(jnp.int32), axis=1)
    picked = (panel_rows[None, None, :] == out_rows[:, None, None]) & (
        within[None, None, :] == depth_iota[None, :, None]
    )
    picked = picked & panel_live[None, None, :] & (out_rows >= 0)[:, None, None]
    picked_int = picked.astype(jnp.int32)
    panel_slot = jnp.sum(picked_int * panel_iota[None, None, :], axis=2)
    found = jnp.sum(picked_int, axis=2) > 0
    inner = jnp.sum(picked_int * panel_cols[None, None, :], axis=2)
    matched = (pair_inner[None, None, :] == inner[:, :, None]) & (
        pair_cols[None, None, :] == out_cols[:, None, None]
    )
    matched = matched & (pair_inner >= 0)[None, None, :] & found[:, :, None]
    matched_int = matched.astype(jnp.int32)
    pair_slot = jnp.sum(matched_int * pair_iota[None, None, :], axis=2)
    weight = (jnp.sum(matched_int, axis=2) > 0).astype(jnp.float32)
    left = panel_vals[panel_slot] * weight[:, :, None, None]
    right = pair_vals[pair_slot]
    return jnp.einsum(
        "tqij,tqjk->tik",
        left,
        right,
        precision=lax.Precision.HIGHEST,
        preferred_element_type=jnp.float32,
    )


def make_pair(first, second, row_span):
    inner = jnp.concatenate([first[1], jnp.where(second[1] >= 0, second[1] + row_span, -1)])
    return (jnp.concatenate([first[0], second[0]]), inner, jnp.concatenate([first[2], second[2]]))


def order_pair(mine, other, is_even, row_span):
    first = tuple((jnp.where(is_even, one, two) for one, two in zip(mine, other)))
    second = tuple((jnp.where(is_even, two, one) for one, two in zip(mine, other)))
    return make_pair(first, second, row_span)


def fetch_panel(tile, row_index, col_count, section):
    root = (row_index // 2 + section) % col_count
    return (
        from_root(tile[0], "col", root),
        from_root(tile[1], "col", root),
        from_root(tile[2], "col", root),
    )


def body(blocks, block_rows, block_cols):
    tile = (blocks[0, 0], block_rows[0, 0], block_cols[0, 0])
    row_count = lax.axis_size("row")
    col_count = lax.axis_size("col")
    row_span = NBLK // row_count
    row_index = lax.axis_index("row")
    is_even = row_index % 2 == 0
    depth = 2 * ACT
    total = jnp.zeros(blocks.shape[2:], jnp.float32)
    partner = from_partner((tile[0], tile[1], tile[2]), "row", 0)
    start_pair = order_pair(tile, partner, is_even, row_span)
    current = start_pair
    for section in range(SECTIONS):
        panel = fetch_panel(tile, row_index, col_count, section)
        if section > 0:
            current = shifted((current[0], current[1], current[2]), "row", -2)
        total = total + section_product(panel, current, tile[1], tile[2], depth)
    return total[None, None]


def solution(mesh):
    return jax.shard_map(
        body,
        mesh=mesh,
        in_specs=(P("row", "col", None, None, None), P("row", "col", None), P("row", "col", None)),
        out_specs=P("row", "col", None, None, None),
        check_vma=False,
    )
```

profile of v0, /device:TPU:0, one launch (start us, length us, event | category | flops | bytes accessed | tf_op | source)
XLA Modules:
  0.0 144.5 jit_solution(15429693145186713196)
XLA Ops:
  6.5 3.0 %collective-permute-start.2 = (f32[8,128,128]{2,1,0:T(8,128)}, f32[8,128,128]{2,1,0:T(8,128)S(1)}, u32[]{:S(2)}, u32[]{:S(2)}) collective-permute-start(f32[8,128,128]{2,1,0:T(8,128)} %bitcast.96), channel_id=1, source_target_pairs={{0,4},{4,0},{8,12},{12,8},{16,20},{20,16},{24,28},{28,24},{1,5},{5... | collective-permute-start | bytes 1572872 | tf_op jit(solution)/shard_map/ppermute | solution.py:17
  9.5 2.0 %collective-permute-start.1 = (s32[8]{0:T(128)}, s32[8]{0:T(128)S(1)}, u32[]{:S(2)}, u32[]{:S(2)}) collective-permute-start(s32[8]{0:T(128)} %bitcast.99), channel_id=1, source_target_pairs={{0,4},{4,0},{8,12},{12,8},{16,20},{20,16},{24,28},{28,24},{1,5},{5... | collective-permute-start | bytes 104 | tf_op jit(solution)/shard_map/ppermute | solution.py:17
  12.2 9.5 %collective-permute-done = s32[8]{0:T(128)S(1)} collective-permute-done((s32[8]{0:T(128)}, s32[8]{0:T(128)S(1)}, u32[]{:S(2)}, u32[]{:S(2)}) %collective-permute-start) | collective-permute-done | bytes 64 | tf_op jit(solution)/shard_map/ppermute | solution.py:17
  23.0 5.1 %all-reduce = (s32[8]{0:T(128)S(1)}, s32[8]{0:T(128)S(1)}, s32[8]{0:T(128)S(1)}, s32[8]{0:T(128)S(1)}, s32[8]{0:T(128)S(1)}, /*index=5*/s32[8]{0:T(128)S(1)}, s32[8]{0:T(128)S(1)}, s32[8]{0:T(128)S(1)}) all-reduce(s32[8]{0:T(128)S(1)} %get-tuple-element.71, s32[8]{0:T(128)S(1)} %get-tuple-element.67, ...), channel_id=1, replica_groups=mesh['row'=8,'col'=4] {'col'}, use_global_device_ids=true, to_apply=%region_28.29 | all-reduce | flops 64 | bytes 512 | tf_op jit(solution)/shard_map/psum | solution.py:13
  30.5 3.6 %collective-permute-start.4 = (s32[16]{0:T(128)S(1)}, s32[16]{0:T(128)S(1)}, u32[]{:S(2)}, u32[]{:S(2)}) collective-permute-start(s32[16]{0:T(128)S(1)} %pad_add_fusion.1), channel_id=1, source_target_pairs={{0,24},{4,28},{8,0},{12,4},{16,8},{20,12},{24,16},{28,20},{1,25},{... | collective-permute-start | bytes 200 | tf_op jit(solution)/shard_map/ppermute | solution.py:23
  35.4 4.0 %collective-permute-start.7 = (s32[16]{0:T(128)S(1)}, s32[16]{0:T(128)S(1)}, u32[]{:S(2)}, u32[]{:S(2)}) collective-permute-start(s32[16]{0:T(128)S(1)} %collective-permute-done.4), channel_id=1, source_target_pairs={{0,24},{4,28},{8,0},{12,4},{16,8},{20,12},{24,16},{28,20},{1,25},{... | collective-permute-start | bytes 200 | tf_op jit(solution)/shard_map/ppermute | solution.py:23
  40.7 4.0 %collective-permute-start.10 = (s32[16]{0:T(128)S(1)}, s32[16]{0:T(128)S(1)}, u32[]{:S(2)}, u32[]{:S(2)}) collective-permute-start(s32[16]{0:T(128)S(1)} %collective-permute-done.7), channel_id=1, source_target_pairs={{0,24},{4,28},{8,0},{12,4},{16,8},{20,12},{24,16},{28,20},{1,25},{... | collective-permute-start | bytes 200 | tf_op jit(solution)/shard_map/ppermute | solution.py:23
  47.1 2.4 %broadcast_select_fusion = (f32[8,128,128]{2,1,0:T(8,128)}, f32[8,128,128]{2,1,0:T(8,128)}, f32[8,128,128]{2,1,0:T(8,128)S(1)}, f32[8,128,128]{2,1,0:T(8,128)S(1...) fusion(pred[]{:T(512)S(6)} %eq.371, f32[1,1,8,128,128]{4,3,2,1,0:T(8,128)} %param.3, pred[]{:T(512)S(6)} %eq.329, ...), kind=kLoop, calls=%fused_computation.29 | loop fusion | flops 786432 | bytes 4194309 | tf_op jit(solution)/shard_map/jit(_where)/select_n | solution.py:13
  49.6 4.1 %collective-permute-start.5 = (f32[16,128,128]{2,1,0:T(8,128)S(1)}, f32[16,128,128]{2,1,0:T(8,128)S(1)}, u32[]{:S(2)}, u32[]{:S(2)}) collective-permute-start(f32[16,128,128]{2,1,0:T(8,128)S(1)} %pad_maximum_fusion), channel_id=1, source_target_pairs={{0,24},{4,28},{8,0},{12,4},{16,8},{20,12},{24,16},{28,20},{1,25},{... | collective-permute-start | bytes 3145736 | tf_op jit(solution)/shard_map/ppermute | solution.py:23
  54.4 18.4 %collective-permute-done.5 = f32[16,128,128]{2,1,0:T(8,128)S(1)} collective-permute-done((f32[16,128,128]{2,1,0:T(8,128)S(1)}, f32[16,128,128]{2,1,0:T(8,128)S(1)}, u32[]{:S(2)}, u32[]{:S(2)}) %collective-permute-start.5) | collective-permute-done | bytes 1048608 | tf_op jit(solution)/shard_map/ppermute | solution.py:23
  72.8 4.3 %collective-permute-start.8 = (f32[16,128,128]{2,1,0:T(8,128)S(1)}, f32[16,128,128]{2,1,0:T(8,128)}, u32[]{:S(2)}, u32[]{:S(2)}) collective-permute-start(f32[16,128,128]{2,1,0:T(8,128)S(1)} %collective-permute-done.5), channel_id=1, source_target_pairs={{0,24},{4,28},{8,0},{12,4},{16,8},{20,12},{24,16},{28,20},{1,25},{... | collective-permute-start | bytes 3145736 | tf_op jit(solution)/shard_map/ppermute | solution.py:23
  78.4 17.4 %collective-permute-done.8 = f32[16,128,128]{2,1,0:T(8,128)} collective-permute-done((f32[16,128,128]{2,1,0:T(8,128)S(1)}, f32[16,128,128]{2,1,0:T(8,128)}, u32[]{:S(2)}, u32[]{:S(2)}) %collective-permute-start.8) | collective-permute-done | bytes 1048608 | tf_op jit(solution)/shard_map/ppermute | solution.py:23
  95.8 4.4 %collective-permute-start.11 = (f32[16,128,128]{2,1,0:T(8,128)}, f32[16,128,128]{2,1,0:T(8,128)}, u32[]{:S(2)}, u32[]{:S(2)}) collective-permute-start(f32[16,128,128]{2,1,0:T(8,128)} %collective-permute-done.8), channel_id=1, source_target_pairs={{0,24},{4,28},{8,0},{12,4},{16,8},{20,12},{24,16},{28,20},{1,25},{... | collective-permute-start | bytes 3145736 | tf_op jit(solution)/shard_map/ppermute | solution.py:23
  100.2 2.0 %gather_fusion.1 = f32[32,128,128]{2,1,0:T(8,128)} fusion(f32[16,128,128]{2,1,0:T(8,128)S(1)} %pad_maximum_fusion, s32[1024]{0:T(1024)S(1)} %pad_clamp_fusion.6), kind=kCustom, calls=%fused_computation.1 | custom fusion | bytes 4194432 | tf_op jit(solution)/shard_map/gather | solution.py:55
  104.1 3.1 %gather_fusion = f32[32,128,128]{2,1,0:T(8,128)} fusion(f32[8,128,128]{2,1,0:T(8,128)} %get-tuple-element.42, s32[1024]{0:T(1024)S(1)} %pad_clamp_fusion.7), kind=kCustom, calls=%fused_computation | custom fusion | bytes 4194432 | tf_op jit(solution)/shard_map/gather | solution.py:54
  107.1 2.0 %gather_fusion.2 = f32[32,128,128]{2,1,0:T(8,128)} fusion(f32[8,128,128]{2,1,0:T(8,128)S(1)} %copy-done.2, s32[1024]{0:T(1024)S(1)} %pad_clamp_fusion.5), kind=kCustom, calls=%fused_computation.2 | custom fusion | bytes 4194432 | tf_op jit(solution)/shard_map/gather | solution.py:54
  109.2 2.0 %gather_fusion.4 = f32[32,128,128]{2,1,0:T(8,128)} fusion(f32[8,128,128]{2,1,0:T(8,128)S(1)} %copy-done.1, s32[1024]{0:T(1024)S(1)} %pad_clamp_fusion.3), kind=kCustom, calls=%fused_computation.4 | custom fusion | bytes 4194432 | tf_op jit(solution)/shard_map/gather | solution.py:54
  111.9 3.3 %gather_fusion.3 = f32[32,128,128]{2,1,0:T(8,128)} fusion(f32[16,128,128]{2,1,0:T(8,128)} %copy-done.5, s32[1024]{0:T(1024)S(1)} %pad_clamp_fusion.4), kind=kCustom, calls=%fused_computation.3 | custom fusion | bytes 4194432 | tf_op jit(solution)/shard_map/gather | solution.py:55
  115.2 4.6 %fusion.8 = f32[8,128,128]{2,1,0:T(8,128)S(1)} fusion(f32[8,4,128,128]{3,2,1,0:T(8,128)} %bitcast.94, f32[8,4,128,128]{3,2,1,0:T(8,128)} %bitcast.95, f32[8,4]{1,0:T(8,128)S(1)} %copy.21), kind=kOutput, calls=%fused_computation.16 | convolution fusion | flops 805830656 | bytes 4718720 | tf_op jit(solution)/shard_map/tqij,tqjk->tik/dot_general | solution.py:56
  119.8 2.3 %fusion.29 = f32[8,128,128]{2,1,0:T(8,128)S(1)} fusion(f32[8,128,128]{2,1,0:T(8,128)S(1)} %fusion.8, f32[8,4,128,128]{3,2,1,0:T(8,128)S(1)} %bitcast.91, f32[8,4,128,128]{3,2,1,0:T(8,128)S(1)} %bitcast.90, f32[8,4]{1,0:T(8,128)S(1)} %copy.24), kind=kOutput, calls=%fused_computation.23 | convolution fusion | flops 805961728 | bytes 5243008 | tf_op jit(solution)/shard_map/tqij,tqjk->tik/dot_general | solution.py:56
  122.1 3.3 %gather_fusion.5 = f32[32,128,128]{2,1,0:T(8,128)} fusion(f32[16,128,128]{2,1,0:T(8,128)} %collective-permute-done.8, s32[1024]{0:T(1024)S(1)} %pad_clamp_fusion.2), kind=kCustom, calls=%fused_computation.5 | custom fusion | bytes 4194432 | tf_op jit(solution)/shard_map/gather | solution.py:55
  125.3 4.5 %fusion.26 = f32[8,128,128]{2,1,0:T(8,128)S(1)} fusion(f32[8,128,128]{2,1,0:T(8,128)S(1)} %fusion.29, f32[8,4,128,128]{3,2,1,0:T(8,128)} %bitcast.93, f32[8,4,128,128]{3,2,1,0:T(8,128)} %bitcast.89, f32[8,4]{1,0:T(8,128)S(1)} %copy.27), kind=kOutput, calls=%fused_computation.22 | convolution fusion | flops 805961728 | bytes 5243008 | tf_op jit(solution)/shard_map/tqij,tqjk->tik/dot_general | solution.py:56
  129.8 3.3 %gather_fusion.7 = f32[32,128,128]{2,1,0:T(8,128)} fusion(f32[16,128,128]{2,1,0:T(8,128)} %collective-permute-done.11, s32[1024]{0:T(1024)S(1)} %pad_clamp_fusion), kind=kCustom, calls=%fused_computation.7 | custom fusion | bytes 4194432 | tf_op jit(solution)/shard_map/gather | solution.py:55
  133.0 4.6 %fusion.23 = f32[1,1,8,128,128]{4,3,2,1,0:T(8,128)} fusion(f32[8,128,128]{2,1,0:T(8,128)S(1)} %fusion.26, f32[8,4,128,128]{3,2,1,0:T(8,128)} %bitcast.92, f32[8,4,128,128]{3,2,1,0:T(8,128)S(1)} %bitcast.88, f32[8,4]{1,0:T(8,128)S(1)} %copy.30), kind=kOutput, calls=%fused_computation.21 | convolution fusion | flops 805961728 | bytes 5243008 | tf_op jit(solution)/shard_map/tqij,tqjk->tik/dot_general | solution.py:56
  (99 shorter events, 13.7 us)
Async XLA Ops:
  6.5 97.5 %all-reduce.4.cloned.1.call-start = ((), (), s32[]{:S(2)}) async-start(), calls=%async_computation | async-start | bytes 4194304 | tf_op jit(solution)/shard_map/psum | solution.py:13
  6.5 40.6 %collective-permute-start.2 = (f32[8,128,128]{2,1,0:T(8,128)}, f32[8,128,128]{2,1,0:T(8,128)S(1)}, u32[]{:S(2)}, u32[]{:S(2)}) collective-permute-start(f32[8,128,128]{2,1,0:T(8,128)} %bitcast.96), channel_id=1, source_target_pairs={{0,4},{4,0},{8,12},{12,8},{16,20},{20,16},{24,28},{28,24},{1,5},{5... | collective-permute-start | bytes 1572872 | tf_op jit(solution)/shard_map/ppermute | solution.py:17
  9.5 12.2 %collective-permute-start = (s32[8]{0:T(128)}, s32[8]{0:T(128)S(1)}, u32[]{:S(2)}, u32[]{:S(2)}) collective-permute-start(s32[8]{0:T(128)} %bitcast.97), channel_id=1, source_target_pairs={{0,4},{4,0},{8,12},{12,8},{16,20},{20,16},{24,28},{28,24},{1,5},{5... | collective-permute-start | bytes 104 | tf_op jit(solution)/shard_map/ppermute | solution.py:17
  9.5 12.8 %collective-permute-start.1 = (s32[8]{0:T(128)}, s32[8]{0:T(128)S(1)}, u32[]{:S(2)}, u32[]{:S(2)}) collective-permute-start(s32[8]{0:T(128)} %bitcast.99), channel_id=1, source_target_pairs={{0,4},{4,0},{8,12},{12,8},{16,20},{20,16},{24,28},{28,24},{1,5},{5... | collective-permute-start | bytes 104 | tf_op jit(solution)/shard_map/ppermute | solution.py:17
  30.5 4.9 %collective-permute-start.4 = (s32[16]{0:T(128)S(1)}, s32[16]{0:T(128)S(1)}, u32[]{:S(2)}, u32[]{:S(2)}) collective-permute-start(s32[16]{0:T(128)S(1)} %pad_add_fusion.1), channel_id=1, source_target_pairs={{0,24},{4,28},{8,0},{12,4},{16,8},{20,12},{24,16},{28,20},{1,25},{... | collective-permute-start | bytes 200 | tf_op jit(solution)/shard_map/ppermute | solution.py:23
  34.4 5.1 %collective-permute-start.3 = (s32[16]{0:T(128)S(1)}, s32[16]{0:T(128)S(1)}, u32[]{:S(2)}, u32[]{:S(2)}) collective-permute-start(s32[16]{0:T(128)S(1)} %get-tuple-element.47), channel_id=1, source_target_pairs={{0,24},{4,28},{8,0},{12,4},{16,8},{20,12},{24,16},{28,20},{1,25},{... | collective-permute-start | bytes 200 | tf_op jit(solution)/shard_map/ppermute | solution.py:23
  35.4 5.3 %collective-permute-start.7 = (s32[16]{0:T(128)S(1)}, s32[16]{0:T(128)S(1)}, u32[]{:S(2)}, u32[]{:S(2)}) collective-permute-start(s32[16]{0:T(128)S(1)} %collective-permute-done.4), channel_id=1, source_target_pairs={{0,24},{4,28},{8,0},{12,4},{16,8},{20,12},{24,16},{28,20},{1,25},{... | collective-permute-start | bytes 200 | tf_op jit(solution)/shard_map/ppermute | solution.py:23
  39.4 5.3 %collective-permute-start.6 = (s32[16]{0:T(128)S(1)}, s32[16]{0:T(128)S(1)}, u32[]{:S(2)}, u32[]{:S(2)}) collective-permute-start(s32[16]{0:T(128)S(1)} %collective-permute-done.3), channel_id=1, source_target_pairs={{0,24},{4,28},{8,0},{12,4},{16,8},{20,12},{24,16},{28,20},{1,25},{... | collective-permute-start | bytes 200 | tf_op jit(solution)/shard_map/ppermute | solution.py:23
  40.7 5.3 %collective-permute-start.10 = (s32[16]{0:T(128)S(1)}, s32[16]{0:T(128)S(1)}, u32[]{:S(2)}, u32[]{:S(2)}) collective-permute-start(s32[16]{0:T(128)S(1)} %collective-permute-done.7), channel_id=1, source_target_pairs={{0,24},{4,28},{8,0},{12,4},{16,8},{20,12},{24,16},{28,20},{1,25},{... | collective-permute-start | bytes 200 | tf_op jit(solution)/shard_map/ppermute | solution.py:23
  44.8 32.3 %collective-permute-start.9 = (s32[16]{0:T(128)S(1)}, s32[16]{0:T(128)S(1)}, u32[]{:S(2)}, u32[]{:S(2)}) collective-permute-start(s32[16]{0:T(128)S(1)} %collective-permute-done.6), channel_id=1, source_target_pairs={{0,24},{4,28},{8,0},{12,4},{16,8},{20,12},{24,16},{28,20},{1,25},{... | collective-permute-start | bytes 200 | tf_op jit(solution)/shard_map/ppermute | solution.py:23
  49.6 23.1 %collective-permute-start.5 = (f32[16,128,128]{2,1,0:T(8,128)S(1)}, f32[16,128,128]{2,1,0:T(8,128)S(1)}, u32[]{:S(2)}, u32[]{:S(2)}) collective-permute-start(f32[16,128,128]{2,1,0:T(8,128)S(1)} %pad_maximum_fusion), channel_id=1, source_target_pairs={{0,24},{4,28},{8,0},{12,4},{16,8},{20,12},{24,16},{28,20},{1,25},{... | collective-permute-start | bytes 3145736 | tf_op jit(solution)/shard_map/ppermute | solution.py:23
  72.8 29.4 %copy-start.5 = (f32[16,128,128]{2,1,0:T(8,128)}, f32[16,128,128]{2,1,0:T(8,128)S(1)}, u32[]{:S(2)}) copy-start(f32[16,128,128]{2,1,0:T(8,128)S(1)} %collective-permute-done.5) | copy-start | bytes 3145732
  72.8 23.0 %collective-permute-start.8 = (f32[16,128,128]{2,1,0:T(8,128)S(1)}, f32[16,128,128]{2,1,0:T(8,128)}, u32[]{:S(2)}, u32[]{:S(2)}) collective-permute-start(f32[16,128,128]{2,1,0:T(8,128)S(1)} %collective-permute-done.5), channel_id=1, source_target_pairs={{0,24},{4,28},{8,0},{12,4},{16,8},{20,12},{24,16},{28,20},{1,25},{... | collective-permute-start | bytes 3145736 | tf_op jit(solution)/shard_map/ppermute | solution.py:23
  95.8 34.0 %collective-permute-start.11 = (f32[16,128,128]{2,1,0:T(8,128)}, f32[16,128,128]{2,1,0:T(8,128)}, u32[]{:S(2)}, u32[]{:S(2)}) collective-permute-start(f32[16,128,128]{2,1,0:T(8,128)} %collective-permute-done.8), channel_id=1, source_target_pairs={{0,24},{4,28},{8,0},{12,4},{16,8},{20,12},{24,16},{28,20},{1,25},{... | collective-permute-start | bytes 3145736 | tf_op jit(solution)/shard_map/ppermute | solution.py:23
  104.1 3.1 %copy-start.2 = (f32[8,128,128]{2,1,0:T(8,128)S(1)}, f32[8,128,128]{2,1,0:T(8,128)}, u32[]{:S(2)}) copy-start(f32[8,128,128]{2,1,0:T(8,128)} %get-tuple-element.43) | copy-start | bytes 1572868
  107.1 2.0 %copy-start.1 = (f32[8,128,128]{2,1,0:T(8,128)S(1)}, f32[8,128,128]{2,1,0:T(8,128)}, u32[]{:S(2)}) copy-start(f32[8,128,128]{2,1,0:T(8,128)} %get-tuple-element.44) | copy-start | bytes 1572868
  109.2 2.0 %copy-start = (f32[8,128,128]{2,1,0:T(8,128)S(1)}, f32[8,128,128]{2,1,0:T(8,128)}, u32[]{:S(2)}) copy-start(f32[8,128,128]{2,1,0:T(8,128)} %get-tuple-element.45) | copy-start | bytes 1572868
  115.2 4.6 %copy-start.3 = (f32[32,128,128]{2,1,0:T(8,128)S(1)}, f32[32,128,128]{2,1,0:T(8,128)}, u32[]{:S(2)}) copy-start(f32[32,128,128]{2,1,0:T(8,128)} %gather_fusion.2) | copy-start | bytes 6291460
  115.2 4.6 %copy-start.4 = (f32[32,128,128]{2,1,0:T(8,128)S(1)}, f32[32,128,128]{2,1,0:T(8,128)}, u32[]{:S(2)}) copy-start(f32[32,128,128]{2,1,0:T(8,128)} %gather_fusion.3) | copy-start | bytes 6291460
Sparse Core Ops, SparseCore 0:
  54.5 49.4 all-reduce.3
where the time goes:
time: 145 us; the launch traced here: 144 us
  waiting for transfers between devices  48.3 us (33%)
  starting transfers between devices  31.3 us (22%)
  local copies, waits for them, and re-layouts  21.3 us (15%)
  matrix products  15.9 us (11%)
  between operations  13.6 us (9%)
  other arithmetic  8.88 us (6%)
  blocking collectives  5.13 us (4%)
    ppermute x9, waiting for transfers between devices, shifted(): return lax.ppermute(value, axis, pairs)  37 us
    ppermute x9, starting transfers between devices, shifted(): return lax.ppermute(value, axis, pairs)  26.3 us
    dot_general x4, matrix products, section_product(): jnp.einsum('tqij,tqjk->tik', left, right, precision=lax.Precision.HIGHEST...  15.9 us
    gather x4, local copies, waits for them, and re-layouts, section_product(): right = pair_vals[pair_slot]  11.8 us
    ppermute x3, waiting for transfers between devices, from_partner(): lax.ppermute(x, axis, [(i, i ^ 1 << bit) for i in range(lax.axis_size(axi...  9.52 us
    gather x4, local copies, waits for them, and re-layouts, section_product(): left = panel_vals[panel_slot] * weight[:, :, None, None]  7.79 us
    psum x1, blocking collectives, from_root(): return lax.psum(jnp.where(mine, x, jnp.zeros_like(x)), axis)  5.13 us
    ppermute x3, starting transfers between devices, from_partner(): lax.ppermute(x, axis, [(i, i ^ 1 << bit) for i in range(lax.axis_size(axi...  4.99 us
  transfers between devices with their start and end apart: 13, of which 6 were waited for; matrix products, arithmetic and copies ran while one was open for 26% of the time, Pallas kernels for 0%

commit v1 on v0

--- a/solution.py
+++ b/solution.py
@@ -1,11 +1,17 @@
 import jax
 import jax.numpy as jnp
 from jax import lax
+from jax.experimental import pallas as pl
+from jax.experimental.pallas import tpu as pltpu
 from jax.sharding import PartitionSpec as P
 
 NBLK = 512
 ACT = 2
 SECTIONS = 4
+BS = 128
+SLOTS = 8
+CAP = 8
+VMEM_LIMIT = 32 * 1024 * 1024
 
 
 def from_root(x, axis, root):
@@ -75,14 +81,10 @@
 
 def fetch_panel(tile, row_index, col_count, section):
     root = (row_index // 2 + section) % col_count
-    return (
-        from_root(tile[0], "col", root),
-        from_root(tile[1], "col", root),
-        from_root(tile[2], "col", root),
-    )
-
-
-def body(blocks, block_rows, block_cols):
+    return tuple(from_root(one, "col", root) for one in tile)
+
+
+def general_body(blocks, block_rows, block_cols):
     tile = (blocks[0, 0], block_rows[0, 0], block_cols[0, 0])
     row_count = lax.axis_size("row")
     col_count = lax.axis_size("col")
@@ -92,8 +94,7 @@
     depth = 2 * ACT
     total = jnp.zeros(blocks.shape[2:], jnp.float32)
     partner = from_partner((tile[0], tile[1], tile[2]), "row", 0)
-    start_pair = order_pair(tile, partner, is_even, row_span)
-    current = start_pair
+    current = order_pair(tile, partner, is_even, row_span)
     for section in range(SECTIONS):
         panel = fetch_panel(tile, row_index, col_count, section)
         if section > 0:
@@ -102,9 +103,205 @@
     return total[None, None]
 
 
+def everything(x, axis):
+    return lax.all_to_all(jnp.broadcast_to(x[None], (lax.axis_size(axis),) + x.shape), axis, 0, 0)
+
+
+def whole_tiles(blocks, block_rows, block_cols):
+    tile = (blocks[0, 0], block_rows[0, 0], block_cols[0, 0])
+    row_span = NBLK // lax.axis_size("row")
+    col_count = lax.axis_size("col")
+    row_index = lax.axis_index("row")
+    panels = tuple(everything(one, "col") for one in tile)
+    column = tuple(everything(one, "row") for one in tile)
+
+    def section(step, total):
+        root = (row_index // 2 + step) % col_count
+        take = lambda arrays, at: tuple(lax.dynamic_index_in_dim(a, at, 0, False) for a in arrays)
+        pair = make_pair(take(column, 2 * root), take(column, 2 * root + 1), row_span)
+        return total + section_product(take(panels, root), pair, tile[1], tile[2], 2 * ACT)
+
+    total = lax.fori_loop(0, SECTIONS, section, jnp.zeros(blocks.shape[2:], jnp.float32))
+    return total[None, None]
+
+
+def spread_kernel(blocks_ref, rows_ref, cols_ref, out_ref):
+    devices = out_ref.shape[0]
+    q = BS // devices
+    sub = lax.broadcasted_iota(jnp.int32, (SLOTS, SLOTS), 0)
+    lane = lax.broadcasted_iota(jnp.int32, (SLOTS, SLOTS), 1)
+
+    def column(ref):
+        one = jnp.broadcast_to(ref[...].astype(jnp.float32), (SLOTS, SLOTS))
+        return jnp.sum(jnp.where(sub == lane, one, 0.0), axis=1, keepdims=True)
+
+    lanes = lax.broadcasted_iota(jnp.int32, (SLOTS, BS), 1)
+    places = jnp.where(lanes == 0, column(rows_ref), jnp.where(lanes == 1, column(cols_ref), 0.0))
+    for p in range(devices):
+        for part in range(q):
+            out_ref[p, :, part * BS : (part + 1) * BS] = blocks_ref[pl.ds(q * p + part, SLOTS, stride=BS), :]
+        out_ref[p, :, q * BS : (q + 1) * BS] = places
+
+
+def bf(x):
+    return x.astype(jnp.bfloat16)
+
+
+def mm(a, b, transposed=False):
+    dims = (((1,), (1 if transposed else 0,)), ((), ()))
+    return lax.dot_general(a, b, dims, preferred_element_type=jnp.float32)
+
+
+def plan_kernel(rows, cols, piece_ref, send_ref, list_ref, most_ref):
+    devices = rows * cols
+    n = devices * SLOTS
+    width = send_ref.shape[1]
+    rb = NBLK // rows
+    cb = NBLK // cols
+    per_row = cols * SLOTS
+    my_row, my_col = lax.axis_index("row"), lax.axis_index("col")
+    me = my_row * cols + my_col
+
+    idx = piece_ref[:, width : width + BS]
+    idx_t = idx.T
+    sub = lax.broadcasted_iota(jnp.int32, (n, 1), 0)
+    lane = lax.broadcasted_iota(jnp.int32, (1, n), 1)
+
+    def places(row, col, at):
+        up = ((at // per_row) * rb).astype(jnp.float32)
+        along = (((at // SLOTS) % cols) * cb).astype(jnp.float32)
+        return jnp.where(row >= 0, row + up, -1.0), jnp.where(col >= 0, col + along, -2.0)
+
+    row_c, col_c = places(idx[:, 0:1], idx[:, 1:2], sub)
+    row_r, col_r = places(idx_t[0:1, :], idx_t[1:2, :], lane)
+
+    same_row = bf(jnp.where(row_c == row_r, 1.0, 0.0))
+    slot_r = (lane % SLOTS).astype(jnp.float32)
+    same_col = bf(jnp.where(col_c == col_r, 1.0 + 16.0 * slot_r, 0.0))
+    hit = mm(same_col, same_row)
+    product = (row_c == col_r) & (hit > 0)
+    product_b = bf(jnp.where(product, 1.0, 0.0))
+
+    dev = lax.broadcasted_iota(jnp.int32, (devices, 1), 0)
+    in_row = (lane // per_row) == (dev // cols)
+    in_col = ((lane // SLOTS) % cols) == (dev % cols)
+    own = (lane // SLOTS) == dev
+    as_left = mm(bf(jnp.where(in_col, 1.0, 0.0)), product_b)
+    as_right = mm(bf(jnp.where(in_row, 1.0, 0.0)), product_b, transposed=True)
+    need = ((in_row & (as_left > 0)) | (in_col & (as_right > 0))) & jnp.logical_not(own)
+    need_f = jnp.where(need, 1.0, 0.0)
+    before = bf(jnp.where(sub < lane, 1.0, 0.0))
+    pos = jnp.where(need, mm(bf(need_f), before), -1.0)
+    most_ref[0, 0] = jnp.max(jnp.sum(need_f, axis=1, keepdims=True)).astype(jnp.int32)
+
+    dev_r = lax.broadcasted_iota(jnp.int32, (1, devices), 1)
+    repeat = bf(jnp.where((sub // CAP) == dev_r, 1.0, 0.0))
+    chosen = bf(jnp.where(mm(repeat, bf(pos)) == (sub % CAP).astype(jnp.float32), 1.0, 0.0))
+    data = piece_ref[:, :width]
+    high = bf(data)
+    low = bf(data - high.astype(jnp.float32))
+    send_ref[...] = mm(chosen, high) + mm(chosen, low)
+
+    my_pos = jnp.sum(jnp.where(dev == me, pos, 0.0), axis=0, keepdims=True)
+    held_r = jnp.where((lane // SLOTS) == me, slot_r, SLOTS + my_pos)
+    held_c = jnp.sum(jnp.where(sub == lane, held_r, 0.0), axis=1, keepdims=True)
+    mine = product & (((sub // SLOTS) % cols) == my_col) & ((lane // per_row) == my_row)
+    earlier = bf(jnp.where(lane < sub, 1.0, 0.0))
+    rank = mm(earlier, bf(jnp.where(mine, 1.0, 0.0)))
+    code = (hit - 1.0) * 16.0 + held_r * 16.0 + held_c + 1.0
+    out_sub = lax.broadcasted_iota(jnp.int32, (list_ref.shape[0], 1), 0)
+    listed = jnp.zeros(list_ref.shape, jnp.float32)
+    for k in range(2 * ACT):
+        one = jnp.sum(jnp.where(mine & (rank == k), code, 0.0), axis=0, keepdims=True)
+        listed = jnp.where(out_sub == k, one, listed)
+    list_ref[...] = listed.astype(jnp.int32) - 1
+
+
+def product_kernel(rows, cols, list_ref, blocks_ref, piece_ref, out_ref, held_ref):
+    devices = rows * cols
+    q = BS // devices
+    per_row = cols * SLOTS
+    first = lax.axis_index("row") * per_row
+    held_ref[: SLOTS * BS, :] = blocks_ref[...]
+    for p in range(devices):
+        for part in range(q):
+            held_ref[pl.ds(SLOTS * BS + q * p + part, CAP, stride=BS), :] = piece_ref[
+                p * CAP : (p + 1) * CAP, part * BS : (part + 1) * BS
+            ]
+    out_ref[...] = jnp.zeros_like(out_ref)
+
+    def block(at):
+        x = held_ref[pl.ds(pl.multiple_of(at * BS, BS), BS), :]
+        high = bf(x)
+        return high, bf(x - high.astype(jnp.float32))
+
+    def entry(i, carry):
+        for k in range(2 * ACT):
+            code = list_ref[k, first + i]
+
+            @pl.when(code >= 0)
+            def _():
+                a_high, a_low = block((code // 16) % 16)
+                b_high, b_low = block(code % 16)
+                at = pl.ds(pl.multiple_of((code // 256) * BS, BS), BS)
+                out_ref[at, :] += mm(a_high, b_high) + (mm(a_high, b_low) + mm(a_low, b_high))
+
+        return carry
+
+    lax.fori_loop(0, per_row, entry, 0)
+
+
+def packed_body(blocks, block_rows, block_cols):
+    rows, cols = lax.axis_size("row"), lax.axis_size("col")
+    devices = rows * cols
+    n = devices * SLOTS
+    q = BS // devices
+    flat = blocks.reshape(SLOTS * BS, BS)
+    params = pltpu.CompilerParams(vmem_limit_bytes=VMEM_LIMIT)
+    vmem = pl.BlockSpec(memory_space=pltpu.VMEM)
+    smem = pl.BlockSpec(memory_space=pltpu.SMEM)
+    spread = pl.pallas_call(
+        spread_kernel,
+        out_shape=jax.ShapeDtypeStruct((devices, SLOTS, (q + 1) * BS), jnp.float32),
+        in_specs=[vmem] * 3,
+        out_specs=vmem,
+        compiler_params=params,
+        name="spread",
+    )(flat, block_rows[0], block_cols[0])
+    pieces = lax.all_to_all(spread, ("row", "col"), 0, 0).reshape(n, (q + 1) * BS)
+    send, listed, most = pl.pallas_call(
+        lambda *refs: plan_kernel(rows, cols, *refs),
+        out_shape=(
+            jax.ShapeDtypeStruct((devices * CAP, q * BS), jnp.float32),
+            jax.ShapeDtypeStruct((8, n), jnp.int32),
+            jax.ShapeDtypeStruct((1, 1), jnp.int32),
+        ),
+        in_specs=[vmem],
+        out_specs=(vmem, vmem, smem),
+        compiler_params=params,
+        name="plan",
+    )(pieces)
+
+    def packed():
+        got = lax.all_to_all(send.reshape(devices, CAP, q * BS), ("row", "col"), 0, 0)
+        out = pl.pallas_call(
+            lambda *refs: product_kernel(rows, cols, *refs),
+            out_shape=jax.ShapeDtypeStruct((SLOTS * BS, BS), jnp.float32),
+            in_specs=[smem, vmem, vmem],
+            out_specs=vmem,
+            scratch_shapes=[pltpu.VMEM(((SLOTS + CAP) * BS, BS), jnp.float32)],
+            compiler_params=params,
+            name="products",
+        )(listed, flat, got.reshape(devices * CAP, q * BS))
+        return out.reshape(blocks.shape)
+
+    return lax.cond(most[0, 0] <= CAP, packed, lambda: whole_tiles(blocks, block_rows, block_cols))
+
+
 def solution(mesh):
+    small = mesh.shape["col"] == SECTIONS and mesh.devices.size * SLOTS <= 256
     return jax.shard_map(
-        body,
+        packed_body if small else general_body,
         mesh=mesh,
         in_specs=(P("row", "col", None, None, None), P("row", "col", None), P("row", "col", None)),
         out_specs=P("row", "col", None, None, None),

time: 145 us -> 54 us (0.37)
  waiting for transfers between devices: 48.3 us -> 17.9 us
  starting transfers between devices: 31.3 us -> 7.3 us
  local copies, waits for them, and re-layouts: 21.3 us -> 0.8 us
  matrix products: 15.9 us -> 0 us
  blocking collectives: 5.13 us -> 19.1 us
  between operations: 13.6 us -> 0.67 us
  other arithmetic: 8.88 us -> 0 us
  Pallas kernels: 0 us -> 7.92 us
    ppermute x12 -> x0, waiting for transfers between devices: 46.5 us -> none  [the longest x9 37 us: shifted(): return lax.ppermute(value, axis, pairs)]
    ppermute x12 -> x0, starting transfers between devices: 31.3 us -> none  [the longest x9 26.3 us: shifted(): return lax.ppermute(value, axis, pairs)]
    gather x8 -> x0, local copies, waits for them, and re-layouts: 19.6 us -> none  [the longest x4 11.8 us: section_product(): right = pair_vals[pair_slot]]
    all_to_all x0 -> x1, blocking collectives: none -> 19.1 us  [packed(): lax.all_to_all(send.reshape(devices, CAP, q * BS), ('row', 'col'), 0, 0)]
    all_to_all x0 -> x1, waiting for transfers between devices: none -> 17.9 us  [packed_body(): lax.all_to_all(spread, ('row', 'col'), 0, 0).reshape(n, (q + 1) * BS)]
    dot_general x4 -> x0, matrix products: 15.9 us -> none  [section_product(): jnp.einsum('tqij,tqjk->tik', left, right, precision=lax.Precision.HIGHEST...]
    pallas_call x0 -> x3, Pallas kernels: none -> 7.92 us  [the longest x1 3.8 us: packed(): pl.pallas_call(lambda *refs: product_kernel(rows, cols, *refs), out_shape...]
    all_to_all x0 -> x1, starting transfers between devices: none -> 7.3 us  [packed_body(): lax.all_to_all(spread, ('row', 'col'), 0, 0).reshape(n, (q + 1) * BS)]
  transfers between devices with their start and end apart: 13 -> 1, of which waited for: 6 -> 1; matrix products, arithmetic and copies ran while one was open for 26% -> 0% of each run, Pallas kernels for 0% -> 0%
where the time goes in v1:
time: 54 us; the launch traced here: 53.7 us
  blocking collectives  19.1 us (35%)
  waiting for transfers between devices  17.9 us (33%)
  Pallas kernels  7.92 us (15%)
  starting transfers between devices  7.3 us (14%)
  local copies, waits for them, and re-layouts  0.8 us (1%)
  between operations  0.67 us (1%)
    all_to_all x1, blocking collectives, packed(): lax.all_to_all(send.reshape(devices, CAP, q * BS), ('row', 'col'), 0, 0)  19.1 us
    all_to_all x1, waiting for transfers between devices, packed_body(): lax.all_to_all(spread, ('row', 'col'), 0, 0).reshape(n, (q + 1) * BS)  17.9 us
    all_to_all x1, starting transfers between devices, packed_body(): lax.all_to_all(spread, ('row', 'col'), 0, 0).reshape(n, (q + 1) * BS)  7.3 us
    pallas_call x1, Pallas kernels, packed(): pl.pallas_call(lambda *refs: product_kernel(rows, cols, *refs), out_shape...  3.8 us
    pallas_call x1, Pallas kernels, packed_body(): pl.pallas_call(spread_kernel, out_shape=jax.ShapeDtypeStruct((devices, SL...  2.27 us
    pallas_call x1, Pallas kernels, packed_body(): pl.pallas_call(lambda *refs: plan_kernel(rows, cols, *refs), out_shape=(j...  1.85 us
  transfers between devices with their start and end apart: 1, of which 1 were waited for; matrix products, arithmetic and copies ran while one was open for 0% of the time, Pallas kernels for 0%

profile of v1, /device:TPU:0, one launch (start us, length us, event | category | flops | bytes accessed | tf_op | source)
XLA Modules:
  0.0 53.7 jit_solution(253320016249732659)
XLA Ops:
  0.0 0.0 copy-start.2
  0.0 0.0 copy-start.3
  0.0 0.0 copy-start.4
  0.0 2.3 %spread.1 = f32[32,8,640]{2,1,0:T(8,128)} custom-call(f32[1024,128]{1,0:T(8,128)} %bitcast.85, s32[1,8]{1,0:T(1,128)} %bitcast.90, s32[1,8]{1,0:T(1,128)} %bitcast.95), custom_call_target="tpu_custom_call" | custom-call | tf_op jit(solution)/shard_map/spread/pallas_call | solution.py:263
  2.3 7.3 %all-to-all-start.7 = ((f32[32,8,640]{2,1,0:T(8,128)}), f32[32,8,640]{2,1,0:T(8,128)S(1)}, u32[]{:S(2)}, u32[]{:S(2)}) async-start(f32[32,8,640]{2,1,0:T(8,128)} %spread.1), calls=%async_computation.7 | async-start | bytes 1310720 | tf_op jit(solution)/shard_map/all_to_all | solution.py:271
  9.6 17.9 %all-to-all-done.7 = f32[32,8,640]{2,1,0:T(8,128)S(1)} async-done(((f32[32,8,640]{2,1,0:T(8,128)}), f32[32,8,640]{2,1,0:T(8,128)S(1)}, u32[]{:S(2)}, u32[]{:S(2)}) %all-to-all-start.7) | async-done | bytes 655392 | tf_op jit(solution)/shard_map/all_to_all | solution.py:271
  27.5 1.9 %plan.1 = (f32[256,512]{1,0:T(8,128)}, s32[8,256]{1,0:T(8,128)S(1)}, s32[1,1]{1,0:T(1,128)}) custom-call(f32[256,640]{1,0:T(8,128)S(1)} %bitcast.79), custom_call_target="tpu_custom_call" | custom-call | tf_op jit(solution)/shard_map/plan/pallas_call | solution.py:272
  30.0 0.0 copy-done.2
  30.0 0.0 copy-done.3
  30.0 0.0 copy-done.4
  30.0 22.9 %conditional.1 = (f32[1,1,8,128,128]{4,3,2,1,0:T(8,128)S(1)}) conditional(s32[]{:T(128)} %bitcast.15, (f32[1,1,8,128,128]{4,3,2,1,0:T(8,128)S(1)}, s32[1,1,8]{2,1,0:T(1,128)S(1)}, s32[1,1,8]{2,1,0:T(1,128)S(1)}) %tuple.87, (f32[256,512]{1,0:T(8,128)}, s32[8,256]{1,0:T(8,128)S(1)}, f32[1024,128]{1,0:T(8,128)S(1)}) %tuple.84), branch_computations={%region_0.9_spmd, %region_9.10_spmd} | conditional | flops 806364224 | bytes 51396960 | solution.py:298
  30.0 19.1 %all_to_all.50 = f32[32,8,512]{2,1,0:T(8,128)S(1)} all-to-all(f32[32,8,512]{2,1,0:T(8,128)} %bitcast.89), channel_id=1, replica_groups=mesh['row'=8,'col'=4] {'row','col'}, dimensions={0} | all-to-all | bytes 1048576 | tf_op jit(solution)/shard_map/cond/branch_1_fun/all_to_all | solution.py:286
  49.1 3.8 %products.1 = f32[1024,128]{1,0:T(8,128)S(1)} custom-call(s32[8,256]{1,0:T(8,128)S(1)} %get-tuple-element.403.refs_0_, f32[1024,128]{1,0:T(8,128)S(1)} %get-tuple-element.404.refs_1_, f32[256,512]{1,0:T(8,128)S(1)} %bitcast.80), custom_call_target="tpu_custom_call" | custom-call | tf_op jit(solution)/shard_map/cond/branch_1_fun/products/pallas_call | solution.py:287
  52.9 0.0 copy-start.1
  52.9 0.8 %copy-done.1 = f32[1,1,8,128,128]{4,3,2,1,0:T(8,128)} copy-done((f32[1,1,8,128,128]{4,3,2,1,0:T(8,128)}, f32[1,1,8,128,128]{4,3,2,1,0:T(8,128)S(1)}, u32[]{:S(2)}) %copy-start.1) | copy-done | bytes 524312
Async XLA Ops:
  0.0 30.0 %copy-start.2 = (f32[1,1,8,128,128]{4,3,2,1,0:T(8,128)S(1)}, f32[1,1,8,128,128]{4,3,2,1,0:T(8,128)}, u32[]{:S(2)}) copy-start(f32[1,1,8,128,128]{4,3,2,1,0:T(8,128)} %param.7) | copy-start | bytes 1572868
  0.0 30.0 %copy-start.3 = (s32[1,1,8]{2,1,0:T(1,128)S(1)}, s32[1,1,8]{2,1,0:T(1,128)}, u32[]{:S(2)}) copy-start(s32[1,1,8]{2,1,0:T(1,128)} %param.8) | copy-start | bytes 100
  0.0 30.0 %copy-start.4 = (s32[1,1,8]{2,1,0:T(1,128)S(1)}, s32[1,1,8]{2,1,0:T(1,128)}, u32[]{:S(2)}) copy-start(s32[1,1,8]{2,1,0:T(1,128)} %param.9) | copy-start | bytes 100
  2.3 25.2 %all-to-all-start.7 = ((f32[32,8,640]{2,1,0:T(8,128)}), f32[32,8,640]{2,1,0:T(8,128)S(1)}, u32[]{:S(2)}, u32[]{:S(2)}) async-start(f32[32,8,640]{2,1,0:T(8,128)} %spread.1), calls=%async_computation.7 | async-start | bytes 1310720 | tf_op jit(solution)/shard_map/all_to_all | solution.py:271
  52.9 0.8 %copy-start.1 = (f32[1,1,8,128,128]{4,3,2,1,0:T(8,128)}, f32[1,1,8,128,128]{4,3,2,1,0:T(8,128)S(1)}, u32[]{:S(2)}) copy-start(f32[1,1,8,128,128]{4,3,2,1,0:T(8,128)S(1)} %get-tuple-element.665) | copy-start | bytes 1572868

commit v2 on v1

--- a/solution.py
+++ b/solution.py
@@ -11,6 +11,7 @@
 BS = 128
 SLOTS = 8
 CAP = 8
+ZCAP = 8
 VMEM_LIMIT = 32 * 1024 * 1024
 
 
@@ -109,11 +110,11 @@
 
 def whole_tiles(blocks, block_rows, block_cols):
     tile = (blocks[0, 0], block_rows[0, 0], block_cols[0, 0])
-    row_span = NBLK // lax.axis_size("row")
+    row_span = NBLK // lax.axis_size(("z", "y"))
     col_count = lax.axis_size("col")
-    row_index = lax.axis_index("row")
+    row_index = lax.axis_index(("z", "y"))
     panels = tuple(everything(one, "col") for one in tile)
-    column = tuple(everything(one, "row") for one in tile)
+    column = tuple(everything(one, ("z", "y")) for one in tile)
 
     def section(step, total):
         root = (row_index // 2 + step) % col_count
@@ -125,26 +126,12 @@
     return total[None, None]
 
 
-def spread_kernel(blocks_ref, rows_ref, cols_ref, out_ref):
-    devices = out_ref.shape[0]
-    q = BS // devices
-    sub = lax.broadcasted_iota(jnp.int32, (SLOTS, SLOTS), 0)
-    lane = lax.broadcasted_iota(jnp.int32, (SLOTS, SLOTS), 1)
-
-    def column(ref):
-        one = jnp.broadcast_to(ref[...].astype(jnp.float32), (SLOTS, SLOTS))
-        return jnp.sum(jnp.where(sub == lane, one, 0.0), axis=1, keepdims=True)
-
-    lanes = lax.broadcasted_iota(jnp.int32, (SLOTS, BS), 1)
-    places = jnp.where(lanes == 0, column(rows_ref), jnp.where(lanes == 1, column(cols_ref), 0.0))
-    for p in range(devices):
-        for part in range(q):
-            out_ref[p, :, part * BS : (part + 1) * BS] = blocks_ref[pl.ds(q * p + part, SLOTS, stride=BS), :]
-        out_ref[p, :, q * BS : (q + 1) * BS] = places
-
-
 def bf(x):
     return x.astype(jnp.bfloat16)
+
+
+def ind(x):
+    return bf(jnp.where(x, 1.0, 0.0))
 
 
 def mm(a, b, transposed=False):
@@ -152,62 +139,92 @@
     return lax.dot_general(a, b, dims, preferred_element_type=jnp.float32)
 
 
-def plan_kernel(rows, cols, piece_ref, send_ref, list_ref, most_ref):
+def plan_kernel(rows, cols, idx_ref, cross_ref, give_ref, list_ref, most_ref):
     devices = rows * cols
+    planes = rows // 2
+    plane = 2 * cols
     n = devices * SLOTS
-    width = send_ref.shape[1]
+    in_plane = plane * SLOTS
     rb = NBLK // rows
     cb = NBLK // cols
     per_row = cols * SLOTS
-    my_row, my_col = lax.axis_index("row"), lax.axis_index("col")
+    my_plane = lax.axis_index("z")
+    my_row = 2 * my_plane + lax.axis_index("y")
+    my_col = lax.axis_index("col")
     me = my_row * cols + my_col
 
-    idx = piece_ref[:, width : width + BS]
-    idx_t = idx.T
     sub = lax.broadcasted_iota(jnp.int32, (n, 1), 0)
     lane = lax.broadcasted_iota(jnp.int32, (1, n), 1)
-
-    def places(row, col, at):
-        up = ((at // per_row) * rb).astype(jnp.float32)
-        along = (((at // SLOTS) % cols) * cb).astype(jnp.float32)
-        return jnp.where(row >= 0, row + up, -1.0), jnp.where(col >= 0, col + along, -2.0)
-
-    row_c, col_c = places(idx[:, 0:1], idx[:, 1:2], sub)
-    row_r, col_r = places(idx_t[0:1, :], idx_t[1:2, :], lane)
-
-    same_row = bf(jnp.where(row_c == row_r, 1.0, 0.0))
+    dev = lax.broadcasted_iota(jnp.int32, (devices, 1), 0)
+    dev_r = lax.broadcasted_iota(jnp.int32, (1, devices), 1)
+    slot = lax.broadcasted_iota(jnp.int32, (1, SLOTS), 1)
+    diagonal = sub == lane
+
+    def as_row(column):
+        return jnp.sum(jnp.where(diagonal, column, 0.0), axis=0, keepdims=True)
+
+    def as_column(row):
+        return jnp.sum(jnp.where(diagonal, row, 0.0), axis=1, keepdims=True)
+
+    repeat = ind((sub // SLOTS) == dev_r)
+
+    def column(k):
+        values = mm(repeat, bf(idx_ref[:, k, :].astype(jnp.float32)))
+        return jnp.sum(jnp.where((sub % SLOTS) == slot, values, 0.0), axis=1, keepdims=True)
+
+    up = ((sub // per_row) * rb).astype(jnp.float32)
+    along = (((sub // SLOTS) % cols) * cb).astype(jnp.float32)
+    row_c, col_c = column(0), column(1)
+    row_c = jnp.where(row_c >= 0, row_c + up, -1.0)
+    col_c = jnp.where(col_c >= 0, col_c + along, -2.0)
+    row_r, col_r = as_row(row_c), as_row(col_c)
+
     slot_r = (lane % SLOTS).astype(jnp.float32)
-    same_col = bf(jnp.where(col_c == col_r, 1.0 + 16.0 * slot_r, 0.0))
-    hit = mm(same_col, same_row)
+    hit = mm(bf(jnp.where(col_c == col_r, 1.0 + 16.0 * slot_r, 0.0)), ind(row_c == row_r))
     product = (row_c == col_r) & (hit > 0)
-    product_b = bf(jnp.where(product, 1.0, 0.0))
-
-    dev = lax.broadcasted_iota(jnp.int32, (devices, 1), 0)
+    product_b = ind(product)
+
     in_row = (lane // per_row) == (dev // cols)
     in_col = ((lane // SLOTS) % cols) == (dev % cols)
-    own = (lane // SLOTS) == dev
-    as_left = mm(bf(jnp.where(in_col, 1.0, 0.0)), product_b)
-    as_right = mm(bf(jnp.where(in_row, 1.0, 0.0)), product_b, transposed=True)
-    need = ((in_row & (as_left > 0)) | (in_col & (as_right > 0))) & jnp.logical_not(own)
-    need_f = jnp.where(need, 1.0, 0.0)
-    before = bf(jnp.where(sub < lane, 1.0, 0.0))
-    pos = jnp.where(need, mm(bf(need_f), before), -1.0)
-    most_ref[0, 0] = jnp.max(jnp.sum(need_f, axis=1, keepdims=True)).astype(jnp.int32)
-
-    dev_r = lax.broadcasted_iota(jnp.int32, (1, devices), 1)
-    repeat = bf(jnp.where((sub // CAP) == dev_r, 1.0, 0.0))
-    chosen = bf(jnp.where(mm(repeat, bf(pos)) == (sub % CAP).astype(jnp.float32), 1.0, 0.0))
-    data = piece_ref[:, :width]
-    high = bf(data)
-    low = bf(data - high.astype(jnp.float32))
-    send_ref[...] = mm(chosen, high) + mm(chosen, low)
+    as_left = mm(ind(in_col), product_b)
+    as_right = mm(ind(in_row), product_b, transposed=True)
+    need = (in_row & (as_left > 0)) | (in_col & (as_right > 0))
+    need = need & ((lane // SLOTS) != dev)
+    before = sub < lane
+    pos = jnp.where(need, mm(ind(need), ind(before)), -1.0)
+
+    zed = lax.broadcasted_iota(jnp.int32, (8, 1), 0)
+    zneed = (mm(ind((dev_r // plane) == zed), ind(need)) > 0) & ((lane // in_plane) != zed)
+    same_plane = (sub // in_plane) == (lane // in_plane)
+    zpos = jnp.where(zneed, mm(ind(zneed), ind(before & same_plane)), -1.0)
+
+    over = jnp.maximum(jnp.max(pos) - (CAP - 1), jnp.max(zpos) - (ZCAP - 1))
+    most_ref[0, 0] = over.astype(jnp.int32)
+
+    lanes = lax.broadcasted_iota(jnp.int32, (1, BS), 1)
+    mine_z = (lane // in_plane) == my_plane
+    local = (lane % in_plane).astype(jnp.float32)
+    cross = jnp.zeros(cross_ref.shape, jnp.float32)
+    for m in range(ZCAP):
+        one = jnp.sum(jnp.where(mine_z & (zpos == m), local, 0.0), axis=1, keepdims=True)
+        cross = jnp.where(lanes == m, one, cross)
+    cross_ref[...] = cross.astype(jnp.int32)
+
+    from_z = jnp.sum(jnp.where(zed == my_plane, zpos, 0.0), axis=0, keepdims=True)
+    source = jnp.where(mine_z, local, in_plane + ZCAP * (lane // in_plane).astype(jnp.float32) + from_z)
+    pick = lax.broadcasted_iota(jnp.int32, (plane, 1), 0) + plane * my_plane
+    pos_p = mm(ind(pick == dev_r), bf(pos))
+    give = jnp.zeros(give_ref.shape, jnp.float32)
+    for m in range(CAP):
+        one = jnp.sum(jnp.where(pos_p == m, source, 0.0), axis=1, keepdims=True)
+        give = jnp.where(lanes == m, one, give)
+    give_ref[...] = give.astype(jnp.int32)
 
     my_pos = jnp.sum(jnp.where(dev == me, pos, 0.0), axis=0, keepdims=True)
     held_r = jnp.where((lane // SLOTS) == me, slot_r, SLOTS + my_pos)
-    held_c = jnp.sum(jnp.where(sub == lane, held_r, 0.0), axis=1, keepdims=True)
+    held_c = as_column(held_r)
     mine = product & (((sub // SLOTS) % cols) == my_col) & ((lane // per_row) == my_row)
-    earlier = bf(jnp.where(lane < sub, 1.0, 0.0))
-    rank = mm(earlier, bf(jnp.where(mine, 1.0, 0.0)))
+    rank = mm(ind(lane < sub), ind(mine))
     code = (hit - 1.0) * 16.0 + held_r * 16.0 + held_c + 1.0
     out_sub = lax.broadcasted_iota(jnp.int32, (list_ref.shape[0], 1), 0)
     listed = jnp.zeros(list_ref.shape, jnp.float32)
@@ -217,17 +234,32 @@
     list_ref[...] = listed.astype(jnp.int32) - 1
 
 
-def product_kernel(rows, cols, list_ref, blocks_ref, piece_ref, out_ref, held_ref):
-    devices = rows * cols
-    q = BS // devices
+def cross_kernel(planes, piece, cross_ref, held_ref, out_ref):
+    for z in range(planes):
+        for m in range(ZCAP):
+            at = pl.ds(pl.multiple_of(cross_ref[z, m] * piece, piece), piece)
+            out_ref[pl.ds((z * ZCAP + m) * piece, piece), :] = held_ref[at, :]
+
+
+def give_kernel(plane, piece, give_ref, held_ref, crossed_ref, out_ref):
+    count = held_ref.shape[0] // piece
+    for p in range(plane):
+        for m in range(CAP):
+            at = give_ref[p, m]
+            here = pl.ds(pl.multiple_of(jnp.minimum(at, count - 1) * piece, piece), piece)
+            there = pl.ds(pl.multiple_of(jnp.maximum(at - count, 0) * piece, piece), piece)
+            out_ref[pl.ds((p * CAP + m) * piece, piece), :] = jnp.where(
+                at < count, held_ref[here, :], crossed_ref[there, :]
+            )
+
+
+def product_kernel(cols, plane, piece, list_ref, blocks_ref, got_ref, out_ref, held_ref):
     per_row = cols * SLOTS
-    first = lax.axis_index("row") * per_row
+    first = (2 * lax.axis_index("z") + lax.axis_index("y")) * per_row
     held_ref[: SLOTS * BS, :] = blocks_ref[...]
-    for p in range(devices):
-        for part in range(q):
-            held_ref[pl.ds(SLOTS * BS + q * p + part, CAP, stride=BS), :] = piece_ref[
-                p * CAP : (p + 1) * CAP, part * BS : (part + 1) * BS
-            ]
+    for p in range(plane):
+        for m in range(CAP):
+            held_ref[pl.ds((SLOTS + m) * BS + p * piece, piece), :] = got_ref[pl.ds((p * CAP + m) * piece, piece), :]
     out_ref[...] = jnp.zeros_like(out_ref)
 
     def block(at):
@@ -252,58 +284,79 @@
 
 
 def packed_body(blocks, block_rows, block_cols):
-    rows, cols = lax.axis_size("row"), lax.axis_size("col")
+    planes, cols = lax.axis_size("z"), lax.axis_size("col")
+    rows = 2 * planes
+    plane = 2 * cols
     devices = rows * cols
     n = devices * SLOTS
-    q = BS // devices
+    piece = BS // plane
     flat = blocks.reshape(SLOTS * BS, BS)
     params = pltpu.CompilerParams(vmem_limit_bytes=VMEM_LIMIT)
     vmem = pl.BlockSpec(memory_space=pltpu.VMEM)
     smem = pl.BlockSpec(memory_space=pltpu.SMEM)
-    spread = pl.pallas_call(
-        spread_kernel,
-        out_shape=jax.ShapeDtypeStruct((devices, SLOTS, (q + 1) * BS), jnp.float32),
-        in_specs=[vmem] * 3,
-        out_specs=vmem,
-        compiler_params=params,
-        name="spread",
-    )(flat, block_rows[0], block_cols[0])
-    pieces = lax.all_to_all(spread, ("row", "col"), 0, 0).reshape(n, (q + 1) * BS)
-    send, listed, most = pl.pallas_call(
+
+    idx = jnp.concatenate([block_rows[0], block_cols[0]])
+    idx = lax.all_to_all(jnp.broadcast_to(idx[None], (devices, 2, SLOTS)), ("z", "y", "col"), 0, 0)
+    spread = blocks.reshape(SLOTS, plane, piece, BS).transpose(1, 0, 2, 3)
+    held = lax.all_to_all(spread, ("y", "col"), 0, 0).reshape(plane * SLOTS * piece, BS)
+    cross, give, listed, most = pl.pallas_call(
         lambda *refs: plan_kernel(rows, cols, *refs),
         out_shape=(
-            jax.ShapeDtypeStruct((devices * CAP, q * BS), jnp.float32),
+            jax.ShapeDtypeStruct((8, BS), jnp.int32),
+            jax.ShapeDtypeStruct((plane, BS), jnp.int32),
             jax.ShapeDtypeStruct((8, n), jnp.int32),
             jax.ShapeDtypeStruct((1, 1), jnp.int32),
         ),
         in_specs=[vmem],
-        out_specs=(vmem, vmem, smem),
+        out_specs=(vmem, vmem, vmem, smem),
         compiler_params=params,
         name="plan",
-    )(pieces)
+    )(idx)
 
     def packed():
-        got = lax.all_to_all(send.reshape(devices, CAP, q * BS), ("row", "col"), 0, 0)
         out = pl.pallas_call(
-            lambda *refs: product_kernel(rows, cols, *refs),
+            lambda *refs: cross_kernel(planes, piece, *refs),
+            out_shape=jax.ShapeDtypeStruct((planes * ZCAP * piece, BS), jnp.float32),
+            in_specs=[smem, vmem],
+            out_specs=vmem,
+            compiler_params=params,
+            name="cross",
+        )(cross, held)
+        crossed = lax.all_to_all(out.reshape(planes, ZCAP, piece, BS), "z", 0, 0)
+        out = pl.pallas_call(
+            lambda *refs: give_kernel(plane, piece, *refs),
+            out_shape=jax.ShapeDtypeStruct((plane * CAP * piece, BS), jnp.float32),
+            in_specs=[smem, vmem, vmem],
+            out_specs=vmem,
+            compiler_params=params,
+            name="give",
+        )(give, held, crossed.reshape(planes * ZCAP * piece, BS))
+        got = lax.all_to_all(out.reshape(plane, CAP, piece, BS), ("y", "col"), 0, 0)
+        out = pl.pallas_call(
+            lambda *refs: product_kernel(cols, plane, piece, *refs),
             out_shape=jax.ShapeDtypeStruct((SLOTS * BS, BS), jnp.float32),
             in_specs=[smem, vmem, vmem],
             out_specs=vmem,
             scratch_shapes=[pltpu.VMEM(((SLOTS + CAP) * BS, BS), jnp.float32)],
             compiler_params=params,
             name="products",
-        )(listed, flat, got.reshape(devices * CAP, q * BS))
+        )(listed, flat, got.reshape(plane * CAP * piece, BS))
         return out.reshape(blocks.shape)
 
-    return lax.cond(most[0, 0] <= CAP, packed, lambda: whole_tiles(blocks, block_rows, block_cols))
+    return lax.cond(most[0, 0] <= 0, packed, lambda: whole_tiles(blocks, block_rows, block_cols))
 
 
 def solution(mesh):
-    small = mesh.shape["col"] == SECTIONS and mesh.devices.size * SLOTS <= 256
+    rows, cols = mesh.devices.shape
+    if cols == SECTIONS and rows == 2 * SECTIONS:
+        body, row = packed_body, ("z", "y")
+        mesh = jax.sharding.Mesh(mesh.devices.reshape(rows // 2, 2, cols), ("z", "y", "col"))
+    else:
+        body, row = general_body, "row"
     return jax.shard_map(
-        packed_body if small else general_body,
+        body,
         mesh=mesh,
-        in_specs=(P("row", "col", None, None, None), P("row", "col", None), P("row", "col", None)),
-        out_specs=P("row", "col", None, None, None),
+        in_specs=(P(row, "col", None, None, None), P(row, "col", None), P(row, "col", None)),
+        out_specs=P(row, "col", None, None, None),
         check_vma=False,
     )

time: 54 us -> 58.1 us (1.076)
  waiting for transfers between devices: 17.9 us -> 12.8 us
  blocking collectives: 19.1 us -> 23.1 us
  starting transfers between devices: 7.3 us -> 10.8 us
  local copies, waits for them, and re-layouts: 0.8 us -> 3.3 us
  Pallas kernels: 7.92 us -> 6.72 us
  other arithmetic: 0 us -> 0.74 us
    all_to_all x1 -> x2, waiting for transfers between devices: 17.9 us -> 12.8 us  [the longest x1 7.41 us: packed_body(): lax.all_to_all(spread, ('y', 'col'), 0, 0)]
    all_to_all x1 -> x2, blocking collectives: 19.1 us -> 23.1 us  [the longest x1 13.6 us: packed(): got = lax.all_to_all(out.reshape(plane, CAP, piece, BS), ('y', 'col'), 0, 0)]
    all_to_all x1 -> x2, starting transfers between devices: 7.3 us -> 10.8 us  [the longest x1 7.3 us: packed_body(): lax.all_to_all(jnp.broadcast_to(idx[None], (devices, 2, SLOTS)), ('z', 'y...]
    transpose x0 -> x1, local copies, waits for them, and re-layouts: none -> 1.89 us  [packed_body(): spread = blocks.reshape(SLOTS, plane, piece, BS).transpose(1, 0, 2, 3)]
    pallas_call x2 -> x3, Pallas kernels: 6.07 us -> 5.02 us  [the longest x1 3.55 us: packed(): pl.pallas_call(lambda *refs: product_kernel(cols, plane, piece, *refs), o...]
    concatenate x0 -> x1, other arithmetic: none -> 0.74 us  [packed_body(): idx = jnp.concatenate([block_rows[0], block_cols[0]])]
    broadcast_in_dim x0 -> x1, local copies, waits for them, and re-layouts: none -> 0.62 us  [packed_body(): jnp.broadcast_to(idx[None], (devices, 2, SLOTS))]
  transfers between devices with their start and end apart: 1 -> 2, of which waited for: 1 -> 2; matrix products, arithmetic and copies ran while one was open for 0% -> 3% of each run, Pallas kernels for 0% -> 3%
where the time goes in v2:
time: 58.1 us
  blocking collectives  23.1 us (40%)
  waiting for transfers between devices  12.8 us (22%)
  starting transfers between devices  10.8 us (19%)
  Pallas kernels  6.72 us (12%)
  local copies, waits for them, and re-layouts  3.3 us (6%)
  other arithmetic  0.74 us (1%)
  between operations  0.61 us (1%)
    all_to_all x1, blocking collectives, packed(): got = lax.all_to_all(out.reshape(plane, CAP, piece, BS), ('y', 'col'), 0, 0)  13.6 us
    all_to_all x1, blocking collectives, packed(): crossed = lax.all_to_all(out.reshape(planes, ZCAP, piece, BS), 'z', 0, 0)  9.51 us
    all_to_all x1, waiting for transfers between devices, packed_body(): lax.all_to_all(spread, ('y', 'col'), 0, 0)  7.41 us
    all_to_all x1, starting transfers between devices, packed_body(): lax.all_to_all(jnp.broadcast_to(idx[None], (devices, 2, SLOTS)), ('z', 'y...  7.3 us
    all_to_all x1, waiting for transfers between devices, packed_body(): lax.all_to_all(jnp.broadcast_to(idx[None], (devices, 2, SLOTS)), ('z', 'y...  5.36 us
    pallas_call x1, Pallas kernels, packed(): pl.pallas_call(lambda *refs: product_kernel(cols, plane, piece, *refs), o...  3.55 us
    all_to_all x1, starting transfers between devices, packed_body(): lax.all_to_all(spread, ('y', 'col'), 0, 0)  3.49 us
    transpose x1, local copies, waits for them, and re-layouts, packed_body(): spread = blocks.reshape(SLOTS, plane, piece, BS).transpose(1, 0, 2, 3)  1.89 us
  transfers between devices with their start and end apart: 2, of which 2 were waited for; matrix products, arithmetic and copies ran while one was open for 3% of the time, Pallas kernels for 3%

profile of v2, /device:TPU:0, one launch (start us, length us, event | category | flops | bytes accessed | tf_op | source)
XLA Modules:
  0.0 58.1 jit_solution(14484728423931424147)
XLA Ops:
  0.0 0.0 copy-start.3
  0.0 0.0 copy-start.4
  0.0 0.0 copy-start.2
  0.0 0.7 %pad_add_fusion.2 = s32[2,8]{1,0:T(2,128)S(1)} fusion(s32[1,8]{1,0:T(1,128)} %bitcast.103, s32[1,8]{1,0:T(1,128)} %bitcast.98), kind=kLoop, calls=%fused_computation.49 | loop fusion | flops 16 | bytes 128 | tf_op jit(solution)/shard_map/concatenate | solution.py:298
  0.7 0.6 %broadcast_in_dim.114 = s32[32,2,8]{2,1,0:T(2,128)} broadcast(s32[2,8]{1,0:T(2,128)S(1)} %pad_add_fusion.2), dimensions={1,2} | broadcast | bytes 2112 | tf_op jit(solution)/shard_map/broadcast_in_dim | solution.py:299
  1.4 7.3 %all-to-all-start.8 = ((s32[32,2,8]{2,1,0:T(2,128)}), s32[32,2,8]{2,1,0:T(2,128)S(1)}, u32[]{:S(2)}, u32[]{:S(2)}) async-start(s32[32,2,8]{2,1,0:T(2,128)} %broadcast_in_dim.114), calls=%async_computation.8 | async-start | bytes 65536 | tf_op jit(solution)/shard_map/all_to_all | solution.py:299
  8.7 1.9 %copy.17 = f32[8,8,16,128]{3,2,1,0:T(8,128)} copy(f32[8,8,16,128]{3,2,0,1:T(8,128)} %bitcast.92) | data formatting | bytes 1048576 | tf_op jit(solution)/shard_map/transpose | solution.py:300
  10.6 5.4 %all-to-all-done.8.refs_0_ = s32[32,2,8]{2,1,0:T(2,128)S(1)} async-done(((s32[32,2,8]{2,1,0:T(2,128)}), s32[32,2,8]{2,1,0:T(2,128)S(1)}, u32[]{:S(2)}, u32[]{:S(2)}) %all-to-all-start.8) | async-done | bytes 2080 | tf_op jit(solution)/shard_map/all_to_all | solution.py:299
  15.9 3.5 %all-to-all-start.9 = ((f32[8,8,16,128]{3,2,1,0:T(8,128)}), f32[8,8,16,128]{3,2,1,0:T(8,128)S(1)}, u32[]{:S(2)}, u32[]{:S(2)}) async-start(f32[8,8,16,128]{3,2,1,0:T(8,128)} %copy.17), calls=%async_computation.9 | async-start | bytes 1048576 | tf_op jit(solution)/shard_map/all_to_all | solution.py:301
  19.4 1.7 %plan.1 = (s32[8,128]{1,0:T(8,128)S(1)}, s32[8,128]{1,0:T(8,128)S(1)}, s32[8,256]{1,0:T(8,128)S(1)}, s32[1,1]{1,0:T(1,128)}) custom-call(s32[32,2,8]{2,1,0:T(2,128)S(1)} %all-to-all-done.8.refs_0_), custom_call_target="tpu_custom_call" | custom-call | tf_op jit(solution)/shard_map/plan/pallas_call | solution.py:302
  21.7 7.4 %all-to-all-done.9 = f32[8,8,16,128]{3,2,1,0:T(8,128)S(1)} async-done(((f32[8,8,16,128]{3,2,1,0:T(8,128)}), f32[8,8,16,128]{3,2,1,0:T(8,128)S(1)}, u32[]{:S(2)}, u32[]{:S(2)}) %all-to-all-start.9) | async-done | bytes 524320 | tf_op jit(solution)/shard_map/all_to_all | solution.py:301
  29.1 0.0 copy-done.3
  29.1 0.0 copy-done.4
  29.1 0.0 copy-done.2
  29.1 28.2 %conditional.1 = (f32[1,1,8,128,128]{4,3,2,1,0:T(8,128)S(1)}) conditional(s32[]{:T(128)} %bitcast.17, (f32[1,1,8,128,128]{4,3,2,1,0:T(8,128)S(1)}, s32[1,1,8]{2,1,0:T(1,128)S(1)}, s32[1,1,8]{2,1,0:T(1,128)S(1)}) %tuple.88, (f32[1,1,8,128,128]{4,3,2,1,0:T(8,128)S(1)}, f32[8,8,16,128]{3,2,1,0:T(8,128)S(1)}, s32[8,128]{1,0:T(8,128)S(1)}, ...), branch_computations={%region_0.9_spmd, %region_9.10_spmd} | conditional | flops 806364224 | bytes 51397016 | solution.py:346
  29.1 0.6 %cross.1 = f32[512,128]{1,0:T(8,128)S(1)} custom-call(s32[8,128]{1,0:T(8,128)S(1)} %get-tuple-element.413.refs_0_, f32[1024,128]{1,0:T(8,128)S(1)} %bitcast.96), custom_call_target="tpu_custom_call" | custom-call | tf_op jit(solution)/shard_map/cond/branch_1_fun/cross/pallas_call | solution.py:317
  29.8 9.5 %all_to_all.59 = f32[4,8,16,128]{3,2,1,0:T(8,128)S(1)} all-to-all(f32[4,8,16,128]{3,2,1,0:T(8,128)S(1)} %bitcast.87), channel_id=1, replica_groups=mesh['z'=4,'y'=2,'col'=4] {'z'}, dimensions={0} | all-to-all | bytes 524288 | tf_op jit(solution)/shard_map/cond/branch_1_fun/all_to_all | solution.py:325
  39.3 0.8 %give.1 = f32[1024,128]{1,0:T(8,128)S(1)} custom-call(s32[8,128]{1,0:T(8,128)S(1)} %get-tuple-element.411.refs_0_, f32[1024,128]{1,0:T(8,128)S(1)} %bitcast.97, f32[512,128]{1,0:T(8,128)S(1)} %bitcast.86), custom_call_target="tpu_custom_call" | custom-call | tf_op jit(solution)/shard_map/cond/branch_1_fun/give/pallas_call | solution.py:326
  40.1 13.6 %all_to_all.60 = f32[8,8,16,128]{3,2,1,0:T(8,128)S(1)} all-to-all(f32[8,8,16,128]{3,2,1,0:T(8,128)S(1)} %bitcast.85), channel_id=1, replica_groups=mesh['z'=4,'y'=2,'col'=4] {'y','col'}, dimensions={0} | all-to-all | bytes 1048576 | tf_op jit(solution)/shard_map/cond/branch_1_fun/all_to_all | solution.py:334
  53.7 3.5 %products.1 = f32[1024,128]{1,0:T(8,128)S(1)} custom-call(s32[8,256]{1,0:T(8,128)S(1)} %get-tuple-element.409.refs_0_, f32[1024,128]{1,0:T(8,128)S(1)} %bitcast.95, f32[1024,128]{1,0:T(8,128)S(1)} %bitcast.84), custom_call_target="tpu_custom_call" | custom-call | tf_op jit(solution)/shard_map/cond/branch_1_fun/products/pallas_call | solution.py:335
  57.3 0.0 copy-start.1
  57.3 0.8 %copy-done.1 = f32[1,1,8,128,128]{4,3,2,1,0:T(8,128)} copy-done((f32[1,1,8,128,128]{4,3,2,1,0:T(8,128)}, f32[1,1,8,128,128]{4,3,2,1,0:T(8,128)S(1)}, u32[]{:S(2)}) %copy-start.1) | copy-done | bytes 524312
Async XLA Ops:
  0.0 29.1 %copy-start.3 = (s32[1,1,8]{2,1,0:T(1,128)S(1)}, s32[1,1,8]{2,1,0:T(1,128)}, u32[]{:S(2)}) copy-start(s32[1,1,8]{2,1,0:T(1,128)} %param.8) | copy-start | bytes 100
  0.0 29.1 %copy-start.4 = (s32[1,1,8]{2,1,0:T(1,128)S(1)}, s32[1,1,8]{2,1,0:T(1,128)}, u32[]{:S(2)}) copy-start(s32[1,1,8]{2,1,0:T(1,128)} %param.9) | copy-start | bytes 100
  0.0 29.1 %copy-start.2 = (f32[1,1,8,128,128]{4,3,2,1,0:T(8,128)S(1)}, f32[1,1,8,128,128]{4,3,2,1,0:T(8,128)}, u32[]{:S(2)}) copy-start(f32[1,1,8,128,128]{4,3,2,1,0:T(8,128)} %param.7) | copy-start | bytes 1572868
  1.4 14.6 %all-to-all-start.8 = ((s32[32,2,8]{2,1,0:T(2,128)}), s32[32,2,8]{2,1,0:T(2,128)S(1)}, u32[]{:S(2)}, u32[]{:S(2)}) async-start(s32[32,2,8]{2,1,0:T(2,128)} %broadcast_in_dim.114), calls=%async_computation.8 | async-start | bytes 65536 | tf_op jit(solution)/shard_map/all_to_all | solution.py:299
  15.9 13.2 %all-to-all-start.9 = ((f32[8,8,16,128]{3,2,1,0:T(8,128)}), f32[8,8,16,128]{3,2,1,0:T(8,128)S(1)}, u32[]{:S(2)}, u32[]{:S(2)}) async-start(f32[8,8,16,128]{3,2,1,0:T(8,128)} %copy.17), calls=%async_computation.9 | async-start | bytes 1048576 | tf_op jit(solution)/shard_map/all_to_all | solution.py:301
  57.3 0.8 %copy-start.1 = (f32[1,1,8,128,128]{4,3,2,1,0:T(8,128)}, f32[1,1,8,128,128]{4,3,2,1,0:T(8,128)S(1)}, u32[]{:S(2)}) copy-start(f32[1,1,8,128,128]{4,3,2,1,0:T(8,128)S(1)} %get-tuple-element.680) | copy-start | bytes 1572868

commit v3 on v2

--- a/solution.py
+++ b/solution.py
@@ -139,16 +139,18 @@
     return lax.dot_general(a, b, dims, preferred_element_type=jnp.float32)
 
 
-def plan_kernel(rows, cols, idx_ref, cross_ref, give_ref, list_ref, most_ref):
+def plan_kernel(rows, cols, *refs):
+    planes = rows // 2
+    idx_refs = refs[: 2 * cols]
+    cross_ref, give_ref, list_ref, most_ref = refs[2 * cols :]
     devices = rows * cols
-    planes = rows // 2
     plane = 2 * cols
     n = devices * SLOTS
     in_plane = plane * SLOTS
     rb = NBLK // rows
     cb = NBLK // cols
     per_row = cols * SLOTS
-    my_plane = lax.axis_index("z")
+    my_plane, my_p = lax.axis_index("z"), lax.axis_index(("y", "col"))
     my_row = 2 * my_plane + lax.axis_index("y")
     my_col = lax.axis_index("col")
     me = my_row * cols + my_col
@@ -157,7 +159,7 @@
     lane = lax.broadcasted_iota(jnp.int32, (1, n), 1)
     dev = lax.broadcasted_iota(jnp.int32, (devices, 1), 0)
     dev_r = lax.broadcasted_iota(jnp.int32, (1, devices), 1)
-    slot = lax.broadcasted_iota(jnp.int32, (1, SLOTS), 1)
+    slot = lax.broadcasted_iota(jnp.int32, (1, BS), 1)
     diagonal = sub == lane
 
     def as_row(column):
@@ -166,11 +168,15 @@
     def as_column(row):
         return jnp.sum(jnp.where(diagonal, row, 0.0), axis=1, keepdims=True)
 
-    repeat = ind((sub // SLOTS) == dev_r)
+    told = jnp.concatenate([ref[ref.shape[0] - 8 :, :] for ref in idx_refs])
+    at = lax.broadcasted_iota(jnp.int32, (1, 8 * plane), 1)
+    from_p = (at // 8) ^ my_p
+    from_plane = (at % 8) ^ my_plane
+    repeat = ind(((sub // SLOTS) == from_plane * plane + from_p) & (at % 8 < planes))
+    values = mm(repeat, bf(told))
 
     def column(k):
-        values = mm(repeat, bf(idx_ref[:, k, :].astype(jnp.float32)))
-        return jnp.sum(jnp.where((sub % SLOTS) == slot, values, 0.0), axis=1, keepdims=True)
+        return jnp.sum(jnp.where((sub % SLOTS) == slot - k * SLOTS, values, 0.0), axis=1, keepdims=True)
 
     up = ((sub // per_row) * rb).astype(jnp.float32)
     along = (((sub // SLOTS) % cols) * cb).astype(jnp.float32)
@@ -203,7 +209,8 @@
 
     lanes = lax.broadcasted_iota(jnp.int32, (1, BS), 1)
     mine_z = (lane // in_plane) == my_plane
-    local = (lane % in_plane).astype(jnp.float32)
+    local = ((((lane // SLOTS) % plane) ^ my_p) * SLOTS + lane % SLOTS).astype(jnp.float32)
+    away = in_plane + ZCAP * (((lane // in_plane) ^ my_plane) - 1)
     cross = jnp.zeros(cross_ref.shape, jnp.float32)
     for m in range(ZCAP):
         one = jnp.sum(jnp.where(mine_z & (zpos == m), local, 0.0), axis=1, keepdims=True)
@@ -211,7 +218,7 @@
     cross_ref[...] = cross.astype(jnp.int32)
 
     from_z = jnp.sum(jnp.where(zed == my_plane, zpos, 0.0), axis=0, keepdims=True)
-    source = jnp.where(mine_z, local, in_plane + ZCAP * (lane // in_plane).astype(jnp.float32) + from_z)
+    source = jnp.where(mine_z, local, away.astype(jnp.float32) + from_z)
     pick = lax.broadcasted_iota(jnp.int32, (plane, 1), 0) + plane * my_plane
     pos_p = mm(ind(pick == dev_r), bf(pos))
     give = jnp.zeros(give_ref.shape, jnp.float32)
@@ -234,32 +241,68 @@
     list_ref[...] = listed.astype(jnp.int32) - 1
 
 
-def cross_kernel(planes, piece, cross_ref, held_ref, out_ref):
-    for z in range(planes):
-        for m in range(ZCAP):
-            at = pl.ds(pl.multiple_of(cross_ref[z, m] * piece, piece), piece)
-            out_ref[pl.ds((z * ZCAP + m) * piece, piece), :] = held_ref[at, :]
-
-
-def give_kernel(plane, piece, give_ref, held_ref, crossed_ref, out_ref):
-    count = held_ref.shape[0] // piece
-    for p in range(plane):
-        for m in range(CAP):
-            at = give_ref[p, m]
-            here = pl.ds(pl.multiple_of(jnp.minimum(at, count - 1) * piece, piece), piece)
-            there = pl.ds(pl.multiple_of(jnp.maximum(at - count, 0) * piece, piece), piece)
-            out_ref[pl.ds((p * CAP + m) * piece, piece), :] = jnp.where(
-                at < count, held_ref[here, :], crossed_ref[there, :]
+def spread_kernel(plane, piece, blocks_ref, *refs):
+    idx_refs, outs = refs[:-plane], refs[-plane:]
+    my_p = lax.axis_index(("y", "col"))
+    sub = lax.broadcasted_iota(jnp.int32, (8, BS), 0)
+    lane = lax.broadcasted_iota(jnp.int32, (8, BS), 1)
+    wide = lax.broadcasted_iota(jnp.int32, (SLOTS, BS), 1)
+    shift = lax.broadcasted_iota(jnp.int32, (SLOTS, BS), 0)
+    told = jnp.zeros((8, BS), jnp.float32)
+    for k, ref in enumerate(idx_refs):
+        for half in range(2):
+            place = ind(wide == shift + half * SLOTS)
+            row = jnp.broadcast_to(ref[half : half + 1, :].astype(jnp.float32), (8, SLOTS))
+            told = jnp.where(
+                (sub == k) & (lane // SLOTS == half), mm(bf(row), place), told
             )
-
-
-def product_kernel(cols, plane, piece, list_ref, blocks_ref, got_ref, out_ref, held_ref):
+    for m, out_ref in enumerate(outs):
+        p = my_p ^ m
+        for t in range(SLOTS):
+            at = pl.ds(pl.multiple_of(t * BS + p * piece, piece), piece)
+            out_ref[t * piece : (t + 1) * piece, :] = blocks_ref[at, :]
+        out_ref[SLOTS * piece :, :] = told
+
+
+def cross_kernel(planes, plane, piece, cross_ref, *refs):
+    piece_refs, outs, held_ref = refs[:plane], refs[plane:-1], refs[-1]
+    size = SLOTS * piece
+    for m, ref in enumerate(piece_refs):
+        held_ref[m * size : (m + 1) * size, :] = ref[:size, :]
+    my_plane = lax.axis_index("z")
+    for m, out_ref in enumerate(outs):
+        z = my_plane ^ (m + 1)
+        for k in range(ZCAP):
+            at = pl.ds(pl.multiple_of(cross_ref[z, k] * piece, piece), piece)
+            out_ref[k * piece : (k + 1) * piece, :] = held_ref[at, :]
+
+
+def give_kernel(planes, plane, piece, give_ref, held_ref, *refs):
+    crossed_refs, outs, all_ref = refs[: planes - 1], refs[planes - 1 : -1], refs[-1]
+    here = held_ref.shape[0]
+    size = ZCAP * piece
+    all_ref[:here, :] = held_ref[...]
+    for m, ref in enumerate(crossed_refs):
+        all_ref[here + m * size : here + (m + 1) * size, :] = ref[...]
+    my_p = lax.axis_index(("y", "col"))
+    for m, out_ref in enumerate(outs):
+        p = my_p ^ m
+        for k in range(CAP):
+            at = pl.ds(pl.multiple_of(give_ref[p, k] * piece, piece), piece)
+            out_ref[k * piece : (k + 1) * piece, :] = all_ref[at, :]
+
+
+def product_kernel(cols, plane, piece, list_ref, blocks_ref, *refs):
+    got_refs, out_ref, held_ref = refs[:plane], refs[plane], refs[plane + 1]
     per_row = cols * SLOTS
     first = (2 * lax.axis_index("z") + lax.axis_index("y")) * per_row
+    my_p = lax.axis_index(("y", "col"))
     held_ref[: SLOTS * BS, :] = blocks_ref[...]
-    for p in range(plane):
-        for m in range(CAP):
-            held_ref[pl.ds((SLOTS + m) * BS + p * piece, piece), :] = got_ref[pl.ds((p * CAP + m) * piece, piece), :]
+    for m, ref in enumerate(got_refs):
+        p = my_p ^ m
+        for k in range(CAP):
+            at = pl.ds(pl.multiple_of((SLOTS + k) * BS + p * piece, piece), piece)
+            held_ref[at, :] = ref[k * piece : (k + 1) * piece, :]
     out_ref[...] = jnp.zeros_like(out_ref)
 
     def block(at):
@@ -283,65 +326,84 @@
     lax.fori_loop(0, per_row, entry, 0)
 
 
+def swapped(arrays, axis):
+    count = lax.axis_size(axis)
+    swap = lambda x, m: lax.ppermute(x, axis, [(i, i ^ m) for i in range(count)])
+    return arrays[:1] + [swap(x, m) for m, x in enumerate(arrays) if m]
+
+
 def packed_body(blocks, block_rows, block_cols):
     planes, cols = lax.axis_size("z"), lax.axis_size("col")
     rows = 2 * planes
     plane = 2 * cols
-    devices = rows * cols
-    n = devices * SLOTS
+    n = rows * cols * SLOTS
     piece = BS // plane
+    in_plane = ("y", "col")
     flat = blocks.reshape(SLOTS * BS, BS)
     params = pltpu.CompilerParams(vmem_limit_bytes=VMEM_LIMIT)
     vmem = pl.BlockSpec(memory_space=pltpu.VMEM)
     smem = pl.BlockSpec(memory_space=pltpu.SMEM)
 
+    def floats(height):
+        return jax.ShapeDtypeStruct((height, BS), jnp.float32)
+
+    def call(kernel, name, ins, outs, scratch=(), specs=None):
+        return pl.pallas_call(
+            kernel,
+            out_shape=outs,
+            in_specs=ins,
+            out_specs=[vmem] * len(outs) if specs is None else specs,
+            scratch_shapes=scratch,
+            compiler_params=params,
+            name=name,
+        )
+
     idx = jnp.concatenate([block_rows[0], block_cols[0]])
-    idx = lax.all_to_all(jnp.broadcast_to(idx[None], (devices, 2, SLOTS)), ("z", "y", "col"), 0, 0)
-    spread = blocks.reshape(SLOTS, plane, piece, BS).transpose(1, 0, 2, 3)
-    held = lax.all_to_all(spread, ("y", "col"), 0, 0).reshape(plane * SLOTS * piece, BS)
-    cross, give, listed, most = pl.pallas_call(
+    line = swapped([idx] * planes, "z")
+    spread = call(
+        lambda *refs: spread_kernel(plane, piece, *refs),
+        "spread",
+        [vmem] * (1 + planes),
+        [floats(SLOTS * piece + 8)] * plane,
+    )(flat, *line)
+    pieces = swapped(list(spread), in_plane)
+    cross, give, listed, most = call(
         lambda *refs: plan_kernel(rows, cols, *refs),
-        out_shape=(
+        "plan",
+        [vmem] * plane,
+        (
             jax.ShapeDtypeStruct((8, BS), jnp.int32),
             jax.ShapeDtypeStruct((plane, BS), jnp.int32),
             jax.ShapeDtypeStruct((8, n), jnp.int32),
             jax.ShapeDtypeStruct((1, 1), jnp.int32),
         ),
-        in_specs=[vmem],
-        out_specs=(vmem, vmem, vmem, smem),
-        compiler_params=params,
-        name="plan",
-    )(idx)
+        specs=(vmem, vmem, vmem, smem),
+    )(*pieces)
 
     def packed():
-        out = pl.pallas_call(
-            lambda *refs: cross_kernel(planes, piece, *refs),
-            out_shape=jax.ShapeDtypeStruct((planes * ZCAP * piece, BS), jnp.float32),
-            in_specs=[smem, vmem],
-            out_specs=vmem,
-            compiler_params=params,
-            name="cross",
-        )(cross, held)
-        crossed = lax.all_to_all(out.reshape(planes, ZCAP, piece, BS), "z", 0, 0)
-        out = pl.pallas_call(
-            lambda *refs: give_kernel(plane, piece, *refs),
-            out_shape=jax.ShapeDtypeStruct((plane * CAP * piece, BS), jnp.float32),
-            in_specs=[smem, vmem, vmem],
-            out_specs=vmem,
-            compiler_params=params,
-            name="give",
-        )(give, held, crossed.reshape(planes * ZCAP * piece, BS))
-        got = lax.all_to_all(out.reshape(plane, CAP, piece, BS), ("y", "col"), 0, 0)
-        out = pl.pallas_call(
+        *crossing, held = call(
+            lambda *refs: cross_kernel(planes, plane, piece, *refs),
+            "cross",
+            [smem] + [vmem] * plane,
+            [floats(ZCAP * piece)] * (planes - 1) + [floats(plane * SLOTS * piece)],
+        )(cross, *pieces)
+        crossed = swapped([held] + crossing, "z")[1:]
+        giving = call(
+            lambda *refs: give_kernel(planes, plane, piece, *refs),
+            "give",
+            [smem] + [vmem] * planes,
+            [floats(CAP * piece)] * plane,
+            [pltpu.VMEM(((plane * SLOTS + (planes - 1) * ZCAP) * piece, BS), jnp.float32)],
+        )(give, held, *crossed)
+        got = swapped(list(giving), in_plane)
+        out = call(
             lambda *refs: product_kernel(cols, plane, piece, *refs),
-            out_shape=jax.ShapeDtypeStruct((SLOTS * BS, BS), jnp.float32),
-            in_specs=[smem, vmem, vmem],
-            out_specs=vmem,
-            scratch_shapes=[pltpu.VMEM(((SLOTS + CAP) * BS, BS), jnp.float32)],
-            compiler_params=params,
-            name="products",
-        )(listed, flat, got.reshape(plane * CAP * piece, BS))
-        return out.reshape(blocks.shape)
+            "products",
+            [smem] + [vmem] * (1 + plane),
+            [floats(SLOTS * BS)],
+            [pltpu.VMEM(((SLOTS + CAP) * BS, BS), jnp.float32)],
+        )(listed, flat, *got)
+        return out[0].reshape(blocks.shape)
 
     return lax.cond(most[0, 0] <= 0, packed, lambda: whole_tiles(blocks, block_rows, block_cols))
 

time: 58.1 us -> 51.8 us (0.89)
  blocking collectives: 23.1 us -> 0 us
  starting transfers between devices: 10.8 us -> 22.7 us
  waiting for transfers between devices: 12.8 us -> 18.5 us
  local copies, waits for them, and re-layouts: 3.3 us -> 0.79 us
  Pallas kernels: 6.72 us -> 8.16 us
    all_to_all x2 -> x0, blocking collectives: 23.1 us -> none  [the longest x1 13.6 us: packed(): got = lax.all_to_all(out.reshape(plane, CAP, piece, BS), ('y', 'col'), 0, 0)]
    ppermute x0 -> x20, starting transfers between devices: none -> 22.7 us  [swapped(): lax.ppermute(x, axis, [(i, i ^ m) for i in range(count)])]
    ppermute x0 -> x20, waiting for transfers between devices: none -> 18.5 us  [swapped(): lax.ppermute(x, axis, [(i, i ^ m) for i in range(count)])]
    all_to_all x2 -> x0, waiting for transfers between devices: 12.8 us -> none  [the longest x1 7.41 us: packed_body(): lax.all_to_all(spread, ('y', 'col'), 0, 0)]
    all_to_all x2 -> x0, starting transfers between devices: 10.8 us -> none  [the longest x1 7.3 us: packed_body(): lax.all_to_all(jnp.broadcast_to(idx[None], (devices, 2, SLOTS)), ('z', 'y...]
    transpose x1 -> x0, local copies, waits for them, and re-layouts: 1.89 us -> none  [packed_body(): spread = blocks.reshape(SLOTS, plane, piece, BS).transpose(1, 0, 2, 3)]
    pallas_call x4 -> x5, Pallas kernels: 6.72 us -> 8.16 us  [the longest x1 3.93 us: packed(): call(lambda *refs: product_kernel(cols, plane, piece, *refs), 'products',...]
    broadcast_in_dim x1 -> x0, local copies, waits for them, and re-layouts: 0.62 us -> none  [packed_body(): jnp.broadcast_to(idx[None], (devices, 2, SLOTS))]
  transfers between devices with their start and end apart: 2 -> 20, of which waited for: 2 -> 10; matrix products, arithmetic and copies ran while one was open for 3% -> 0% of each run, Pallas kernels for 3% -> 0%
where the time goes in v3:
time: 51.8 us; the launch traced here: 51.6 us
  starting transfers between devices  22.7 us (44%)
  waiting for transfers between devices  18.5 us (36%)
  Pallas kernels  8.16 us (16%)
  local copies, waits for them, and re-layouts  0.79 us (2%)
  between operations  0.69 us (1%)
  other arithmetic  0.68 us (1%)
    ppermute x20, starting transfers between devices, swapped(): lax.ppermute(x, axis, [(i, i ^ m) for i in range(count)])  22.7 us
    ppermute x20, waiting for transfers between devices, swapped(): lax.ppermute(x, axis, [(i, i ^ m) for i in range(count)])  18.5 us
    pallas_call x1, Pallas kernels, packed(): call(lambda *refs: product_kernel(cols, plane, piece, *refs), 'products',...  3.93 us
    pallas_call x1, Pallas kernels, packed_body(): call(lambda *refs: plan_kernel(rows, cols, *refs), 'plan', [vmem] * plane...  1.67 us
    pallas_call x1, Pallas kernels, packed_body(): call(lambda *refs: spread_kernel(plane, piece, *refs), 'spread', [vmem] *...  1.19 us
  transfers between devices with their start and end apart: 20, of which 10 were waited for; matrix products, arithmetic and copies ran while one was open for 0% of the time, Pallas kernels for 0%

profile of v3, /device:TPU:0, one launch (start us, length us, event | category | flops | bytes accessed | tf_op | source)
XLA Modules:
  0.0 51.6 jit_solution(5721369915961386391)
XLA Ops:
  0.7 3.0 %collective-permute-start.10 = (s32[2,8]{1,0:T(2,128)S(1)}, s32[2,8]{1,0:T(2,128)S(1)}, u32[]{:S(2)}, u32[]{:S(2)}) collective-permute-start(s32[2,8]{1,0:T(2,128)S(1)} %pad_add_fusion.2.refs_1_), channel_id=1, source_target_pairs={{0,8},{8,0},{16,24},{24,16},{1,9},{9,1},{17,25},{25,17},{2,10},{10... | collective-permute-start | bytes 200 | tf_op jit(solution)/shard_map/ppermute | solution.py:331
  3.7 2.6 %collective-permute-start.11 = (s32[2,8]{1,0:T(2,128)S(1)}, s32[2,8]{1,0:T(2,128)S(1)}, u32[]{:S(2)}, u32[]{:S(2)}) collective-permute-start(s32[2,8]{1,0:T(2,128)S(1)} %pad_add_fusion.2.refs_1_), channel_id=1, source_target_pairs={{0,16},{8,24},{16,0},{24,8},{1,17},{9,25},{17,1},{25,9},{2,18},{10... | collective-permute-start | bytes 200 | tf_op jit(solution)/shard_map/ppermute | solution.py:331
  6.3 1.9 %collective-permute-done.11.refs_3_ = s32[2,8]{1,0:T(2,128)S(1)} collective-permute-done((s32[2,8]{1,0:T(2,128)S(1)}, s32[2,8]{1,0:T(2,128)S(1)}, u32[]{:S(2)}, u32[]{:S(2)}) %collective-permute-start.11) | collective-permute-done | bytes 96 | tf_op jit(solution)/shard_map/ppermute | solution.py:331
  8.2 3.5 %collective-permute-done.12.refs_4_ = s32[2,8]{1,0:T(2,128)S(1)} collective-permute-done((s32[2,8]{1,0:T(2,128)S(1)}, s32[2,8]{1,0:T(2,128)S(1)}, u32[]{:S(2)}, u32[]{:S(2)}) %collective-permute-start.12) | collective-permute-done | bytes 96 | tf_op jit(solution)/shard_map/ppermute | solution.py:331
  11.7 1.2 %spread.1 = (f32[136,128]{1,0:T(8,128)S(1)}, f32[136,128]{1,0:T(8,128)S(1)}, f32[136,128]{1,0:T(8,128)S(1)}, f32[136,128]{1,0:T(8,128)S(1)}, f32[136,128]{1,0:T(...) custom-call(f32[1024,128]{1,0:T(8,128)} %bitcast.80, ...), custom_call_target="tpu_custom_call" | custom-call | tf_op jit(solution)/shard_map/spread/pallas_call | solution.py:363
  12.9 1.6 %collective-permute-start.14 = (f32[136,128]{1,0:T(8,128)S(1)}, f32[136,128]{1,0:T(8,128)S(1)}, u32[]{:S(2)}, u32[]{:S(2)}) collective-permute-start(f32[136,128]{1,0:T(8,128)S(1)} %get-tuple-element.459), channel_id=1, source_target_pairs={{0,2},{1,3},{2,0},{3,1},{4,6},{5,7},{6,4},{7,5},{8,10},{9,11},{10,... | collective-permute-start | bytes 208904 | tf_op jit(solution)/shard_map/ppermute | solution.py:331
  14.8 1.5 %collective-permute-start.16 = (f32[136,128]{1,0:T(8,128)S(1)}, f32[136,128]{1,0:T(8,128)S(1)}, u32[]{:S(2)}, u32[]{:S(2)}) collective-permute-start(f32[136,128]{1,0:T(8,128)S(1)} %get-tuple-element.461), channel_id=1, source_target_pairs={{0,4},{1,5},{2,6},{3,7},{4,0},{5,1},{6,2},{7,3},{8,12},{9,13},{10,... | collective-permute-start | bytes 208904 | tf_op jit(solution)/shard_map/ppermute | solution.py:331
  16.5 2.4 %collective-permute-start.18 = (f32[136,128]{1,0:T(8,128)S(1)}, f32[136,128]{1,0:T(8,128)S(1)}, u32[]{:S(2)}, u32[]{:S(2)}) collective-permute-start(f32[136,128]{1,0:T(8,128)S(1)} %get-tuple-element.463), channel_id=1, source_target_pairs={{0,6},{1,7},{2,4},{3,5},{4,2},{5,3},{6,0},{7,1},{8,14},{9,15},{10,... | collective-permute-start | bytes 208904 | tf_op jit(solution)/shard_map/ppermute | solution.py:331
  19.2 3.5 %collective-permute-done.17.refs_5_ = f32[136,128]{1,0:T(8,128)S(1)} collective-permute-done((f32[136,128]{1,0:T(8,128)S(1)}, f32[136,128]{1,0:T(8,128)S(1)}, u32[]{:S(2)}, u32[]{:S(2)}) %collective-permute-start.17) | collective-permute-done | bytes 69664 | tf_op jit(solution)/shard_map/ppermute | solution.py:331
  22.8 1.2 %collective-permute-done.19.refs_7_ = f32[136,128]{1,0:T(8,128)S(1)} collective-permute-done((f32[136,128]{1,0:T(8,128)S(1)}, f32[136,128]{1,0:T(8,128)S(1)}, u32[]{:S(2)}, u32[]{:S(2)}) %collective-permute-start.19) | collective-permute-done | bytes 69664 | tf_op jit(solution)/shard_map/ppermute | solution.py:331
  24.0 1.7 %plan.1 = (s32[8,128]{1,0:T(8,128)S(1)}, s32[8,128]{1,0:T(8,128)S(1)}, s32[8,256]{1,0:T(8,128)S(1)}, s32[1,1]{1,0:T(1,128)}) custom-call(f32[136,128]{1,0:T(8,128)S(1)} %get-tuple-element.457.refs_0_, f32[136,128]{1,0:T(8,128)S(1)} %collective-permute-done.13.refs_1_, f32[136,128]{1,0:T(8,128)S(1)} %collective-permute-done.14.refs_2_, ...), custom_call_target="tpu_custom_call" | custom-call | tf_op jit(solution)/shard_map/plan/pallas_call | solution.py:370
  26.3 24.5 %conditional.1 = (f32[1,1,8,128,128]{4,3,2,1,0:T(8,128)S(1)}) conditional(s32[]{:T(128)} %bitcast.12, (f32[1,1,8,128,128]{4,3,2,1,0:T(8,128)}, s32[1,1,8]{2,1,0:T(1,128)}, s32[1,1,8]{2,1,0:T(1,128)}) %tuple.36, (s32[8,128]{1,0:T(8,128)S(1)}, f32[136,128]{1,0:T(8,128)S(1)}, f32[136,128]{1,0:T(8,128)S(1)}, f32[136,128]{1,0:T(8,128)S(1)}, ...), branch_computations={%region_0.9_spmd, %region_9.10_spmd} | conditional | flops 806364224 | bytes 53494504 | solution.py:408
  27.8 3.6 %collective-permute-start.2 = (f32[128,128]{1,0:T(8,128)S(1)}, f32[128,128]{1,0:T(8,128)S(1)}, u32[]{:S(2)}, u32[]{:S(2)}) collective-permute-start(f32[128,128]{1,0:T(8,128)S(1)} %get-tuple-element.436), channel_id=1, source_target_pairs={{0,24},{8,16},{16,8},{24,0},{1,25},{9,17},{17,9},{25,1},{2,26},{10... | collective-permute-start | bytes 196616 | tf_op jit(solution)/shard_map/cond/branch_1_fun/ppermute | solution.py:331
  31.4 0.8 %collective-permute-done.refs_2_ = f32[128,128]{1,0:T(8,128)S(1)} collective-permute-done((f32[128,128]{1,0:T(8,128)S(1)}, f32[128,128]{1,0:T(8,128)S(1)}, u32[]{:S(2)}, u32[]{:S(2)}) %collective-permute-start) | collective-permute-done | bytes 65568 | tf_op jit(solution)/shard_map/cond/branch_1_fun/ppermute | solution.py:331
  32.2 3.5 %collective-permute-done.1.refs_3_ = f32[128,128]{1,0:T(8,128)S(1)} collective-permute-done((f32[128,128]{1,0:T(8,128)S(1)}, f32[128,128]{1,0:T(8,128)S(1)}, u32[]{:S(2)}, u32[]{:S(2)}) %collective-permute-start.1) | collective-permute-done | bytes 65568 | tf_op jit(solution)/shard_map/cond/branch_1_fun/ppermute | solution.py:331
  36.5 1.1 %collective-permute-start.4 = (f32[128,128]{1,0:T(8,128)S(1)}, f32[128,128]{1,0:T(8,128)S(1)}, u32[]{:S(2)}, u32[]{:S(2)}) collective-permute-start(f32[128,128]{1,0:T(8,128)S(1)} %get-tuple-element.439), channel_id=1, source_target_pairs={{0,2},{1,3},{2,0},{3,1},{4,6},{5,7},{6,4},{7,5},{8,10},{9,11},{10,... | collective-permute-start | bytes 196616 | tf_op jit(solution)/shard_map/cond/branch_1_fun/ppermute | solution.py:331
  37.6 0.8 %collective-permute-start.5 = (f32[128,128]{1,0:T(8,128)S(1)}, f32[128,128]{1,0:T(8,128)S(1)}, u32[]{:S(2)}, u32[]{:S(2)}) collective-permute-start(f32[128,128]{1,0:T(8,128)S(1)} %get-tuple-element.440), channel_id=1, source_target_pairs={{0,3},{1,2},{2,1},{3,0},{4,7},{5,6},{6,5},{7,4},{8,11},{9,10},{10,... | collective-permute-start | bytes 196616 | tf_op jit(solution)/shard_map/cond/branch_1_fun/ppermute | solution.py:331
  38.4 0.9 %collective-permute-start.6 = (f32[128,128]{1,0:T(8,128)S(1)}, f32[128,128]{1,0:T(8,128)S(1)}, u32[]{:S(2)}, u32[]{:S(2)}) collective-permute-start(f32[128,128]{1,0:T(8,128)S(1)} %get-tuple-element.441), channel_id=1, source_target_pairs={{0,4},{1,5},{2,6},{3,7},{4,0},{5,1},{6,2},{7,3},{8,12},{9,13},{10,... | collective-permute-start | bytes 196616 | tf_op jit(solution)/shard_map/cond/branch_1_fun/ppermute | solution.py:331
  39.3 0.8 %collective-permute-start.7 = (f32[128,128]{1,0:T(8,128)S(1)}, f32[128,128]{1,0:T(8,128)S(1)}, u32[]{:S(2)}, u32[]{:S(2)}) collective-permute-start(f32[128,128]{1,0:T(8,128)S(1)} %get-tuple-element.442), channel_id=1, source_target_pairs={{0,5},{1,4},{2,7},{3,6},{4,1},{5,0},{6,3},{7,2},{8,13},{9,12},{10,... | collective-permute-start | bytes 196616 | tf_op jit(solution)/shard_map/cond/branch_1_fun/ppermute | solution.py:331
  40.1 1.8 %collective-permute-start.8 = (f32[128,128]{1,0:T(8,128)S(1)}, f32[128,128]{1,0:T(8,128)S(1)}, u32[]{:S(2)}, u32[]{:S(2)}) collective-permute-start(f32[128,128]{1,0:T(8,128)S(1)} %get-tuple-element.443), channel_id=1, source_target_pairs={{0,6},{1,7},{2,4},{3,5},{4,2},{5,3},{6,0},{7,1},{8,14},{9,15},{10,... | collective-permute-start | bytes 196616 | tf_op jit(solution)/shard_map/cond/branch_1_fun/ppermute | solution.py:331
  41.9 0.9 %collective-permute-start.9 = (f32[128,128]{1,0:T(8,128)S(1)}, f32[128,128]{1,0:T(8,128)S(1)}, u32[]{:S(2)}, u32[]{:S(2)}) collective-permute-start(f32[128,128]{1,0:T(8,128)S(1)} %get-tuple-element.444), channel_id=1, source_target_pairs={{0,7},{1,6},{2,5},{3,4},{4,3},{5,2},{6,1},{7,0},{8,15},{9,14},{10,... | collective-permute-start | bytes 196616 | tf_op jit(solution)/shard_map/cond/branch_1_fun/ppermute | solution.py:331
  43.7 1.9 %collective-permute-done.8.refs_8_ = f32[128,128]{1,0:T(8,128)S(1)} collective-permute-done((f32[128,128]{1,0:T(8,128)S(1)}, f32[128,128]{1,0:T(8,128)S(1)}, u32[]{:S(2)}, u32[]{:S(2)}) %collective-permute-start.8) | collective-permute-done | bytes 65568 | tf_op jit(solution)/shard_map/cond/branch_1_fun/ppermute | solution.py:331
  45.5 1.3 %collective-permute-done.9.refs_9_ = f32[128,128]{1,0:T(8,128)S(1)} collective-permute-done((f32[128,128]{1,0:T(8,128)S(1)}, f32[128,128]{1,0:T(8,128)S(1)}, u32[]{:S(2)}, u32[]{:S(2)}) %collective-permute-start.9) | collective-permute-done | bytes 65568 | tf_op jit(solution)/shard_map/cond/branch_1_fun/ppermute | solution.py:331
  46.8 3.9 %products.1 = f32[1024,128]{1,0:T(8,128)S(1)} custom-call(s32[8,256]{1,0:T(8,128)S(1)} %get-tuple-element.421.refs_0_, f32[1024,128]{1,0:T(8,128)} %get-tuple-element.422.refs_1_, f32[128,128]{1,0:T(8,128)S(1)} %get-tuple-element.437.refs_2_, f32[128,128]{1,0:T(8,128)S(1)} %collective-permute-done.3.refs_3_, f32[128,128]{1,0:T(8,128)S(1)} %collective-permute-done.4.refs_4_, ...), custom_call_target="tpu_custom_call" | custom-call | tf_op jit(solution)/shard_map/cond/branch_1_fun/products/pallas_call | solution.py:399
  (25 shorter events, 5.5 us)
Async XLA Ops:
  0.7 5.6 %collective-permute-start.10 = (s32[2,8]{1,0:T(2,128)S(1)}, s32[2,8]{1,0:T(2,128)S(1)}, u32[]{:S(2)}, u32[]{:S(2)}) collective-permute-start(s32[2,8]{1,0:T(2,128)S(1)} %pad_add_fusion.2.refs_1_), channel_id=1, source_target_pairs={{0,8},{8,0},{16,24},{24,16},{1,9},{9,1},{17,25},{25,17},{2,10},{10... | collective-permute-start | bytes 200 | tf_op jit(solution)/shard_map/ppermute | solution.py:331
  3.7 4.5 %collective-permute-start.11 = (s32[2,8]{1,0:T(2,128)S(1)}, s32[2,8]{1,0:T(2,128)S(1)}, u32[]{:S(2)}, u32[]{:S(2)}) collective-permute-start(s32[2,8]{1,0:T(2,128)S(1)} %pad_add_fusion.2.refs_1_), channel_id=1, source_target_pairs={{0,16},{8,24},{16,0},{24,8},{1,17},{9,25},{17,1},{25,9},{2,18},{10... | collective-permute-start | bytes 200 | tf_op jit(solution)/shard_map/ppermute | solution.py:331
  6.3 5.4 %collective-permute-start.12 = (s32[2,8]{1,0:T(2,128)S(1)}, s32[2,8]{1,0:T(2,128)S(1)}, u32[]{:S(2)}, u32[]{:S(2)}) collective-permute-start(s32[2,8]{1,0:T(2,128)S(1)} %pad_add_fusion.2.refs_1_), channel_id=1, source_target_pairs={{0,24},{8,16},{16,8},{24,0},{1,25},{9,17},{17,9},{25,1},{2,26},{10... | collective-permute-start | bytes 200 | tf_op jit(solution)/shard_map/ppermute | solution.py:331
  12.8 3.6 %collective-permute-start.13 = (f32[136,128]{1,0:T(8,128)S(1)}, f32[136,128]{1,0:T(8,128)S(1)}, u32[]{:S(2)}, u32[]{:S(2)}) collective-permute-start(f32[136,128]{1,0:T(8,128)S(1)} %get-tuple-element.458), channel_id=1, source_target_pairs={{0,1},{1,0},{2,3},{3,2},{4,5},{5,4},{6,7},{7,6},{8,9},{9,8},{10,11... | collective-permute-start | bytes 208904 | tf_op jit(solution)/shard_map/ppermute | solution.py:331
  12.9 6.0 %collective-permute-start.14 = (f32[136,128]{1,0:T(8,128)S(1)}, f32[136,128]{1,0:T(8,128)S(1)}, u32[]{:S(2)}, u32[]{:S(2)}) collective-permute-start(f32[136,128]{1,0:T(8,128)S(1)} %get-tuple-element.459), channel_id=1, source_target_pairs={{0,2},{1,3},{2,0},{3,1},{4,6},{5,7},{6,4},{7,5},{8,10},{9,11},{10,... | collective-permute-start | bytes 208904 | tf_op jit(solution)/shard_map/ppermute | solution.py:331
  14.5 4.8 %collective-permute-start.15 = (f32[136,128]{1,0:T(8,128)S(1)}, f32[136,128]{1,0:T(8,128)S(1)}, u32[]{:S(2)}, u32[]{:S(2)}) collective-permute-start(f32[136,128]{1,0:T(8,128)S(1)} %get-tuple-element.460), channel_id=1, source_target_pairs={{0,3},{1,2},{2,1},{3,0},{4,7},{5,6},{6,5},{7,4},{8,11},{9,10},{10,... | collective-permute-start | bytes 208904 | tf_op jit(solution)/shard_map/ppermute | solution.py:331
  14.8 4.5 %collective-permute-start.16 = (f32[136,128]{1,0:T(8,128)S(1)}, f32[136,128]{1,0:T(8,128)S(1)}, u32[]{:S(2)}, u32[]{:S(2)}) collective-permute-start(f32[136,128]{1,0:T(8,128)S(1)} %get-tuple-element.461), channel_id=1, source_target_pairs={{0,4},{1,5},{2,6},{3,7},{4,0},{5,1},{6,2},{7,3},{8,12},{9,13},{10,... | collective-permute-start | bytes 208904 | tf_op jit(solution)/shard_map/ppermute | solution.py:331
  16.3 6.5 %collective-permute-start.17 = (f32[136,128]{1,0:T(8,128)S(1)}, f32[136,128]{1,0:T(8,128)S(1)}, u32[]{:S(2)}, u32[]{:S(2)}) collective-permute-start(f32[136,128]{1,0:T(8,128)S(1)} %get-tuple-element.462), channel_id=1, source_target_pairs={{0,5},{1,4},{2,7},{3,6},{4,1},{5,0},{6,3},{7,2},{8,13},{9,12},{10,... | collective-permute-start | bytes 208904 | tf_op jit(solution)/shard_map/ppermute | solution.py:331
  16.5 6.3 %collective-permute-start.18 = (f32[136,128]{1,0:T(8,128)S(1)}, f32[136,128]{1,0:T(8,128)S(1)}, u32[]{:S(2)}, u32[]{:S(2)}) collective-permute-start(f32[136,128]{1,0:T(8,128)S(1)} %get-tuple-element.463), channel_id=1, source_target_pairs={{0,6},{1,7},{2,4},{3,5},{4,2},{5,3},{6,0},{7,1},{8,14},{9,15},{10,... | collective-permute-start | bytes 208904 | tf_op jit(solution)/shard_map/ppermute | solution.py:331
  18.9 5.0 %collective-permute-start.19 = (f32[136,128]{1,0:T(8,128)S(1)}, f32[136,128]{1,0:T(8,128)S(1)}, u32[]{:S(2)}, u32[]{:S(2)}) collective-permute-start(f32[136,128]{1,0:T(8,128)S(1)} %get-tuple-element.464), channel_id=1, source_target_pairs={{0,7},{1,6},{2,5},{3,4},{4,3},{5,2},{6,1},{7,0},{8,15},{9,14},{10,... | collective-permute-start | bytes 208904 | tf_op jit(solution)/shard_map/ppermute | solution.py:331
  27.0 5.2 %collective-permute-start = (f32[128,128]{1,0:T(8,128)S(1)}, f32[128,128]{1,0:T(8,128)S(1)}, u32[]{:S(2)}, u32[]{:S(2)}) collective-permute-start(f32[128,128]{1,0:T(8,128)S(1)} %get-tuple-element.434), channel_id=1, source_target_pairs={{0,8},{8,0},{16,24},{24,16},{1,9},{9,1},{17,25},{25,17},{2,10},{10... | collective-permute-start | bytes 196616 | tf_op jit(solution)/shard_map/cond/branch_1_fun/ppermute | solution.py:331
  27.1 8.6 %collective-permute-start.1 = (f32[128,128]{1,0:T(8,128)S(1)}, f32[128,128]{1,0:T(8,128)S(1)}, u32[]{:S(2)}, u32[]{:S(2)}) collective-permute-start(f32[128,128]{1,0:T(8,128)S(1)} %get-tuple-element.435), channel_id=1, source_target_pairs={{0,16},{8,24},{16,0},{24,8},{1,17},{9,25},{17,1},{25,9},{2,18},{10... | collective-permute-start | bytes 196616 | tf_op jit(solution)/shard_map/cond/branch_1_fun/ppermute | solution.py:331
  27.8 7.9 %collective-permute-start.2 = (f32[128,128]{1,0:T(8,128)S(1)}, f32[128,128]{1,0:T(8,128)S(1)}, u32[]{:S(2)}, u32[]{:S(2)}) collective-permute-start(f32[128,128]{1,0:T(8,128)S(1)} %get-tuple-element.436), channel_id=1, source_target_pairs={{0,24},{8,16},{16,8},{24,0},{1,25},{9,17},{17,9},{25,1},{2,26},{10... | collective-permute-start | bytes 196616 | tf_op jit(solution)/shard_map/cond/branch_1_fun/ppermute | solution.py:331
  36.4 3.6 %collective-permute-start.3 = (f32[128,128]{1,0:T(8,128)S(1)}, f32[128,128]{1,0:T(8,128)S(1)}, u32[]{:S(2)}, u32[]{:S(2)}) collective-permute-start(f32[128,128]{1,0:T(8,128)S(1)} %get-tuple-element.438), channel_id=1, source_target_pairs={{0,1},{1,0},{2,3},{3,2},{4,5},{5,4},{6,7},{7,6},{8,9},{9,8},{10,11... | collective-permute-start | bytes 196616 | tf_op jit(solution)/shard_map/cond/branch_1_fun/ppermute | solution.py:331
  36.5 5.4 %collective-permute-start.4 = (f32[128,128]{1,0:T(8,128)S(1)}, f32[128,128]{1,0:T(8,128)S(1)}, u32[]{:S(2)}, u32[]{:S(2)}) collective-permute-start(f32[128,128]{1,0:T(8,128)S(1)} %get-tuple-element.439), channel_id=1, source_target_pairs={{0,2},{1,3},{2,0},{3,1},{4,6},{5,7},{6,4},{7,5},{8,10},{9,11},{10,... | collective-permute-start | bytes 196616 | tf_op jit(solution)/shard_map/cond/branch_1_fun/ppermute | solution.py:331
  37.6 5.2 %collective-permute-start.5 = (f32[128,128]{1,0:T(8,128)S(1)}, f32[128,128]{1,0:T(8,128)S(1)}, u32[]{:S(2)}, u32[]{:S(2)}) collective-permute-start(f32[128,128]{1,0:T(8,128)S(1)} %get-tuple-element.440), channel_id=1, source_target_pairs={{0,3},{1,2},{2,1},{3,0},{4,7},{5,6},{6,5},{7,4},{8,11},{9,10},{10,... | collective-permute-start | bytes 196616 | tf_op jit(solution)/shard_map/cond/branch_1_fun/ppermute | solution.py:331
  38.4 4.8 %collective-permute-start.6 = (f32[128,128]{1,0:T(8,128)S(1)}, f32[128,128]{1,0:T(8,128)S(1)}, u32[]{:S(2)}, u32[]{:S(2)}) collective-permute-start(f32[128,128]{1,0:T(8,128)S(1)} %get-tuple-element.441), channel_id=1, source_target_pairs={{0,4},{1,5},{2,6},{3,7},{4,0},{5,1},{6,2},{7,3},{8,12},{9,13},{10,... | collective-permute-start | bytes 196616 | tf_op jit(solution)/shard_map/cond/branch_1_fun/ppermute | solution.py:331
  39.3 4.4 %collective-permute-start.7 = (f32[128,128]{1,0:T(8,128)S(1)}, f32[128,128]{1,0:T(8,128)S(1)}, u32[]{:S(2)}, u32[]{:S(2)}) collective-permute-start(f32[128,128]{1,0:T(8,128)S(1)} %get-tuple-element.442), channel_id=1, source_target_pairs={{0,5},{1,4},{2,7},{3,6},{4,1},{5,0},{6,3},{7,2},{8,13},{9,12},{10,... | collective-permute-start | bytes 196616 | tf_op jit(solution)/shard_map/cond/branch_1_fun/ppermute | solution.py:331
  40.1 5.5 %collective-permute-start.8 = (f32[128,128]{1,0:T(8,128)S(1)}, f32[128,128]{1,0:T(8,128)S(1)}, u32[]{:S(2)}, u32[]{:S(2)}) collective-permute-start(f32[128,128]{1,0:T(8,128)S(1)} %get-tuple-element.443), channel_id=1, source_target_pairs={{0,6},{1,7},{2,4},{3,5},{4,2},{5,3},{6,0},{7,1},{8,14},{9,15},{10,... | collective-permute-start | bytes 196616 | tf_op jit(solution)/shard_map/cond/branch_1_fun/ppermute | solution.py:331
  41.9 4.9 %collective-permute-start.9 = (f32[128,128]{1,0:T(8,128)S(1)}, f32[128,128]{1,0:T(8,128)S(1)}, u32[]{:S(2)}, u32[]{:S(2)}) collective-permute-start(f32[128,128]{1,0:T(8,128)S(1)} %get-tuple-element.444), channel_id=1, source_target_pairs={{0,7},{1,6},{2,5},{3,4},{4,3},{5,2},{6,1},{7,0},{8,15},{9,14},{10,... | collective-permute-start | bytes 196616 | tf_op jit(solution)/shard_map/cond/branch_1_fun/ppermute | solution.py:331
  50.8 0.8 %copy-start.1 = (f32[1,1,8,128,128]{4,3,2,1,0:T(8,128)}, f32[1,1,8,128,128]{4,3,2,1,0:T(8,128)S(1)}, u32[]{:S(2)}) copy-start(f32[1,1,8,128,128]{4,3,2,1,0:T(8,128)S(1)} %get-tuple-element.754) | copy-start | bytes 1572868

commit v4 on v3

v4 whole, which is shorter than its diff:
```python
import jax
import jax.numpy as jnp
from jax import lax
from jax.experimental import pallas as pl
from jax.experimental.pallas import tpu as pltpu
from jax.sharding import PartitionSpec as P

NBLK = 512
ACT = 2
SECTIONS = 4
BS = 128
SLOTS = 8
LCAP = 5
RCAP = 5
ZCAP = 6
VMEM_LIMIT = 32 * 1024 * 1024


def from_root(x, axis, root):
    mine = lax.axis_index(axis) == root
    return lax.psum(jnp.where(mine, x, jnp.zeros_like(x)), axis)


def from_partner(x, axis, bit):
    return lax.ppermute(x, axis, [(i, i ^ 1 << bit) for i in range(lax.axis_size(axis))])


def shifted(value, axis, steps):
    count = lax.axis_size(axis)
    pairs = [(source, (source + steps) % count) for source in range(count)]
    return lax.ppermute(value, axis, pairs)


def section_product(panel, pair, out_rows, out_cols, depth):
    panel_vals, panel_rows, panel_cols = panel
    pair_vals, pair_inner, pair_cols = pair
    panel_iota = jnp.arange(panel_rows.shape[0], dtype=jnp.int32)
    pair_iota = jnp.arange(pair_inner.shape[0], dtype=jnp.int32)
    depth_iota = jnp.arange(depth, dtype=jnp.int32)
    panel_live = panel_rows >= 0
    earlier = (
        (panel_rows[None, :] == panel_rows[:, None])
        & panel_live[None, :]
        & (panel_iota[None, :] < panel_iota[:, None])
    )
    within = jnp.sum(earlier.astype(jnp.int32), axis=1)
    picked = (panel_rows[None, None, :] == out_rows[:, None, None]) & (
        within[None, None, :] == depth_iota[None, :, None]
    )
    picked = picked & panel_live[None, None, :] & (out_rows >= 0)[:, None, None]
    picked_int = picked.astype(jnp.int32)
    panel_slot = jnp.sum(picked_int * panel_iota[None, None, :], axis=2)
    found = jnp.sum(picked_int, axis=2) > 0
    inner = jnp.sum(picked_int * panel_cols[None, None, :], axis=2)
    matched = (pair_inner[None, None, :] == inner[:, :, None]) & (
        pair_cols[None, None, :] == out_cols[:, None, None]
    )
    matched = matched & (pair_inner >= 0)[None, None, :] & found[:, :, None]
    matched_int = matched.astype(jnp.int32)
    pair_slot = jnp.sum(matched_int * pair_iota[None, None, :], axis=2)
    weight = (jnp.sum(matched_int, axis=2) > 0).astype(jnp.float32)
    left = panel_vals[panel_slot] * weight[:, :, None, None]
    right = pair_vals[pair_slot]
    return jnp.einsum(
        "tqij,tqjk->tik",
        left,
        right,
        precision=lax.Precision.HIGHEST,
        preferred_element_type=jnp.float32,
    )


def make_pair(first, second, row_span):
    inner = jnp.concatenate([first[1], jnp.where(second[1] >= 0, second[1] + row_span, -1)])
    return (jnp.concatenate([first[0], second[0]]), inner, jnp.concatenate([first[2], second[2]]))


def order_pair(mine, other, is_even, row_span):
    first = tuple((jnp.where(is_even, one, two) for one, two in zip(mine, other)))
    second = tuple((jnp.where(is_even, two, one) for one, two in zip(mine, other)))
    return make_pair(first, second, row_span)


def fetch_panel(tile, row_index, col_count, section):
    root = (row_index // 2 + section) % col_count
    return tuple(from_root(one, "col", root) for one in tile)


def general_body(blocks, block_rows, block_cols):
    tile = (blocks[0, 0], block_rows[0, 0], block_cols[0, 0])
    row_count = lax.axis_size("row")
    col_count = lax.axis_size("col")
    row_span = NBLK // row_count
    row_index = lax.axis_index("row")
    is_even = row_index % 2 == 0
    depth = 2 * ACT
    total = jnp.zeros(blocks.shape[2:], jnp.float32)
    partner = from_partner((tile[0], tile[1], tile[2]), "row", 0)
    current = order_pair(tile, partner, is_even, row_span)
    for section in range(SECTIONS):
        panel = fetch_panel(tile, row_index, col_count, section)
        if section > 0:
            current = shifted((current[0], current[1], current[2]), "row", -2)
        total = total + section_product(panel, current, tile[1], tile[2], depth)
    return total[None, None]


def everything(x, axis):
    return lax.all_to_all(jnp.broadcast_to(x[None], (lax.axis_size(axis),) + x.shape), axis, 0, 0)


def whole_tiles(blocks, block_rows, block_cols):
    tile = (blocks[0, 0], block_rows[0, 0], block_cols[0, 0])
    row_span = NBLK // lax.axis_size(("z", "y"))
    col_count = lax.axis_size("col")
    row_index = lax.axis_index(("z", "y"))
    panels = tuple(everything(one, "col") for one in tile)
    column = tuple(everything(one, ("z", "y")) for one in tile)

    def section(step, total):
        root = (row_index // 2 + step) % col_count
        take = lambda arrays, at: tuple(lax.dynamic_index_in_dim(a, at, 0, False) for a in arrays)
        pair = make_pair(take(column, 2 * root), take(column, 2 * root + 1), row_span)
        return total + section_product(take(panels, root), pair, tile[1], tile[2], 2 * ACT)

    total = lax.fori_loop(0, SECTIONS, section, jnp.zeros(blocks.shape[2:], jnp.float32))
    return total[None, None]


GROUP = (0, 4)


def piece_of(p):
    return p // 4


def group_of(p):
    return p % 4


def bf(x):
    return x.astype(jnp.bfloat16)


def ind(x):
    return bf(jnp.where(x, 1.0, 0.0))


def mm(a, b, transposed=False):
    dims = (((1,), (1 if transposed else 0,)), ((), ()))
    return lax.dot_general(a, b, dims, preferred_element_type=jnp.float32)


def plan_kernel(rows, cols, idx_ref, table_ref, list_ref, over_ref):
    devices = rows * cols
    plane = 2 * cols
    n = devices * SLOTS
    in_plane = plane * SLOTS
    rb = NBLK // rows
    cb = NBLK // cols
    per_row = cols * SLOTS
    lefts = (cols - 1) * LCAP
    my_plane, my_p = lax.axis_index("z"), lax.axis_index(("y", "col"))
    my_row = 2 * my_plane + lax.axis_index("y")
    my_col = lax.axis_index("col")
    me = my_row * cols + my_col

    sub = lax.broadcasted_iota(jnp.int32, (n, 1), 0)
    lane = lax.broadcasted_iota(jnp.int32, (1, n), 1)
    dev = lax.broadcasted_iota(jnp.int32, (devices, 1), 0)
    dev_r = lax.broadcasted_iota(jnp.int32, (1, devices), 1)
    slot = lax.broadcasted_iota(jnp.int32, (1, 2 * SLOTS), 1)
    diagonal = sub == lane

    def as_row(column):
        return jnp.sum(jnp.where(diagonal, column, 0.0), axis=0, keepdims=True)

    def as_column(row):
        return jnp.sum(jnp.where(diagonal, row, 0.0), axis=1, keepdims=True)

    values = mm(ind((sub // SLOTS) == dev_r), bf(idx_ref[...].astype(jnp.float32)))

    def column(k):
        return jnp.sum(jnp.where((sub % SLOTS) == slot - k * SLOTS, values, 0.0), axis=1, keepdims=True)

    up = ((sub // per_row) * rb).astype(jnp.float32)
    along = (((sub // SLOTS) % cols) * cb).astype(jnp.float32)
    row_c, col_c = column(0), column(1)
    row_c = jnp.where(row_c >= 0, row_c + up, -1.0)
    col_c = jnp.where(col_c >= 0, col_c + along, -2.0)
    row_r, col_r = as_row(row_c), as_row(col_c)

    slot_r = (lane % SLOTS).astype(jnp.float32)
    hit = mm(bf(jnp.where(col_c == col_r, 1.0 + 16.0 * slot_r, 0.0)), ind(row_c == row_r))
    product = (row_c == col_r) & (hit > 0)
    product_b = ind(product)

    in_row = (lane // per_row) == (dev // cols)
    in_col = ((lane // SLOTS) % cols) == (dev % cols)
    other = (lane // SLOTS) != dev
    left = in_row & other & (mm(ind(in_col), product_b) > 0)
    right = in_col & other & (mm(ind(in_row), product_b, transposed=True) > 0)
    before = sub < lane
    same_device = (sub // SLOTS) == (lane // SLOTS)
    left_at = jnp.where(left, mm(ind(left), ind(before & same_device)), -1.0)
    right_at = jnp.where(right, mm(ind(right), ind(before)), -1.0)

    zed = lax.broadcasted_iota(jnp.int32, (8, 1), 0)
    cross = (mm(ind((dev_r // plane) == zed), ind(right)) > 0) & ((lane // in_plane) != zed)
    together = ((sub // in_plane) == (lane // in_plane)) & (
        group_of((sub // SLOTS) % plane) == group_of((lane // SLOTS) % plane)
    )
    cross_at = jnp.where(cross, mm(ind(cross), ind(before & together)), -1.0)

    over = jnp.maximum(jnp.max(left_at) - (LCAP - 1), jnp.max(right_at) - (RCAP - 1))
    over_ref[0, 0] = jnp.maximum(over, jnp.max(cross_at) - (ZCAP - 1)).astype(jnp.int32)

    lanes = lax.broadcasted_iota(jnp.int32, (1, BS), 1)

    def table(first, at, value, most):
        out = jnp.zeros((8, BS), jnp.float32)
        for k in range(most):
            one = jnp.sum(jnp.where(at == k, value, 0.0), axis=1, keepdims=True)
            out = jnp.where(lanes == k, one, out)
        table_ref[first : first + 8, :] = out.astype(jnp.int32)

    mine = (lane // SLOTS) == me
    to_col = mm(ind(my_row * cols + zed % cols == dev_r), bf(left_at))
    table(0, jnp.where(mine, to_col, -1.0), slot_r, LCAP)
    here = ((lane // in_plane) == my_plane) & (group_of((lane // SLOTS) % plane) == group_of(my_p))
    partner = piece_of((lane // SLOTS) % plane) ^ piece_of(my_p)
    local = (partner * SLOTS + lane % SLOTS).astype(jnp.float32)
    table(8, jnp.where(here, cross_at, -1.0), local, ZCAP)
    came = jnp.sum(jnp.where(zed == my_plane, cross_at, 0.0), axis=0, keepdims=True)
    away = len(GROUP) * SLOTS + ZCAP * (((lane // in_plane) ^ my_plane) - 1)
    source = jnp.where((lane // in_plane) == my_plane, local, away.astype(jnp.float32) + came)
    partners = jnp.zeros((8, devices), jnp.bool_)
    for g, mask in enumerate(GROUP):
        partners = partners | ((zed == g) & (dev_r == my_plane * plane + (my_p ^ mask)))
    table(16, mm(ind(partners), bf(right_at)), source, RCAP)

    left_me = jnp.sum(jnp.where(dev == me, left_at, 0.0), axis=0, keepdims=True)
    right_me = jnp.sum(jnp.where(dev == me, right_at, 0.0), axis=0, keepdims=True)
    from_col = ((lane // SLOTS) % cols) ^ my_col
    held_a = jnp.where(mine, slot_r, (SLOTS + LCAP * (from_col - 1)).astype(jnp.float32) + left_me)
    held_b = as_column(jnp.where(mine, slot_r, SLOTS + lefts + right_me))
    my_product = product & (((sub // SLOTS) % cols) == my_col) & ((lane // per_row) == my_row)
    rank = mm(ind(lane < sub), ind(my_product))
    code = (hit - 1.0) * 64.0 + held_a * 32.0 + held_b + 1.0
    out_sub = lax.broadcasted_iota(jnp.int32, (list_ref.shape[0], 1), 0)
    listed = jnp.zeros(list_ref.shape, jnp.float32)
    for k in range(2 * ACT):
        one = jnp.sum(jnp.where(my_product & (rank == k), code, 0.0), axis=0, keepdims=True)
        listed = jnp.where(out_sub == k, one, listed)
    list_ref[...] = listed.astype(jnp.int32) - 1


def spread_kernel(piece, blocks_ref, *outs):
    mine = piece_of(lax.axis_index(("y", "col")))
    for g, out_ref in enumerate(outs):
        for t in range(SLOTS):
            at = pl.ds(pl.multiple_of(t * BS + (mine ^ (g + 1)) * piece, piece), piece)
            out_ref[t * piece : (t + 1) * piece, :] = blocks_ref[at, :]


def cross_kernel(planes, cols, piece, table_ref, blocks_ref, *refs):
    partners = len(GROUP) - 1
    piece_refs, left_refs = refs[:partners], refs[partners : partners + cols - 1]
    cross_refs, held_ref = refs[partners + cols - 1 : -1], refs[-1]
    mine = piece_of(lax.axis_index(("y", "col")))
    for t in range(SLOTS):
        at = pl.ds(pl.multiple_of(t * BS + mine * piece, piece), piece)
        held_ref[t * piece : (t + 1) * piece, :] = blocks_ref[at, :]
    size = SLOTS * piece
    for g, ref in enumerate(piece_refs):
        held_ref[(g + 1) * size : (g + 2) * size, :] = ref[...]
    for m, out_ref in enumerate(cross_refs):
        z = lax.axis_index("z") ^ (m + 1)
        for k in range(ZCAP):
            at = pl.ds(pl.multiple_of(table_ref[8 + z, k] * piece, piece), piece)
            out_ref[k * piece : (k + 1) * piece, :] = held_ref[at, :]
    for m, out_ref in enumerate(left_refs):
        col = lax.axis_index("col") ^ (m + 1)
        for k in range(LCAP):
            at = pl.ds(pl.multiple_of(table_ref[col, k] * BS, BS), BS)
            out_ref[k * BS : (k + 1) * BS, :] = blocks_ref[at, :]


def give_kernel(planes, piece, table_ref, held_ref, *refs):
    crossed_refs, outs, all_ref = refs[: planes - 1], refs[planes - 1 : -1], refs[-1]
    here = held_ref.shape[0]
    size = ZCAP * piece
    all_ref[:here, :] = held_ref[...]
    for m, ref in enumerate(crossed_refs):
        all_ref[here + m * size : here + (m + 1) * size, :] = ref[...]
    for g, out_ref in enumerate(outs):
        for k in range(RCAP):
            at = pl.ds(pl.multiple_of(table_ref[16 + g, k] * piece, piece), piece)
            out_ref[k * piece : (k + 1) * piece, :] = all_ref[at, :]


def add_products(per_row, list_ref, held_ref, out_ref, wanted):
    first = (2 * lax.axis_index("z") + lax.axis_index("y")) * per_row

    def block(at):
        x = held_ref[pl.ds(pl.multiple_of(at * BS, BS), BS), :]
        high = bf(x)
        return high, bf(x - high.astype(jnp.float32))

    def entry(i, carry):
        for k in range(2 * ACT):
            code = list_ref[k, first + i]
            a, b = (code // 32) % 32, code % 32

            @pl.when((code >= 0) & wanted(a, b))
            def _():
                a_high, a_low = block(a)
                b_high, b_low = block(b)
                at = pl.ds(pl.multiple_of((code // 1024) * BS, BS), BS)
                out_ref[at, :] += mm(a_high, b_high) + (mm(a_high, b_low) + mm(a_low, b_high))

        return carry

    lax.fori_loop(0, per_row, entry, 0)


def own_kernel(per_row, list_ref, blocks_ref, out_ref):
    out_ref[...] = jnp.zeros_like(out_ref)
    add_products(per_row, list_ref, blocks_ref, out_ref, lambda a, b: (a < SLOTS) & (b < SLOTS))


def product_kernel(cols, piece, list_ref, blocks_ref, start_ref, *refs):
    lefts, group = cols - 1, len(GROUP)
    left_refs, right_refs = refs[:lefts], refs[lefts : lefts + group]
    out_ref, held_ref = refs[lefts + group :]
    mine = piece_of(lax.axis_index(("y", "col")))
    out_ref[...] = start_ref[...]
    held_ref[: SLOTS * BS, :] = blocks_ref[...]
    at = SLOTS * BS
    for ref in left_refs:
        held_ref[at : at + LCAP * BS, :] = ref[...]
        at += LCAP * BS
    for g, ref in enumerate(right_refs):
        for k in range(RCAP):
            to = pl.ds(pl.multiple_of(at + k * BS + (mine ^ g) * piece, piece), piece)
            held_ref[to, :] = ref[k * piece : (k + 1) * piece, :]
    add_products(cols * SLOTS, list_ref, held_ref, out_ref, lambda a, b: (a >= SLOTS) | (b >= SLOTS))


def swapped(x, axis, mask):
    return lax.ppermute(x, axis, [(i, i ^ mask) for i in range(lax.axis_size(axis))])


def packed_body(blocks, block_rows, block_cols):
    planes, cols = lax.axis_size("z"), lax.axis_size("col")
    rows = 2 * planes
    plane = 2 * cols
    devices = rows * cols
    n = devices * SLOTS
    group = len(GROUP)
    piece = BS // group
    in_plane = ("y", "col")
    flat = blocks.reshape(SLOTS * BS, BS)
    params = pltpu.CompilerParams(vmem_limit_bytes=VMEM_LIMIT)
    vmem = pl.BlockSpec(memory_space=pltpu.VMEM)
    smem = pl.BlockSpec(memory_space=pltpu.SMEM)

    def floats(height):
        return jax.ShapeDtypeStruct((height, BS), jnp.float32)

    def ints(*shape):
        return jax.ShapeDtypeStruct(shape, jnp.int32)

    def call(kernel, name, ins, outs, scratch=(), specs=None):
        return pl.pallas_call(
            kernel,
            out_shape=outs,
            in_specs=ins,
            out_specs=[vmem] * len(outs) if specs is None else specs,
            scratch_shapes=scratch,
            compiler_params=params,
            name=name,
        )

    spread = call(
        lambda *refs: spread_kernel(piece, *refs), "spread", [vmem], [floats(SLOTS * piece)] * (group - 1)
    )(flat)
    pieces = [swapped(x, in_plane, mask) for x, mask in zip(spread, GROUP[1:])]
    me = lax.axis_index(("z", "y", "col"))
    idx = jnp.concatenate([block_rows[0], block_cols[0]], axis=1)
    idx = lax.psum(jnp.where(jnp.arange(devices)[:, None] == me, idx, 0), ("z", "y", "col"))
    table, listed, over = call(
        lambda *refs: plan_kernel(rows, cols, *refs),
        "plan",
        [vmem],
        [ints(24, BS), ints(8, n), ints(1, 1)],
        specs=[vmem, vmem, smem],
    )(idx)

    def packed():
        *outgoing, held = call(
            lambda *refs: cross_kernel(planes, cols, piece, *refs),
            "cross",
            [smem] + [vmem] * group,
            [floats(LCAP * BS)] * (cols - 1) + [floats(ZCAP * piece)] * (planes - 1) + [floats(group * SLOTS * piece)],
        )(table, flat, *pieces)
        crossed = [swapped(x, "z", m + 1) for m, x in enumerate(outgoing[cols - 1 :])]
        lefts = [swapped(x, "col", m + 1) for m, x in enumerate(outgoing[: cols - 1])]
        own = call(
            lambda *refs: own_kernel(cols * SLOTS, *refs), "own", [smem, vmem], [floats(SLOTS * BS)]
        )(listed, flat)
        giving = call(
            lambda *refs: give_kernel(planes, piece, *refs),
            "give",
            [smem] + [vmem] * planes,
            [floats(RCAP * piece)] * group,
            [pltpu.VMEM(((group * SLOTS + (planes - 1) * ZCAP) * piece, BS), jnp.float32)],
        )(table, held, *crossed)
        rights = [swapped(x, in_plane, mask) if mask else x for x, mask in zip(giving, GROUP)]
        out = call(
            lambda *refs: product_kernel(cols, piece, *refs),
            "products",
            [smem] + [vmem] * (2 + cols - 1 + group),
            [floats(SLOTS * BS)],
            [pltpu.VMEM(((SLOTS + (cols - 1) * LCAP + RCAP) * BS, BS), jnp.float32)],
        )(listed, flat, *own, *lefts, *rights)
        return out[0].reshape(blocks.shape)

    return lax.cond(over[0, 0] <= 0, packed, lambda: whole_tiles(blocks, block_rows, block_cols))


def solution(mesh):
    rows, cols = mesh.devices.shape
    if cols == SECTIONS and rows == 2 * SECTIONS:
        body, row = packed_body, ("z", "y")
        mesh = jax.sharding.Mesh(mesh.devices.reshape(rows // 2, 2, cols), ("z", "y", "col"))
    else:
        body, row = general_body, "row"
    return jax.shard_map(
        body,
        mesh=mesh,
        in_specs=(P(row, "col", None, None, None), P(row, "col", None), P(row, "col", None)),
        out_specs=P(row, "col", None, None, None),
        check_vma=False,
    )
```

time: 51.8 us -> 79.8 us (1.54)
  blocking collectives: 0 us -> 40.2 us
  starting transfers between devices: 22.7 us -> 12.1 us
  waiting for transfers between devices: 18.5 us -> 11.2 us
  Pallas kernels: 8.16 us -> 13.5 us
    psum x0 -> x1, blocking collectives: none -> 40.2 us  [packed_body(): lax.psum(jnp.where(jnp.arange(devices)[:, None] == me, idx, 0), ('z', 'y'...]
    ppermute x20 -> x8, starting transfers between devices: 22.7 us -> 12.1 us  [swapped(): lax.ppermute(x, axis, [(i, i ^ mask) for i in range(lax.axis_size(axis))])]
    ppermute x20 -> x8, waiting for transfers between devices: 18.5 us -> 11.2 us  [swapped(): lax.ppermute(x, axis, [(i, i ^ mask) for i in range(lax.axis_size(axis))])]
    pallas_call x5 -> x6, Pallas kernels: 8.16 us -> 13.5 us  [the longest x1 4.98 us: packed(): call(lambda *refs: own_kernel(cols * SLOTS, *refs), 'own', [smem, vmem],...]
  transfers between devices with their start and end apart: 20 -> 8, of which waited for: 10 -> 2; matrix products, arithmetic and copies ran while one was open for 0% -> 1% of each run, Pallas kernels for 0% -> 9%
where the time goes in v4:
time: 79.8 us; the launch traced here: 79.4 us
  blocking collectives  40.2 us (50%)
  Pallas kernels  13.5 us (17%)
  starting transfers between devices  12.1 us (15%)
  waiting for transfers between devices  11.2 us (14%)
  other arithmetic  0.82 us (1%)
    psum x1, blocking collectives, packed_body(): lax.psum(jnp.where(jnp.arange(devices)[:, None] == me, idx, 0), ('z', 'y'...  40.2 us
    ppermute x8, starting transfers between devices, swapped(): lax.ppermute(x, axis, [(i, i ^ mask) for i in range(lax.axis_size(axis))])  12.1 us
    ppermute x8, waiting for transfers between devices, swapped(): lax.ppermute(x, axis, [(i, i ^ mask) for i in range(lax.axis_size(axis))])  11.2 us
    pallas_call x1, Pallas kernels, packed(): call(lambda *refs: own_kernel(cols * SLOTS, *refs), 'own', [smem, vmem],...  4.98 us
    pallas_call x1, Pallas kernels, packed(): call(lambda *refs: product_kernel(cols, piece, *refs), 'products', [smem]...  3.72 us
    pallas_call x1, Pallas kernels, packed_body(): call(lambda *refs: plan_kernel(rows, cols, *refs), 'plan', [vmem], [ints(...  1.64 us
  transfers between devices with their start and end apart: 8, of which 2 were waited for; matrix products, arithmetic and copies ran while one was open for 1% of the time, Pallas kernels for 9%

profile of v4, /device:TPU:0, one launch (start us, length us, event | category | flops | bytes accessed | tf_op | source)
XLA Modules:
  0.0 79.4 jit_solution(4178477228389184594)
XLA Ops:
  0.0 1.1 %spread.1 = f32[512,128]{1,0:T(8,128)S(1)} custom-call(f32[1024,128]{1,0:T(8,128)} %bitcast.80), custom_call_target="tpu_custom_call" | custom-call | tf_op jit(solution)/shard_map/spread/pallas_call | solution.py:385
  1.1 3.0 %collective-permute-start.7 = (f32[512,128]{1,0:T(8,128)S(1)}, f32[512,128]{1,0:T(8,128)S(1)}, u32[]{:S(2)}, u32[]{:S(2)}) collective-permute-start(f32[512,128]{1,0:T(8,128)S(1)} %spread.1), channel_id=1, source_target_pairs={{0,4},{1,5},{2,6},{3,7},{4,0},{5,1},{6,2},{7,3},{8,12},{9,13},{10,... | collective-permute-start | bytes 786440 | tf_op jit(solution)/shard_map/ppermute | solution.py:351
  4.1 0.7 add_bitcast_fusion
  4.8 0.1 broadcast_select_fusion
  4.9 40.2 %psum.7.refs_0_ = s32[32,16]{1,0:T(8,128)S(1)} all-reduce(s32[32,16]{1,0:T(8,128)S(1)} %broadcast_select_fusion), channel_id=1, replica_groups=mesh['z'=4,'y'=2,'col'=4] {'z','y','col'}, use_global_device_ids=true, to_apply=%region_0.1 | all-reduce | flops 512 | bytes 4096 | tf_op jit(solution)/shard_map/psum | solution.py:391
  45.1 1.6 %plan.1 = (s32[24,128]{1,0:T(8,128)S(1)}, s32[8,256]{1,0:T(8,128)S(1)}, s32[1,1]{1,0:T(1,128)}) custom-call(s32[32,16]{1,0:T(8,128)S(1)} %psum.7.refs_0_), custom_call_target="tpu_custom_call" | custom-call | tf_op jit(solution)/shard_map/plan/pallas_call | solution.py:392
  47.4 31.2 %conditional.1 = (f32[1,1,8,128,128]{4,3,2,1,0:T(8,128)S(1)}) conditional(s32[]{:T(128)} %bitcast.12, (f32[1,1,8,128,128]{4,3,2,1,0:T(8,128)}, s32[1,1,8]{2,1,0:T(1,128)}, s32[1,1,8]{2,1,0:T(1,128)}) %tuple.36, (s32[8,256]{1,0:T(8,128)S(1)}, f32[1024,128]{1,0:T(8,128)}, s32[24,128]{1,0:T(8,128)S(1)}, f32[512,128]{1,0:T(8,128)S(1)}) %tuple.82), branch_computations={%region_1.10_spmd, %region_10.11_spmd} | conditional | flops 806364224 | bytes 53494504 | solution.py:429
  47.4 0.0 copy-start.2
  47.4 1.3 %cross.1 = (f32[640,128]{1,0:T(8,128)S(1)}, f32[640,128]{1,0:T(8,128)S(1)}, f32[640,128]{1,0:T(8,128)S(1)}, f32[384,128]{1,0:T(8,128)S(1)}, f32[384,128]{1,0:T(8...) custom-call(s32[24,128]{1,0:T(8,128)S(1)} %get-tuple-element.407.refs_0_, ...), custom_call_target="tpu_custom_call" | custom-call | tf_op jit(solution)/shard_map/cond/branch_1_fun/cross/pallas_call | solution.py:401
  48.7 1.0 %collective-permute-start.3 = (f32[384,128]{1,0:T(8,128)S(1)}, f32[384,128]{1,0:T(8,128)S(1)}, u32[]{:S(2)}, u32[]{:S(2)}) collective-permute-start(f32[384,128]{1,0:T(8,128)S(1)} %get-tuple-element.413), channel_id=1, source_target_pairs={{0,8},{8,0},{16,24},{24,16},{1,9},{9,1},{17,25},{25,17},{2,10},{10... | collective-permute-start | bytes 589832 | tf_op jit(solution)/shard_map/cond/branch_1_fun/ppermute | solution.py:351
  49.7 1.3 %collective-permute-start.4 = (f32[384,128]{1,0:T(8,128)S(1)}, f32[384,128]{1,0:T(8,128)S(1)}, u32[]{:S(2)}, u32[]{:S(2)}) collective-permute-start(f32[384,128]{1,0:T(8,128)S(1)} %get-tuple-element.414), channel_id=1, source_target_pairs={{0,16},{8,24},{16,0},{24,8},{1,17},{9,25},{17,1},{25,9},{2,18},{10... | collective-permute-start | bytes 589832 | tf_op jit(solution)/shard_map/cond/branch_1_fun/ppermute | solution.py:351
  50.9 2.2 %collective-permute-start.5 = (f32[384,128]{1,0:T(8,128)S(1)}, f32[384,128]{1,0:T(8,128)S(1)}, u32[]{:S(2)}, u32[]{:S(2)}) collective-permute-start(f32[384,128]{1,0:T(8,128)S(1)} %get-tuple-element.415), channel_id=1, source_target_pairs={{0,24},{8,16},{16,8},{24,0},{1,25},{9,17},{17,9},{25,1},{2,26},{10... | collective-permute-start | bytes 589832 | tf_op jit(solution)/shard_map/cond/branch_1_fun/ppermute | solution.py:351
  53.2 2.3 %collective-permute-start.1 = (f32[640,128]{1,0:T(8,128)S(1)}, f32[640,128]{1,0:T(8,128)S(1)}, u32[]{:S(2)}, u32[]{:S(2)}) collective-permute-start(f32[640,128]{1,0:T(8,128)S(1)} %get-tuple-element.410), channel_id=1, source_target_pairs={{0,2},{1,3},{2,0},{3,1},{4,6},{5,7},{6,4},{7,5},{8,10},{9,11},{10,... | collective-permute-start | bytes 983048 | tf_op jit(solution)/shard_map/cond/branch_1_fun/ppermute | solution.py:351
  55.4 2.1 %collective-permute-done.3.refs_2_ = f32[384,128]{1,0:T(8,128)S(1)} collective-permute-done((f32[384,128]{1,0:T(8,128)S(1)}, f32[384,128]{1,0:T(8,128)S(1)}, u32[]{:S(2)}, u32[]{:S(2)}) %collective-permute-start.3) | collective-permute-done | bytes 196640 | tf_op jit(solution)/shard_map/cond/branch_1_fun/ppermute | solution.py:351
  57.5 0.0 collective-permute-start.2
  57.5 9.1 %collective-permute-done.4.refs_3_ = f32[384,128]{1,0:T(8,128)S(1)} collective-permute-done((f32[384,128]{1,0:T(8,128)S(1)}, f32[384,128]{1,0:T(8,128)S(1)}, u32[]{:S(2)}, u32[]{:S(2)}) %collective-permute-start.4) | collective-permute-done | bytes 196640 | tf_op jit(solution)/shard_map/cond/branch_1_fun/ppermute | solution.py:351
  66.7 0.0 collective-permute-done.5.refs_4_
  66.7 0.8 %give.1 = (f32[320,128]{1,0:T(8,128)S(1)}, f32[320,128]{1,0:T(8,128)S(1)}) custom-call(s32[24,128]{1,0:T(8,128)S(1)} %get-tuple-element.407.refs_0_, f32[1024,128]{1,0:T(8,128)S(1)} %get-tuple-element.412.refs_1_, f32[384,128]{1,0:T(8,128)S(1)} %collective-permute-done.3.refs_2_, f32[384,128]{1,0:T(8,128)S(1)} %collective-permute-done.4.refs_3_, ...), custom_call_target="tpu_custom_call" | custom-call | tf_op jit(solution)/shard_map/cond/branch_1_fun/give/pallas_call | solution.py:412
  67.5 2.4 %collective-permute-start.6 = (f32[320,128]{1,0:T(8,128)S(1)}, f32[320,128]{1,0:T(8,128)S(1)}, u32[]{:S(2)}, u32[]{:S(2)}) collective-permute-start(f32[320,128]{1,0:T(8,128)S(1)} %get-tuple-element.417), channel_id=1, source_target_pairs={{0,4},{1,5},{2,6},{3,7},{4,0},{5,1},{6,2},{7,3},{8,12},{9,13},{10,... | collective-permute-start | bytes 491528 | tf_op jit(solution)/shard_map/cond/branch_1_fun/ppermute | solution.py:351
  69.9 5.0 %own.1.refs_2_ = f32[1024,128]{1,0:T(8,128)S(1)} custom-call(s32[8,256]{1,0:T(8,128)S(1)} %get-tuple-element.405.refs_0_, f32[1024,128]{1,0:T(8,128)S(1)} %copy-done.2), custom_call_target="tpu_custom_call" | custom-call | tf_op jit(solution)/shard_map/cond/branch_1_fun/own/pallas_call | solution.py:409
  74.9 0.0 collective-permute-done.1.refs_4_
  74.9 3.7 %products.1 = f32[1024,128]{1,0:T(8,128)S(1)} custom-call(s32[8,256]{1,0:T(8,128)S(1)} %get-tuple-element.405.refs_0_, f32[1024,128]{1,0:T(8,128)S(1)} %copy-done.2, f32[1024,128]{1,0:T(8,128)S(1)} %own.1.refs_2_, f32[640,128]{1,0:T(8,128)S(1)} %collective-permute-done.refs_3_, f32[640,128]{1,0:T(8,128)S(1)} %collective-permute-done.1.refs_4_, ...), custom_call_target="tpu_custom_call" | custom-call | tf_op jit(solution)/shard_map/cond/branch_1_fun/products/pallas_call | solution.py:420
  78.6 0.0 copy-start.3
  78.7 0.8 copy-done.3
  (7 shorter events, 0.0 us)
Async XLA Ops:
  1.1 46.3 %collective-permute-start.7 = (f32[512,128]{1,0:T(8,128)S(1)}, f32[512,128]{1,0:T(8,128)S(1)}, u32[]{:S(2)}, u32[]{:S(2)}) collective-permute-start(f32[512,128]{1,0:T(8,128)S(1)} %spread.1), channel_id=1, source_target_pairs={{0,4},{1,5},{2,6},{3,7},{4,0},{5,1},{6,2},{7,3},{8,12},{9,13},{10,... | collective-permute-start | bytes 786440 | tf_op jit(solution)/shard_map/ppermute | solution.py:351
  47.4 22.4 %copy-start.2 = (f32[1024,128]{1,0:T(8,128)S(1)}, f32[1024,128]{1,0:T(8,128)}, u32[]{:S(2)}) copy-start(f32[1024,128]{1,0:T(8,128)} %get-tuple-element.406.refs_1_) | copy-start | bytes 1572868 | tf_op jit(solution)/shard_map/cond
  48.7 8.8 %collective-permute-start.3 = (f32[384,128]{1,0:T(8,128)S(1)}, f32[384,128]{1,0:T(8,128)S(1)}, u32[]{:S(2)}, u32[]{:S(2)}) collective-permute-start(f32[384,128]{1,0:T(8,128)S(1)} %get-tuple-element.413), channel_id=1, source_target_pairs={{0,8},{8,0},{16,24},{24,16},{1,9},{9,1},{17,25},{25,17},{2,10},{10... | collective-permute-start | bytes 589832 | tf_op jit(solution)/shard_map/cond/branch_1_fun/ppermute | solution.py:351
  49.7 17.0 %collective-permute-start.4 = (f32[384,128]{1,0:T(8,128)S(1)}, f32[384,128]{1,0:T(8,128)S(1)}, u32[]{:S(2)}, u32[]{:S(2)}) collective-permute-start(f32[384,128]{1,0:T(8,128)S(1)} %get-tuple-element.414), channel_id=1, source_target_pairs={{0,16},{8,24},{16,0},{24,8},{1,17},{9,25},{17,1},{25,9},{2,18},{10... | collective-permute-start | bytes 589832 | tf_op jit(solution)/shard_map/cond/branch_1_fun/ppermute | solution.py:351
  50.9 15.7 %collective-permute-start.5 = (f32[384,128]{1,0:T(8,128)S(1)}, f32[384,128]{1,0:T(8,128)S(1)}, u32[]{:S(2)}, u32[]{:S(2)}) collective-permute-start(f32[384,128]{1,0:T(8,128)S(1)} %get-tuple-element.415), channel_id=1, source_target_pairs={{0,24},{8,16},{16,8},{24,0},{1,25},{9,17},{17,9},{25,1},{2,26},{10... | collective-permute-start | bytes 589832 | tf_op jit(solution)/shard_map/cond/branch_1_fun/ppermute | solution.py:351
  53.2 21.7 %collective-permute-start = (f32[640,128]{1,0:T(8,128)S(1)}, f32[640,128]{1,0:T(8,128)S(1)}, u32[]{:S(2)}, u32[]{:S(2)}) collective-permute-start(f32[640,128]{1,0:T(8,128)S(1)} %get-tuple-element.409), channel_id=1, source_target_pairs={{0,1},{1,0},{2,3},{3,2},{4,5},{5,4},{6,7},{7,6},{8,9},{9,8},{10,11... | collective-permute-start | bytes 983048 | tf_op jit(solution)/shard_map/cond/branch_1_fun/ppermute | solution.py:351
  53.2 21.7 %collective-permute-start.1 = (f32[640,128]{1,0:T(8,128)S(1)}, f32[640,128]{1,0:T(8,128)S(1)}, u32[]{:S(2)}, u32[]{:S(2)}) collective-permute-start(f32[640,128]{1,0:T(8,128)S(1)} %get-tuple-element.410), channel_id=1, source_target_pairs={{0,2},{1,3},{2,0},{3,1},{4,6},{5,7},{6,4},{7,5},{8,10},{9,11},{10,... | collective-permute-start | bytes 983048 | tf_op jit(solution)/shard_map/cond/branch_1_fun/ppermute | solution.py:351
  57.5 17.4 %collective-permute-start.2 = (f32[640,128]{1,0:T(8,128)S(1)}, f32[640,128]{1,0:T(8,128)S(1)}, u32[]{:S(2)}, u32[]{:S(2)}) collective-permute-start(f32[640,128]{1,0:T(8,128)S(1)} %get-tuple-element.411), channel_id=1, source_target_pairs={{0,3},{1,2},{2,1},{3,0},{4,7},{5,6},{6,5},{7,4},{8,11},{9,10},{10,... | collective-permute-start | bytes 983048 | tf_op jit(solution)/shard_map/cond/branch_1_fun/ppermute | solution.py:351
  67.5 7.4 %collective-permute-start.6 = (f32[320,128]{1,0:T(8,128)S(1)}, f32[320,128]{1,0:T(8,128)S(1)}, u32[]{:S(2)}, u32[]{:S(2)}) collective-permute-start(f32[320,128]{1,0:T(8,128)S(1)} %get-tuple-element.417), channel_id=1, source_target_pairs={{0,4},{1,5},{2,6},{3,7},{4,0},{5,1},{6,2},{7,3},{8,12},{9,13},{10,... | collective-permute-start | bytes 491528 | tf_op jit(solution)/shard_map/cond/branch_1_fun/ppermute | solution.py:351
  78.6 0.8 %copy-start.3 = (f32[1,1,8,128,128]{4,3,2,1,0:T(8,128)}, f32[1,1,8,128,128]{4,3,2,1,0:T(8,128)S(1)}, u32[]{:S(2)}) copy-start(f32[1,1,8,128,128]{4,3,2,1,0:T(8,128)S(1)} %get-tuple-element.691) | copy-start | bytes 1572868

commit v5 on v4

--- a/solution.py
+++ b/solution.py
@@ -169,7 +169,7 @@
     lane = lax.broadcasted_iota(jnp.int32, (1, n), 1)
     dev = lax.broadcasted_iota(jnp.int32, (devices, 1), 0)
     dev_r = lax.broadcasted_iota(jnp.int32, (1, devices), 1)
-    slot = lax.broadcasted_iota(jnp.int32, (1, 2 * SLOTS), 1)
+    slot = lax.broadcasted_iota(jnp.int32, (1, SLOTS), 1)
     diagonal = sub == lane
 
     def as_row(column):
@@ -178,10 +178,11 @@
     def as_column(row):
         return jnp.sum(jnp.where(diagonal, row, 0.0), axis=1, keepdims=True)
 
-    values = mm(ind((sub // SLOTS) == dev_r), bf(idx_ref[...].astype(jnp.float32)))
+    repeat = ind((sub // SLOTS) == dev_r)
 
     def column(k):
-        return jnp.sum(jnp.where((sub % SLOTS) == slot - k * SLOTS, values, 0.0), axis=1, keepdims=True)
+        values = mm(repeat, bf(idx_ref[:, k, :].astype(jnp.float32)))
+        return jnp.sum(jnp.where((sub % SLOTS) == slot, values, 0.0), axis=1, keepdims=True)
 
     up = ((sub // per_row) * rb).astype(jnp.float32)
     along = (((sub // SLOTS) % cols) * cb).astype(jnp.float32)
@@ -220,9 +221,9 @@
     def table(first, at, value, most):
         out = jnp.zeros((8, BS), jnp.float32)
         for k in range(most):
-            one = jnp.sum(jnp.where(at == k, value, 0.0), axis=1, keepdims=True)
+            one = jnp.sum(jnp.where(at == k, value + 1.0, 0.0), axis=1, keepdims=True)
             out = jnp.where(lanes == k, one, out)
-        table_ref[first : first + 8, :] = out.astype(jnp.int32)
+        table_ref[first : first + 8, :] = out.astype(jnp.int32) - 1
 
     mine = (lane // SLOTS) == me
     to_col = mm(ind(my_row * cols + zed % cols == dev_r), bf(left_at))
@@ -255,6 +256,16 @@
     list_ref[...] = listed.astype(jnp.int32) - 1
 
 
+def copy_listed(table_ref, row, most, height, from_ref, to_ref):
+    for k in range(most):
+        at = table_ref[row, k]
+
+        @pl.when(at >= 0)
+        def _():
+            here = pl.ds(pl.multiple_of(at * height, height), height)
+            to_ref[k * height : (k + 1) * height, :] = from_ref[here, :]
+
+
 def spread_kernel(piece, blocks_ref, *outs):
     mine = piece_of(lax.axis_index(("y", "col")))
     for g, out_ref in enumerate(outs):
@@ -275,15 +286,9 @@
     for g, ref in enumerate(piece_refs):
         held_ref[(g + 1) * size : (g + 2) * size, :] = ref[...]
     for m, out_ref in enumerate(cross_refs):
-        z = lax.axis_index("z") ^ (m + 1)
-        for k in range(ZCAP):
-            at = pl.ds(pl.multiple_of(table_ref[8 + z, k] * piece, piece), piece)
-            out_ref[k * piece : (k + 1) * piece, :] = held_ref[at, :]
+        copy_listed(table_ref, 8 + (lax.axis_index("z") ^ (m + 1)), ZCAP, piece, held_ref, out_ref)
     for m, out_ref in enumerate(left_refs):
-        col = lax.axis_index("col") ^ (m + 1)
-        for k in range(LCAP):
-            at = pl.ds(pl.multiple_of(table_ref[col, k] * BS, BS), BS)
-            out_ref[k * BS : (k + 1) * BS, :] = blocks_ref[at, :]
+        copy_listed(table_ref, lax.axis_index("col") ^ (m + 1), LCAP, BS, blocks_ref, out_ref)
 
 
 def give_kernel(planes, piece, table_ref, held_ref, *refs):
@@ -294,9 +299,7 @@
     for m, ref in enumerate(crossed_refs):
         all_ref[here + m * size : here + (m + 1) * size, :] = ref[...]
     for g, out_ref in enumerate(outs):
-        for k in range(RCAP):
-            at = pl.ds(pl.multiple_of(table_ref[16 + g, k] * piece, piece), piece)
-            out_ref[k * piece : (k + 1) * piece, :] = all_ref[at, :]
+        copy_listed(table_ref, 16 + g, RCAP, piece, all_ref, out_ref)
 
 
 def add_products(per_row, list_ref, held_ref, out_ref, wanted):
@@ -307,18 +310,27 @@
         high = bf(x)
         return high, bf(x - high.astype(jnp.float32))
 
+    def one(i, k):
+        code = list_ref[k, first + i]
+        a, b = (code // 32) % 32, code % 32
+
+        @pl.when((code >= 0) & wanted(a, b))
+        def _():
+            a_high, a_low = block(a)
+            b_high, b_low = block(b)
+            at = pl.ds(pl.multiple_of((code // 1024) * BS, BS), BS)
+            out_ref[at, :] += mm(
+                jnp.concatenate([a_high, a_high, a_low], axis=1), jnp.concatenate([b_high, b_low, b_high], axis=0)
+            )
+
+        if k + 1 < 2 * ACT:
+
+            @pl.when(code >= 0)
+            def _():
+                one(i, k + 1)
+
     def entry(i, carry):
-        for k in range(2 * ACT):
-            code = list_ref[k, first + i]
-            a, b = (code // 32) % 32, code % 32
-
-            @pl.when((code >= 0) & wanted(a, b))
-            def _():
-                a_high, a_low = block(a)
-                b_high, b_low = block(b)
-                at = pl.ds(pl.multiple_of((code // 1024) * BS, BS), BS)
-                out_ref[at, :] += mm(a_high, b_high) + (mm(a_high, b_low) + mm(a_low, b_high))
-
+        one(i, 0)
         return carry
 
     lax.fori_loop(0, per_row, entry, 0)
@@ -386,9 +398,8 @@
         lambda *refs: spread_kernel(piece, *refs), "spread", [vmem], [floats(SLOTS * piece)] * (group - 1)
     )(flat)
     pieces = [swapped(x, in_plane, mask) for x, mask in zip(spread, GROUP[1:])]
-    me = lax.axis_index(("z", "y", "col"))
-    idx = jnp.concatenate([block_rows[0], block_cols[0]], axis=1)
-    idx = lax.psum(jnp.where(jnp.arange(devices)[:, None] == me, idx, 0), ("z", "y", "col"))
+    idx = jnp.concatenate([block_rows[0], block_cols[0]])
+    idx = lax.all_to_all(jnp.broadcast_to(idx[None], (devices, 2, SLOTS)), ("z", "y", "col"), 0, 0)
     table, listed, over = call(
         lambda *refs: plan_kernel(rows, cols, *refs),
         "plan",
@@ -409,6 +420,7 @@
         own = call(
             lambda *refs: own_kernel(cols * SLOTS, *refs), "own", [smem, vmem], [floats(SLOTS * BS)]
         )(listed, flat)
+        held, *own = lax.optimization_barrier((held, *own))
         giving = call(
             lambda *refs: give_kernel(planes, piece, *refs),
             "give",

time: 79.8 us -> 48.8 us (0.61)
  blocking collectives: 40.2 us -> 0 us
  waiting for transfers between devices: 11.2 us -> 21.3 us
  Pallas kernels: 13.5 us -> 10.6 us
  starting transfers between devices: 12.1 us -> 13.5 us
    psum x1 -> x0, blocking collectives: 40.2 us -> none  [packed_body(): lax.psum(jnp.where(jnp.arange(devices)[:, None] == me, idx, 0), ('z', 'y'...]
    all_to_all x0 -> x1, waiting for transfers between devices: none -> 7.25 us  [packed_body(): lax.all_to_all(jnp.broadcast_to(idx[None], (devices, 2, SLOTS)), ('z', 'y...]
    all_to_all x0 -> x1, starting transfers between devices: none -> 4.89 us  [packed_body(): lax.all_to_all(jnp.broadcast_to(idx[None], (devices, 2, SLOTS)), ('z', 'y...]
    ppermute x8, starting transfers between devices: 12.1 us -> 8.57 us  [swapped(): lax.ppermute(x, axis, [(i, i ^ mask) for i in range(lax.axis_size(axis))])]
    ppermute x8, waiting for transfers between devices: 11.2 us -> 14 us  [swapped(): lax.ppermute(x, axis, [(i, i ^ mask) for i in range(lax.axis_size(axis))])]
    pallas_call x1, Pallas kernels: 3.72 us -> 1.98 us  [packed(): call(lambda *refs: product_kernel(cols, piece, *refs), 'products', [smem]...]
    pallas_call x1, Pallas kernels: 4.98 us -> 3.59 us  [packed(): call(lambda *refs: own_kernel(cols * SLOTS, *refs), 'own', [smem, vmem],...]
  transfers between devices with their start and end apart: 8 -> 9, of which waited for: 2 -> 5; matrix products, arithmetic and copies ran while one was open for 1% -> 3% of each run, Pallas kernels for 9% -> 13%
where the time goes in v5:
time: 48.8 us; the launch traced here: 48.2 us
  waiting for transfers between devices  21.3 us (44%)
  starting transfers between devices  13.5 us (28%)
  Pallas kernels  10.6 us (22%)
  local copies, waits for them, and re-layouts  1.42 us (3%)
  between operations  0.69 us (1%)
  other arithmetic  0.68 us (1%)
    ppermute x8, waiting for transfers between devices, swapped(): lax.ppermute(x, axis, [(i, i ^ mask) for i in range(lax.axis_size(axis))])  14 us
    ppermute x8, starting transfers between devices, swapped(): lax.ppermute(x, axis, [(i, i ^ mask) for i in range(lax.axis_size(axis))])  8.57 us
    all_to_all x1, waiting for transfers between devices, packed_body(): lax.all_to_all(jnp.broadcast_to(idx[None], (devices, 2, SLOTS)), ('z', 'y...  7.25 us
    all_to_all x1, starting transfers between devices, packed_body(): lax.all_to_all(jnp.broadcast_to(idx[None], (devices, 2, SLOTS)), ('z', 'y...  4.89 us
    pallas_call x1, Pallas kernels, packed(): call(lambda *refs: own_kernel(cols * SLOTS, *refs), 'own', [smem, vmem],...  3.59 us
    pallas_call x1, Pallas kernels, packed(): call(lambda *refs: product_kernel(cols, piece, *refs), 'products', [smem]...  1.98 us
    pallas_call x1, Pallas kernels, packed_body(): call(lambda *refs: plan_kernel(rows, cols, *refs), 'plan', [vmem], [ints(...  1.65 us
    pallas_call x1, Pallas kernels, packed(): call(lambda *refs: cross_kernel(planes, cols, piece, *refs), 'cross', [sm...  1.45 us
  transfers between devices with their start and end apart: 9, of which 5 were waited for; matrix products, arithmetic and copies ran while one was open for 3% of the time, Pallas kernels for 13%

profile of v5, /device:TPU:0, one launch (start us, length us, event | category | flops | bytes accessed | tf_op | source)
XLA Modules:
  0.0 48.2 jit_solution(1582152697057344050)
XLA Ops:
  0.0 1.1 %spread.1 = f32[512,128]{1,0:T(8,128)S(1)} custom-call(f32[1024,128]{1,0:T(8,128)} %bitcast.78), custom_call_target="tpu_custom_call" | custom-call | tf_op jit(solution)/shard_map/spread/pallas_call | solution.py:397
  1.1 3.0 %collective-permute-start.7 = (f32[512,128]{1,0:T(8,128)S(1)}, f32[512,128]{1,0:T(8,128)S(1)}, u32[]{:S(2)}, u32[]{:S(2)}) collective-permute-start(f32[512,128]{1,0:T(8,128)S(1)} %spread.1), channel_id=1, source_target_pairs={{0,4},{1,5},{2,6},{3,7},{4,0},{5,1},{6,2},{7,3},{8,12},{9,13},{10,... | collective-permute-start | bytes 786440 | tf_op jit(solution)/shard_map/ppermute | solution.py:363
  4.1 0.7 %pad_add_fusion.2 = s32[2,8]{1,0:T(2,128)S(1)} fusion(s32[1,8]{1,0:T(1,128)} %bitcast.89, s32[1,8]{1,0:T(1,128)} %bitcast.84), kind=kLoop, calls=%fused_computation.49 | loop fusion | flops 16 | bytes 128 | tf_op jit(solution)/shard_map/concatenate | solution.py:401
  4.8 0.6 %broadcast_in_dim.114 = s32[32,2,8]{2,1,0:T(2,128)} broadcast(s32[2,8]{1,0:T(2,128)S(1)} %pad_add_fusion.2), dimensions={1,2} | broadcast | bytes 2112 | tf_op jit(solution)/shard_map/broadcast_in_dim | solution.py:402
  5.4 4.9 %all-to-all-start.6 = ((s32[32,2,8]{2,1,0:T(2,128)}), s32[32,2,8]{2,1,0:T(2,128)S(1)}, u32[]{:S(2)}, u32[]{:S(2)}) async-start(s32[32,2,8]{2,1,0:T(2,128)} %broadcast_in_dim.114), calls=%async_computation.6 | async-start | bytes 65536 | tf_op jit(solution)/shard_map/all_to_all | solution.py:402
  10.3 7.2 %all-to-all-done.6.refs_0_ = s32[32,2,8]{2,1,0:T(2,128)S(1)} async-done(((s32[32,2,8]{2,1,0:T(2,128)}), s32[32,2,8]{2,1,0:T(2,128)S(1)}, u32[]{:S(2)}, u32[]{:S(2)}) %all-to-all-start.6) | async-done | bytes 2080 | tf_op jit(solution)/shard_map/all_to_all | solution.py:402
  17.6 1.7 %plan.1 = (s32[24,128]{1,0:T(8,128)S(1)}, s32[8,256]{1,0:T(8,128)S(1)}, s32[1,1]{1,0:T(1,128)}) custom-call(s32[32,2,8]{2,1,0:T(2,128)S(1)} %all-to-all-done.6.refs_0_), custom_call_target="tpu_custom_call" | custom-call | tf_op jit(solution)/shard_map/plan/pallas_call | solution.py:403
  19.9 27.5 %conditional.1 = (f32[1,1,8,128,128]{4,3,2,1,0:T(8,128)S(1)}) conditional(s32[]{:T(128)} %bitcast.11, (f32[1,1,8,128,128]{4,3,2,1,0:T(8,128)}, s32[1,1,8]{2,1,0:T(1,128)}, s32[1,1,8]{2,1,0:T(1,128)}) %tuple.37, (s32[24,128]{1,0:T(8,128)S(1)}, f32[1024,128]{1,0:T(8,128)}, f32[512,128]{1,0:T(8,128)S(1)}, s32[8,256]{1,0:T(8,128)S(1)}) %tuple.83), branch_computations={%region_0.9_spmd, %region_9.10_spmd} | conditional | flops 806364224 | bytes 53494504 | solution.py:441
  19.9 0.0 copy-start.2
  19.9 1.5 %cross.1 = (f32[640,128]{1,0:T(8,128)S(1)}, f32[640,128]{1,0:T(8,128)S(1)}, f32[640,128]{1,0:T(8,128)S(1)}, f32[384,128]{1,0:T(8,128)S(1)}, f32[384,128]{1,0:T(8...) custom-call(s32[24,128]{1,0:T(8,128)S(1)} %get-tuple-element.407.refs_0_, ...), custom_call_target="tpu_custom_call" | custom-call | tf_op jit(solution)/shard_map/cond/branch_1_fun/cross/pallas_call | solution.py:412
  21.4 0.6 %collective-permute-start.3 = (f32[384,128]{1,0:T(8,128)S(1)}, f32[384,128]{1,0:T(8,128)S(1)}, u32[]{:S(2)}, u32[]{:S(2)}) collective-permute-start(f32[384,128]{1,0:T(8,128)S(1)} %get-tuple-element.415), channel_id=1, source_target_pairs={{0,8},{8,0},{16,24},{24,16},{1,9},{9,1},{17,25},{25,17},{2,10},{10... | collective-permute-start | bytes 589832 | tf_op jit(solution)/shard_map/cond/branch_1_fun/ppermute | solution.py:363
  22.0 0.6 %collective-permute-start.4 = (f32[384,128]{1,0:T(8,128)S(1)}, f32[384,128]{1,0:T(8,128)S(1)}, u32[]{:S(2)}, u32[]{:S(2)}) collective-permute-start(f32[384,128]{1,0:T(8,128)S(1)} %get-tuple-element.416), channel_id=1, source_target_pairs={{0,16},{8,24},{16,0},{24,8},{1,17},{9,25},{17,1},{25,9},{2,18},{10... | collective-permute-start | bytes 589832 | tf_op jit(solution)/shard_map/cond/branch_1_fun/ppermute | solution.py:363
  22.6 3.2 %collective-permute-start.5 = (f32[384,128]{1,0:T(8,128)S(1)}, f32[384,128]{1,0:T(8,128)S(1)}, u32[]{:S(2)}, u32[]{:S(2)}) collective-permute-start(f32[384,128]{1,0:T(8,128)S(1)} %get-tuple-element.417), channel_id=1, source_target_pairs={{0,24},{8,16},{16,8},{24,0},{1,25},{9,17},{17,9},{25,1},{2,26},{10... | collective-permute-start | bytes 589832 | tf_op jit(solution)/shard_map/cond/branch_1_fun/ppermute | solution.py:363
  25.8 0.5 %collective-permute-start.1 = (f32[640,128]{1,0:T(8,128)S(1)}, f32[640,128]{1,0:T(8,128)S(1)}, u32[]{:S(2)}, u32[]{:S(2)}) collective-permute-start(f32[640,128]{1,0:T(8,128)S(1)} %get-tuple-element.412), channel_id=1, source_target_pairs={{0,2},{1,3},{2,0},{3,1},{4,6},{5,7},{6,4},{7,5},{8,10},{9,11},{10,... | collective-permute-start | bytes 983048 | tf_op jit(solution)/shard_map/cond/branch_1_fun/ppermute | solution.py:363
  26.3 5.2 %collective-permute-done.3.refs_2_ = f32[384,128]{1,0:T(8,128)S(1)} collective-permute-done((f32[384,128]{1,0:T(8,128)S(1)}, f32[384,128]{1,0:T(8,128)S(1)}, u32[]{:S(2)}, u32[]{:S(2)}) %collective-permute-start.3) | collective-permute-done | bytes 196640 | tf_op jit(solution)/shard_map/cond/branch_1_fun/ppermute | solution.py:363
  31.5 3.6 %own.1.refs_2_ = f32[1024,128]{1,0:T(8,128)S(1)} custom-call(s32[8,256]{1,0:T(8,128)S(1)} %get-tuple-element.405.refs_0_, f32[1024,128]{1,0:T(8,128)} %get-tuple-element.406.refs_1_), custom_call_target="tpu_custom_call" | custom-call | tf_op jit(solution)/shard_map/cond/branch_1_fun/own/pallas_call | solution.py:420
  35.1 4.0 %collective-permute-done.4.refs_3_ = f32[384,128]{1,0:T(8,128)S(1)} collective-permute-done((f32[384,128]{1,0:T(8,128)S(1)}, f32[384,128]{1,0:T(8,128)S(1)}, u32[]{:S(2)}, u32[]{:S(2)}) %collective-permute-start.4) | collective-permute-done | bytes 196640 | tf_op jit(solution)/shard_map/cond/branch_1_fun/ppermute | solution.py:363
  39.2 0.9 %give.1 = (f32[320,128]{1,0:T(8,128)S(1)}, f32[320,128]{1,0:T(8,128)S(1)}) custom-call(s32[24,128]{1,0:T(8,128)S(1)} %get-tuple-element.407.refs_0_, f32[1024,128]{1,0:T(8,128)S(1)} %get-tuple-element.414.refs_1_, f32[384,128]{1,0:T(8,128)S(1)} %collective-permute-done.3.refs_2_, f32[384,128]{1,0:T(8,128)S(1)} %collective-permute-done.4.refs_3_, ...), custom_call_target="tpu_custom_call" | custom-call | tf_op jit(solution)/shard_map/cond/branch_1_fun/give/pallas_call | solution.py:424
  40.0 0.6 %collective-permute-start.6 = (f32[320,128]{1,0:T(8,128)S(1)}, f32[320,128]{1,0:T(8,128)S(1)}, u32[]{:S(2)}, u32[]{:S(2)}) collective-permute-start(f32[320,128]{1,0:T(8,128)S(1)} %get-tuple-element.419), channel_id=1, source_target_pairs={{0,4},{1,5},{2,6},{3,7},{4,0},{5,1},{6,2},{7,3},{8,12},{9,13},{10,... | collective-permute-start | bytes 491528 | tf_op jit(solution)/shard_map/cond/branch_1_fun/ppermute | solution.py:363
  40.6 1.9 %collective-permute-done.2.refs_5_ = f32[640,128]{1,0:T(8,128)S(1)} collective-permute-done((f32[640,128]{1,0:T(8,128)S(1)}, f32[640,128]{1,0:T(8,128)S(1)}, u32[]{:S(2)}, u32[]{:S(2)}) %collective-permute-start.2) | collective-permute-done | bytes 327712 | tf_op jit(solution)/shard_map/cond/branch_1_fun/ppermute | solution.py:363
  42.6 2.9 %collective-permute-done.6.refs_7_ = f32[320,128]{1,0:T(8,128)S(1)} collective-permute-done((f32[320,128]{1,0:T(8,128)S(1)}, f32[320,128]{1,0:T(8,128)S(1)}, u32[]{:S(2)}, u32[]{:S(2)}) %collective-permute-start.6) | collective-permute-done | bytes 163872 | tf_op jit(solution)/shard_map/cond/branch_1_fun/ppermute | solution.py:363
  45.4 2.0 %products.1 = f32[1024,128]{1,0:T(8,128)S(1)} custom-call(s32[8,256]{1,0:T(8,128)S(1)} %get-tuple-element.405.refs_0_, f32[1024,128]{1,0:T(8,128)S(1)} %copy-done.2, f32[1024,128]{1,0:T(8,128)S(1)} %own.1.refs_2_, f32[640,128]{1,0:T(8,128)S(1)} %collective-permute-done.refs_3_, f32[640,128]{1,0:T(8,128)S(1)} %collective-permute-done.1.refs_4_, ...), custom_call_target="tpu_custom_call" | custom-call | tf_op jit(solution)/shard_map/cond/branch_1_fun/products/pallas_call | solution.py:432
  47.4 0.0 copy-start.3
  47.4 0.8 %copy-done.3 = f32[1,1,8,128,128]{4,3,2,1,0:T(8,128)} copy-done((f32[1,1,8,128,128]{4,3,2,1,0:T(8,128)}, f32[1,1,8,128,128]{4,3,2,1,0:T(8,128)S(1)}, u32[]{:S(2)}) %copy-start.3) | copy-done | bytes 524312
  (7 shorter events, 0.0 us)
Async XLA Ops:
  1.1 18.8 %collective-permute-start.7 = (f32[512,128]{1,0:T(8,128)S(1)}, f32[512,128]{1,0:T(8,128)S(1)}, u32[]{:S(2)}, u32[]{:S(2)}) collective-permute-start(f32[512,128]{1,0:T(8,128)S(1)} %spread.1), channel_id=1, source_target_pairs={{0,4},{1,5},{2,6},{3,7},{4,0},{5,1},{6,2},{7,3},{8,12},{9,13},{10,... | collective-permute-start | bytes 786440 | tf_op jit(solution)/shard_map/ppermute | solution.py:363
  5.4 12.2 %all-to-all-start.6 = ((s32[32,2,8]{2,1,0:T(2,128)}), s32[32,2,8]{2,1,0:T(2,128)S(1)}, u32[]{:S(2)}, u32[]{:S(2)}) async-start(s32[32,2,8]{2,1,0:T(2,128)} %broadcast_in_dim.114), calls=%async_computation.6 | async-start | bytes 65536 | tf_op jit(solution)/shard_map/all_to_all | solution.py:402
  19.9 25.5 %copy-start.2 = (f32[1024,128]{1,0:T(8,128)S(1)}, f32[1024,128]{1,0:T(8,128)}, u32[]{:S(2)}) copy-start(f32[1024,128]{1,0:T(8,128)} %get-tuple-element.406.refs_1_) | copy-start | bytes 1572868 | tf_op jit(solution)/shard_map/cond
  21.4 10.2 %collective-permute-start.3 = (f32[384,128]{1,0:T(8,128)S(1)}, f32[384,128]{1,0:T(8,128)S(1)}, u32[]{:S(2)}, u32[]{:S(2)}) collective-permute-start(f32[384,128]{1,0:T(8,128)S(1)} %get-tuple-element.415), channel_id=1, source_target_pairs={{0,8},{8,0},{16,24},{24,16},{1,9},{9,1},{17,25},{25,17},{2,10},{10... | collective-permute-start | bytes 589832 | tf_op jit(solution)/shard_map/cond/branch_1_fun/ppermute | solution.py:363
  22.0 17.1 %collective-permute-start.4 = (f32[384,128]{1,0:T(8,128)S(1)}, f32[384,128]{1,0:T(8,128)S(1)}, u32[]{:S(2)}, u32[]{:S(2)}) collective-permute-start(f32[384,128]{1,0:T(8,128)S(1)} %get-tuple-element.416), channel_id=1, source_target_pairs={{0,16},{8,24},{16,0},{24,8},{1,17},{9,25},{17,1},{25,9},{2,18},{10... | collective-permute-start | bytes 589832 | tf_op jit(solution)/shard_map/cond/branch_1_fun/ppermute | solution.py:363
  22.6 16.6 %collective-permute-start.5 = (f32[384,128]{1,0:T(8,128)S(1)}, f32[384,128]{1,0:T(8,128)S(1)}, u32[]{:S(2)}, u32[]{:S(2)}) collective-permute-start(f32[384,128]{1,0:T(8,128)S(1)} %get-tuple-element.417), channel_id=1, source_target_pairs={{0,24},{8,16},{16,8},{24,0},{1,25},{9,17},{17,9},{25,1},{2,26},{10... | collective-permute-start | bytes 589832 | tf_op jit(solution)/shard_map/cond/branch_1_fun/ppermute | solution.py:363
  25.8 14.8 %collective-permute-start = (f32[640,128]{1,0:T(8,128)S(1)}, f32[640,128]{1,0:T(8,128)S(1)}, u32[]{:S(2)}, u32[]{:S(2)}) collective-permute-start(f32[640,128]{1,0:T(8,128)S(1)} %get-tuple-element.411), channel_id=1, source_target_pairs={{0,1},{1,0},{2,3},{3,2},{4,5},{5,4},{6,7},{7,6},{8,9},{9,8},{10,11... | collective-permute-start | bytes 983048 | tf_op jit(solution)/shard_map/cond/branch_1_fun/ppermute | solution.py:363
  25.8 14.8 %collective-permute-start.1 = (f32[640,128]{1,0:T(8,128)S(1)}, f32[640,128]{1,0:T(8,128)S(1)}, u32[]{:S(2)}, u32[]{:S(2)}) collective-permute-start(f32[640,128]{1,0:T(8,128)S(1)} %get-tuple-element.412), channel_id=1, source_target_pairs={{0,2},{1,3},{2,0},{3,1},{4,6},{5,7},{6,4},{7,5},{8,10},{9,11},{10,... | collective-permute-start | bytes 983048 | tf_op jit(solution)/shard_map/cond/branch_1_fun/ppermute | solution.py:363
  31.5 11.1 %collective-permute-start.2 = (f32[640,128]{1,0:T(8,128)S(1)}, f32[640,128]{1,0:T(8,128)S(1)}, u32[]{:S(2)}, u32[]{:S(2)}) collective-permute-start(f32[640,128]{1,0:T(8,128)S(1)} %get-tuple-element.413), channel_id=1, source_target_pairs={{0,3},{1,2},{2,1},{3,0},{4,7},{5,6},{6,5},{7,4},{8,11},{9,10},{10,... | collective-permute-start | bytes 983048 | tf_op jit(solution)/shard_map/cond/branch_1_fun/ppermute | solution.py:363
  40.0 5.4 %collective-permute-start.6 = (f32[320,128]{1,0:T(8,128)S(1)}, f32[320,128]{1,0:T(8,128)S(1)}, u32[]{:S(2)}, u32[]{:S(2)}) collective-permute-start(f32[320,128]{1,0:T(8,128)S(1)} %get-tuple-element.419), channel_id=1, source_target_pairs={{0,4},{1,5},{2,6},{3,7},{4,0},{5,1},{6,2},{7,3},{8,12},{9,13},{10,... | collective-permute-start | bytes 491528 | tf_op jit(solution)/shard_map/cond/branch_1_fun/ppermute | solution.py:363
  47.4 0.8 %copy-start.3 = (f32[1,1,8,128,128]{4,3,2,1,0:T(8,128)}, f32[1,1,8,128,128]{4,3,2,1,0:T(8,128)S(1)}, u32[]{:S(2)}) copy-start(f32[1,1,8,128,128]{4,3,2,1,0:T(8,128)S(1)} %get-tuple-element.694) | copy-start | bytes 1572868

commit v6 on v5

--- a/solution.py
+++ b/solution.py
@@ -10,9 +10,8 @@
 SECTIONS = 4
 BS = 128
 SLOTS = 8
-LCAP = 5
-RCAP = 5
-ZCAP = 6
+SIZES = ((4, 5, 6), (8, 8, 12))
+LMOST, RMOST, ZMOST = SIZES[-1]
 VMEM_LIMIT = 32 * 1024 * 1024
 
 
@@ -127,15 +126,15 @@
     return total[None, None]
 
 
-GROUP = (0, 4)
+GROUP = (0, 1, 4, 5)
 
 
 def piece_of(p):
-    return p // 4
+    return 2 * (p // 4) + p % 2
 
 
 def group_of(p):
-    return p % 4
+    return (p // 2) % 2
 
 
 def bf(x):
@@ -151,7 +150,7 @@
     return lax.dot_general(a, b, dims, preferred_element_type=jnp.float32)
 
 
-def plan_kernel(rows, cols, idx_ref, table_ref, list_ref, over_ref):
+def plan_kernel(rows, cols, idx_ref, table_ref, list_ref, size_ref):
     devices = rows * cols
     plane = 2 * cols
     n = devices * SLOTS
@@ -159,7 +158,7 @@
     rb = NBLK // rows
     cb = NBLK // cols
     per_row = cols * SLOTS
-    lefts = (cols - 1) * LCAP
+    lefts = (cols - 1) * LMOST
     my_plane, my_p = lax.axis_index("z"), lax.axis_index(("y", "col"))
     my_row = 2 * my_plane + lax.axis_index("y")
     my_col = lax.axis_index("col")
@@ -213,8 +212,12 @@
     )
     cross_at = jnp.where(cross, mm(ind(cross), ind(before & together)), -1.0)
 
-    over = jnp.maximum(jnp.max(left_at) - (LCAP - 1), jnp.max(right_at) - (RCAP - 1))
-    over_ref[0, 0] = jnp.maximum(over, jnp.max(cross_at) - (ZCAP - 1)).astype(jnp.int32)
+    tops = [jnp.max(at) + 1.0 for at in (left_at, right_at, cross_at)]
+    size = jnp.int32(0)
+    for most in SIZES:
+        fits = (tops[0] <= most[0]) & (tops[1] <= most[1]) & (tops[2] <= most[2])
+        size = size + jnp.where(fits, 0, 1)
+    size_ref[0, 0] = size
 
     lanes = lax.broadcasted_iota(jnp.int32, (1, BS), 1)
 
@@ -227,27 +230,27 @@
 
     mine = (lane // SLOTS) == me
     to_col = mm(ind(my_row * cols + zed % cols == dev_r), bf(left_at))
-    table(0, jnp.where(mine, to_col, -1.0), slot_r, LCAP)
+    table(0, jnp.where(mine, to_col, -1.0), slot_r, LMOST)
     here = ((lane // in_plane) == my_plane) & (group_of((lane // SLOTS) % plane) == group_of(my_p))
     partner = piece_of((lane // SLOTS) % plane) ^ piece_of(my_p)
     local = (partner * SLOTS + lane % SLOTS).astype(jnp.float32)
-    table(8, jnp.where(here, cross_at, -1.0), local, ZCAP)
+    table(8, jnp.where(here, cross_at, -1.0), local, ZMOST)
     came = jnp.sum(jnp.where(zed == my_plane, cross_at, 0.0), axis=0, keepdims=True)
-    away = len(GROUP) * SLOTS + ZCAP * (((lane // in_plane) ^ my_plane) - 1)
+    away = len(GROUP) * SLOTS + ZMOST * (((lane // in_plane) ^ my_plane) - 1)
     source = jnp.where((lane // in_plane) == my_plane, local, away.astype(jnp.float32) + came)
     partners = jnp.zeros((8, devices), jnp.bool_)
     for g, mask in enumerate(GROUP):
         partners = partners | ((zed == g) & (dev_r == my_plane * plane + (my_p ^ mask)))
-    table(16, mm(ind(partners), bf(right_at)), source, RCAP)
+    table(16, mm(ind(partners), bf(right_at)), source, RMOST)
 
     left_me = jnp.sum(jnp.where(dev == me, left_at, 0.0), axis=0, keepdims=True)
     right_me = jnp.sum(jnp.where(dev == me, right_at, 0.0), axis=0, keepdims=True)
     from_col = ((lane // SLOTS) % cols) ^ my_col
-    held_a = jnp.where(mine, slot_r, (SLOTS + LCAP * (from_col - 1)).astype(jnp.float32) + left_me)
+    held_a = jnp.where(mine, slot_r, (SLOTS + LMOST * (from_col - 1)).astype(jnp.float32) + left_me)
     held_b = as_column(jnp.where(mine, slot_r, SLOTS + lefts + right_me))
     my_product = product & (((sub // SLOTS) % cols) == my_col) & ((lane // per_row) == my_row)
     rank = mm(ind(lane < sub), ind(my_product))
-    code = (hit - 1.0) * 64.0 + held_a * 32.0 + held_b + 1.0
+    code = (hit - 1.0) * 256.0 + held_a * 64.0 + held_b + 1.0
     out_sub = lax.broadcasted_iota(jnp.int32, (list_ref.shape[0], 1), 0)
     listed = jnp.zeros(list_ref.shape, jnp.float32)
     for k in range(2 * ACT):
@@ -256,50 +259,56 @@
     list_ref[...] = listed.astype(jnp.int32) - 1
 
 
-def copy_listed(table_ref, row, most, height, from_ref, to_ref):
+def copy_listed(table_ref, row, most, height, sources, to_ref):
     for k in range(most):
         at = table_ref[row, k]
 
         @pl.when(at >= 0)
         def _():
-            here = pl.ds(pl.multiple_of(at * height, height), height)
-            to_ref[k * height : (k + 1) * height, :] = from_ref[here, :]
-
-
-def spread_kernel(piece, blocks_ref, *outs):
+            for ref, first, count, stride, skip in sources:
+
+                @pl.when((at >= first) & (at < first + count))
+                def _():
+                    here = pl.ds(pl.multiple_of((at - first) * stride + skip, height), height)
+                    to_ref[k * height : (k + 1) * height, :] = ref[here, :]
+
+
+def group_pieces(piece, blocks_ref, piece_refs):
     mine = piece_of(lax.axis_index(("y", "col")))
+    sources = [(blocks_ref, 0, SLOTS, BS, mine * piece)]
+    return sources + [(ref, (g + 1) * SLOTS, SLOTS, piece, 0) for g, ref in enumerate(piece_refs)]
+
+
+def spread_kernel(piece, blocks_ref, rows_ref, cols_ref, idx_ref, *outs):
+    mine = piece_of(lax.axis_index(("y", "col")))
+    for half, ref in enumerate((rows_ref, cols_ref)):
+        idx_ref[:, half, :] = jnp.broadcast_to(ref[...], (idx_ref.shape[0], SLOTS))
     for g, out_ref in enumerate(outs):
         for t in range(SLOTS):
             at = pl.ds(pl.multiple_of(t * BS + (mine ^ (g + 1)) * piece, piece), piece)
             out_ref[t * piece : (t + 1) * piece, :] = blocks_ref[at, :]
 
 
-def cross_kernel(planes, cols, piece, table_ref, blocks_ref, *refs):
+def cross_kernel(piece, most, table_ref, blocks_ref, *refs):
     partners = len(GROUP) - 1
-    piece_refs, left_refs = refs[:partners], refs[partners : partners + cols - 1]
-    cross_refs, held_ref = refs[partners + cols - 1 : -1], refs[-1]
-    mine = piece_of(lax.axis_index(("y", "col")))
-    for t in range(SLOTS):
-        at = pl.ds(pl.multiple_of(t * BS + mine * piece, piece), piece)
-        held_ref[t * piece : (t + 1) * piece, :] = blocks_ref[at, :]
-    size = SLOTS * piece
-    for g, ref in enumerate(piece_refs):
-        held_ref[(g + 1) * size : (g + 2) * size, :] = ref[...]
-    for m, out_ref in enumerate(cross_refs):
-        copy_listed(table_ref, 8 + (lax.axis_index("z") ^ (m + 1)), ZCAP, piece, held_ref, out_ref)
-    for m, out_ref in enumerate(left_refs):
-        copy_listed(table_ref, lax.axis_index("col") ^ (m + 1), LCAP, BS, blocks_ref, out_ref)
-
-
-def give_kernel(planes, piece, table_ref, held_ref, *refs):
-    crossed_refs, outs, all_ref = refs[: planes - 1], refs[planes - 1 : -1], refs[-1]
-    here = held_ref.shape[0]
-    size = ZCAP * piece
-    all_ref[:here, :] = held_ref[...]
-    for m, ref in enumerate(crossed_refs):
-        all_ref[here + m * size : here + (m + 1) * size, :] = ref[...]
-    for g, out_ref in enumerate(outs):
-        copy_listed(table_ref, 16 + g, RCAP, piece, all_ref, out_ref)
+    sources = group_pieces(piece, blocks_ref, refs[:partners])
+    for m, out_ref in enumerate(refs[partners:]):
+        copy_listed(table_ref, 8 + (lax.axis_index("z") ^ (m + 1)), most, piece, sources, out_ref)
+
+
+def left_kernel(most, table_ref, blocks_ref, *outs):
+    for m, out_ref in enumerate(outs):
+        copy_listed(table_ref, lax.axis_index("col") ^ (m + 1), most, BS, [(blocks_ref, 0, SLOTS, BS, 0)], out_ref)
+
+
+def give_kernel(planes, piece, zmost, most, table_ref, blocks_ref, *refs):
+    partners = len(GROUP) - 1
+    piece_refs, crossed_refs = refs[:partners], refs[partners : partners + planes - 1]
+    sources = group_pieces(piece, blocks_ref, piece_refs)
+    first = len(GROUP) * SLOTS
+    sources += [(ref, first + m * ZMOST, zmost, piece, 0) for m, ref in enumerate(crossed_refs)]
+    for g, out_ref in enumerate(refs[partners + planes - 1 :]):
+        copy_listed(table_ref, 16 + g, most, piece, sources, out_ref)
 
 
 def add_products(per_row, list_ref, held_ref, out_ref, wanted):
@@ -312,13 +321,13 @@
 
     def one(i, k):
         code = list_ref[k, first + i]
-        a, b = (code // 32) % 32, code % 32
+        a, b = (code // 64) % 64, code % 64
 
         @pl.when((code >= 0) & wanted(a, b))
         def _():
             a_high, a_low = block(a)
             b_high, b_low = block(b)
-            at = pl.ds(pl.multiple_of((code // 1024) * BS, BS), BS)
+            at = pl.ds(pl.multiple_of((code // 4096) * BS, BS), BS)
             out_ref[at, :] += mm(
                 jnp.concatenate([a_high, a_high, a_low], axis=1), jnp.concatenate([b_high, b_low, b_high], axis=0)
             )
@@ -341,7 +350,7 @@
     add_products(per_row, list_ref, blocks_ref, out_ref, lambda a, b: (a < SLOTS) & (b < SLOTS))
 
 
-def product_kernel(cols, piece, list_ref, blocks_ref, start_ref, *refs):
+def product_kernel(cols, piece, lmost, rmost, list_ref, blocks_ref, start_ref, *refs):
     lefts, group = cols - 1, len(GROUP)
     left_refs, right_refs = refs[:lefts], refs[lefts : lefts + group]
     out_ref, held_ref = refs[lefts + group :]
@@ -350,10 +359,10 @@
     held_ref[: SLOTS * BS, :] = blocks_ref[...]
     at = SLOTS * BS
     for ref in left_refs:
-        held_ref[at : at + LCAP * BS, :] = ref[...]
-        at += LCAP * BS
+        held_ref[at : at + lmost * BS, :] = ref[...]
+        at += LMOST * BS
     for g, ref in enumerate(right_refs):
-        for k in range(RCAP):
+        for k in range(rmost):
             to = pl.ds(pl.multiple_of(at + k * BS + (mine ^ g) * piece, piece), piece)
             held_ref[to, :] = ref[k * piece : (k + 1) * piece, :]
     add_products(cols * SLOTS, list_ref, held_ref, out_ref, lambda a, b: (a >= SLOTS) | (b >= SLOTS))
@@ -394,13 +403,15 @@
             name=name,
         )
 
-    spread = call(
-        lambda *refs: spread_kernel(piece, *refs), "spread", [vmem], [floats(SLOTS * piece)] * (group - 1)
-    )(flat)
+    idx, *spread = call(
+        lambda *refs: spread_kernel(piece, *refs),
+        "spread",
+        [vmem] * 3,
+        [ints(devices, 2, SLOTS)] + [floats(SLOTS * piece)] * (group - 1),
+    )(flat, block_rows[0], block_cols[0])
     pieces = [swapped(x, in_plane, mask) for x, mask in zip(spread, GROUP[1:])]
-    idx = jnp.concatenate([block_rows[0], block_cols[0]])
-    idx = lax.all_to_all(jnp.broadcast_to(idx[None], (devices, 2, SLOTS)), ("z", "y", "col"), 0, 0)
-    table, listed, over = call(
+    idx = lax.all_to_all(idx, ("z", "y", "col"), 0, 0)
+    table, listed, size = call(
         lambda *refs: plan_kernel(rows, cols, *refs),
         "plan",
         [vmem],
@@ -408,37 +419,40 @@
         specs=[vmem, vmem, smem],
     )(idx)
 
-    def packed():
-        *outgoing, held = call(
-            lambda *refs: cross_kernel(planes, cols, piece, *refs),
+    def packed(lmost, rmost, zmost):
+        crossing = call(
+            lambda *refs: cross_kernel(piece, zmost, *refs),
             "cross",
             [smem] + [vmem] * group,
-            [floats(LCAP * BS)] * (cols - 1) + [floats(ZCAP * piece)] * (planes - 1) + [floats(group * SLOTS * piece)],
+            [floats(zmost * piece)] * (planes - 1),
         )(table, flat, *pieces)
-        crossed = [swapped(x, "z", m + 1) for m, x in enumerate(outgoing[cols - 1 :])]
-        lefts = [swapped(x, "col", m + 1) for m, x in enumerate(outgoing[: cols - 1])]
+        crossed = [swapped(x, "z", m + 1) for m, x in enumerate(crossing)]
         own = call(
             lambda *refs: own_kernel(cols * SLOTS, *refs), "own", [smem, vmem], [floats(SLOTS * BS)]
         )(listed, flat)
-        held, *own = lax.optimization_barrier((held, *own))
+        later, *own = lax.optimization_barrier((table, *own))
+        leaving = call(
+            lambda *refs: left_kernel(lmost, *refs), "left", [smem, vmem], [floats(lmost * BS)] * (cols - 1)
+        )(later, flat)
+        lefts = [swapped(x, "col", m + 1) for m, x in enumerate(leaving)]
         giving = call(
-            lambda *refs: give_kernel(planes, piece, *refs),
+            lambda *refs: give_kernel(planes, piece, zmost, rmost, *refs),
             "give",
-            [smem] + [vmem] * planes,
-            [floats(RCAP * piece)] * group,
-            [pltpu.VMEM(((group * SLOTS + (planes - 1) * ZCAP) * piece, BS), jnp.float32)],
-        )(table, held, *crossed)
+            [smem] + [vmem] * (group + planes - 1),
+            [floats(rmost * piece)] * group,
+        )(later, flat, *pieces, *crossed)
         rights = [swapped(x, in_plane, mask) if mask else x for x, mask in zip(giving, GROUP)]
         out = call(
-            lambda *refs: product_kernel(cols, piece, *refs),
+            lambda *refs: product_kernel(cols, piece, lmost, rmost, *refs),
             "products",
             [smem] + [vmem] * (2 + cols - 1 + group),
             [floats(SLOTS * BS)],
-            [pltpu.VMEM(((SLOTS + (cols - 1) * LCAP + RCAP) * BS, BS), jnp.float32)],
+            [pltpu.VMEM(((SLOTS + (cols - 1) * LMOST + rmost) * BS, BS), jnp.float32)],
         )(listed, flat, *own, *lefts, *rights)
         return out[0].reshape(blocks.shape)
 
-    return lax.cond(over[0, 0] <= 0, packed, lambda: whole_tiles(blocks, block_rows, block_cols))
+    branches = [lambda most=most: packed(*most) for most in SIZES]
+    return lax.switch(size[0, 0], branches + [lambda: whole_tiles(blocks, block_rows, block_cols)])
 
 
 def solution(mesh):

time: 48.8 us -> 48 us (0.984)
  waiting for transfers between devices: 21.3 us -> 16.8 us
  starting transfers between devices: 13.5 us -> 16.9 us
  Pallas kernels: 10.6 us -> 13.3 us
  local copies, waits for them, and re-layouts: 1.42 us -> 0.01 us
  other arithmetic: 0.68 us -> 0 us
    ppermute x8 -> x12, waiting for transfers between devices: 14 us -> 9.55 us  [swapped(): lax.ppermute(x, axis, [(i, i ^ mask) for i in range(lax.axis_size(axis))])]
    pallas_call x4 -> x5, Pallas kernels: 5.37 us -> 7.97 us  [the longest x1 2.96 us: packed(): call(lambda *refs: product_kernel(cols, piece, lmost, rmost, *refs), 'pro...]
    ppermute x8 -> x12, starting transfers between devices: 8.57 us -> 10.9 us  [swapped(): lax.ppermute(x, axis, [(i, i ^ mask) for i in range(lax.axis_size(axis))])]
    all_to_all x1, starting transfers between devices: 4.89 us -> 6.04 us  [packed_body(): idx = lax.all_to_all(idx, ('z', 'y', 'col'), 0, 0)]
    unnamed x2 -> x0, local copies, waits for them, and re-layouts: 0.79 us -> none
    concatenate x1 -> x0, other arithmetic: 0.68 us -> none  [packed_body(): idx = jnp.concatenate([block_rows[0], block_cols[0]])]
    broadcast_in_dim x1 -> x0, local copies, waits for them, and re-layouts: 0.63 us -> none  [packed_body(): jnp.broadcast_to(idx[None], (devices, 2, SLOTS))]
  transfers between devices with their start and end apart: 9 -> 13, of which waited for: 5 -> 6; matrix products, arithmetic and copies ran while one was open for 3% -> 0% of each run, Pallas kernels for 13% -> 15%
where the time goes in v6:
time: 48 us; the launch traced here: 47.8 us
  starting transfers between devices  16.9 us (35%)
  waiting for transfers between devices  16.8 us (35%)
  Pallas kernels  13.3 us (28%)
  between operations  0.69 us (1%)
    ppermute x12, starting transfers between devices, swapped(): lax.ppermute(x, axis, [(i, i ^ mask) for i in range(lax.axis_size(axis))])  10.9 us
    ppermute x12, waiting for transfers between devices, swapped(): lax.ppermute(x, axis, [(i, i ^ mask) for i in range(lax.axis_size(axis))])  9.55 us
    all_to_all x1, waiting for transfers between devices, packed_body(): idx = lax.all_to_all(idx, ('z', 'y', 'col'), 0, 0)  7.25 us
    all_to_all x1, starting transfers between devices, packed_body(): idx = lax.all_to_all(idx, ('z', 'y', 'col'), 0, 0)  6.04 us
    pallas_call x1, Pallas kernels, packed(): call(lambda *refs: own_kernel(cols * SLOTS, *refs), 'own', [smem, vmem],...  3.62 us
    pallas_call x1, Pallas kernels, packed(): call(lambda *refs: product_kernel(cols, piece, lmost, rmost, *refs), 'pro...  2.96 us
    pallas_call x1, Pallas kernels, packed_body(): call(lambda *refs: spread_kernel(piece, *refs), 'spread', [vmem] * 3, [in...  1.7 us
    pallas_call x1, Pallas kernels, packed_body(): call(lambda *refs: plan_kernel(rows, cols, *refs), 'plan', [vmem], [ints(...  1.67 us
  transfers between devices with their start and end apart: 13, of which 6 were waited for; matrix products, arithmetic and copies ran while one was open for 0% of the time, Pallas kernels for 15%

profile of v6, /device:TPU:0, one launch (start us, length us, event | category | flops | bytes accessed | tf_op | source)
XLA Modules:
  0.0 47.8 jit_solution(15123554628946858380)
XLA Ops:
  0.0 1.7 %spread.1 = (s32[32,2,8]{2,1,0:T(2,128)}, f32[256,128]{1,0:T(8,128)S(1)}, f32[256,128]{1,0:T(8,128)S(1)}, f32[256,128]{1,0:T(8,128)S(1)}) custom-call(f32[1024,128]{1,0:T(8,128)} %bitcast.79, s32[1,8]{1,0:T(1,128)} %bitcast.84, s32[1,8]{1,0:T(1,128)} %bitcast.89), custom_call_target="tpu_custom_call" | custom-call | tf_op jit(solution)/shard_map/spread/pallas_call | solution.py:406
  1.7 0.5 collective-permute-start.18
  2.1 2.5 %collective-permute-start.19 = (f32[256,128]{1,0:T(8,128)S(1)}, f32[256,128]{1,0:T(8,128)S(1)}, u32[]{:S(2)}, u32[]{:S(2)}) collective-permute-start(f32[256,128]{1,0:T(8,128)S(1)} %get-tuple-element.470), channel_id=1, source_target_pairs={{0,4},{1,5},{2,6},{3,7},{4,0},{5,1},{6,2},{7,3},{8,12},{9,13},{10,... | collective-permute-start | bytes 393224 | tf_op jit(solution)/shard_map/ppermute | solution.py:372
  4.8 6.0 %all-to-all-start.6 = ((s32[32,2,8]{2,1,0:T(2,128)}), s32[32,2,8]{2,1,0:T(2,128)S(1)}, u32[]{:S(2)}, u32[]{:S(2)}) async-start(s32[32,2,8]{2,1,0:T(2,128)} %get-tuple-element.465), calls=%async_computation.6 | async-start | bytes 65536 | tf_op jit(solution)/shard_map/all_to_all | solution.py:413
  10.9 7.2 %all-to-all-done.6.refs_0_ = s32[32,2,8]{2,1,0:T(2,128)S(1)} async-done(((s32[32,2,8]{2,1,0:T(2,128)}), s32[32,2,8]{2,1,0:T(2,128)S(1)}, u32[]{:S(2)}, u32[]{:S(2)}) %all-to-all-start.6) | async-done | bytes 2080 | tf_op jit(solution)/shard_map/all_to_all | solution.py:413
  18.1 1.7 %plan.1 = (s32[24,128]{1,0:T(8,128)S(1)}, s32[8,256]{1,0:T(8,128)S(1)}, s32[1,1]{1,0:T(1,128)}) custom-call(s32[32,2,8]{2,1,0:T(2,128)S(1)} %all-to-all-done.6.refs_0_), custom_call_target="tpu_custom_call" | custom-call | tf_op jit(solution)/shard_map/plan/pallas_call | solution.py:414
  20.5 27.3 %conditional.1 = (f32[1,1,8,128,128]{4,3,2,1,0:T(8,128)}) conditional(s32[]{:T(128)} %bitcast.13, (s32[8,256]{1,0:T(8,128)S(1)}, f32[1024,128]{1,0:T(8,128)}, s32[24,128]{1,0:T(8,128)S(1)}, f32[256,128]{1,0:T(8,128)S(1)}, f32[256,128]{1,0:T(8,128)S(1)}, /*index=5*/f32[256,128]{1,0:T(8,128)S(1)}) %tuple.89, (s32[8,256]{1,0:T(8,128)S(1)}, ...), branch_computations={%region_0.0_spmd, %region_1.0_spmd, %region_2.11_spmd} | conditional | flops 806364224 | bytes 53494504 | solution.py:455
  20.5 1.4 %cross.2 = (f32[192,128]{1,0:T(8,128)S(1)}, f32[192,128]{1,0:T(8,128)S(1)}, f32[192,128]{1,0:T(8,128)S(1)}) custom-call(s32[24,128]{1,0:T(8,128)S(1)} %get-tuple-element.409.refs_0_, f32[1024,128]{1,0:T(8,128)} %get-tuple-element.406.refs_1_, f32[256,128]{1,0:T(8,128)S(1)} %get-tuple-element.413.refs_2_, f32[256,128]{1,0:T(8,128)S(1)} %get-tuple-element.414.refs_3_, ...), custom_call_target="tpu_custom_call" | custom-call | tf_op jit(solution)/shard_map/cond/branch_0_fun/cross/pallas_call | solution.py:423
  21.9 0.6 %collective-permute-start.3 = (f32[192,128]{1,0:T(8,128)S(1)}, f32[192,128]{1,0:T(8,128)S(1)}, u32[]{:S(2)}, u32[]{:S(2)}) collective-permute-start(f32[192,128]{1,0:T(8,128)S(1)} %get-tuple-element.416), channel_id=1, source_target_pairs={{0,8},{8,0},{16,24},{24,16},{1,9},{9,1},{17,25},{25,17},{2,10},{10... | collective-permute-start | bytes 294920 | tf_op jit(solution)/shard_map/cond/branch_0_fun/ppermute | solution.py:372
  22.5 0.5 %collective-permute-start.4 = (f32[192,128]{1,0:T(8,128)S(1)}, f32[192,128]{1,0:T(8,128)S(1)}, u32[]{:S(2)}, u32[]{:S(2)}) collective-permute-start(f32[192,128]{1,0:T(8,128)S(1)} %get-tuple-element.417), channel_id=1, source_target_pairs={{0,16},{8,24},{16,0},{24,8},{1,17},{9,25},{17,1},{25,9},{2,18},{10... | collective-permute-start | bytes 294920 | tf_op jit(solution)/shard_map/cond/branch_0_fun/ppermute | solution.py:372
  23.0 3.3 %collective-permute-start.5 = (f32[192,128]{1,0:T(8,128)S(1)}, f32[192,128]{1,0:T(8,128)S(1)}, u32[]{:S(2)}, u32[]{:S(2)}) collective-permute-start(f32[192,128]{1,0:T(8,128)S(1)} %get-tuple-element.418), channel_id=1, source_target_pairs={{0,24},{8,16},{16,8},{24,0},{1,25},{9,17},{17,9},{25,1},{2,26},{10... | collective-permute-start | bytes 294920 | tf_op jit(solution)/shard_map/cond/branch_0_fun/ppermute | solution.py:372
  26.3 3.6 %own.2.refs_2_ = f32[1024,128]{1,0:T(8,128)S(1)} custom-call(s32[8,256]{1,0:T(8,128)S(1)} %get-tuple-element.405.refs_0_, f32[1024,128]{1,0:T(8,128)} %get-tuple-element.406.refs_1_), custom_call_target="tpu_custom_call" | custom-call | tf_op jit(solution)/shard_map/cond/branch_0_fun/own/pallas_call | solution.py:430
  30.0 0.9 %left.2 = (f32[512,128]{1,0:T(8,128)S(1)}, f32[512,128]{1,0:T(8,128)S(1)}, f32[512,128]{1,0:T(8,128)S(1)}) custom-call(s32[24,128]{1,0:T(8,128)S(1)} %get-tuple-element.409.refs_0_, f32[1024,128]{1,0:T(8,128)S(1)} %copy-done.1), custom_call_target="tpu_custom_call" | custom-call | tf_op jit(solution)/shard_map/cond/branch_0_fun/left/pallas_call | solution.py:434
  31.0 1.8 %collective-permute-start.2 = (f32[512,128]{1,0:T(8,128)S(1)}, f32[512,128]{1,0:T(8,128)S(1)}, u32[]{:S(2)}, u32[]{:S(2)}) collective-permute-start(f32[512,128]{1,0:T(8,128)S(1)} %get-tuple-element.412), channel_id=1, source_target_pairs={{0,3},{1,2},{2,1},{3,0},{4,7},{5,6},{6,5},{7,4},{8,11},{9,10},{10,... | collective-permute-start | bytes 786440 | tf_op jit(solution)/shard_map/cond/branch_0_fun/ppermute | solution.py:372
  32.8 0.3 collective-permute-done.4.refs_6_
  33.1 1.1 %give.2 = (f32[160,128]{1,0:T(8,128)S(1)}, f32[160,128]{1,0:T(8,128)S(1)}, f32[160,128]{1,0:T(8,128)S(1)}, f32[160,128]{1,0:T(8,128)S(1)}) custom-call(s32[24,128]{1,0:T(8,128)S(1)} %get-tuple-element.409.refs_0_, f32[1024,128]{1,0:T(8,128)S(1)} %copy-done.1, f32[256,128]{1,0:T(8,128)S(1)} %get-tuple-element.413.refs_2_, ...), custom_call_target="tpu_custom_call" | custom-call | tf_op jit(solution)/shard_map/cond/branch_0_fun/give/pallas_call | solution.py:438
  34.1 0.2 collective-permute-start.6
  34.3 0.7 %collective-permute-start.7 = (f32[160,128]{1,0:T(8,128)S(1)}, f32[160,128]{1,0:T(8,128)S(1)}, u32[]{:S(2)}, u32[]{:S(2)}) collective-permute-start(f32[160,128]{1,0:T(8,128)S(1)} %get-tuple-element.421), channel_id=1, source_target_pairs={{0,4},{1,5},{2,6},{3,7},{4,0},{5,1},{6,2},{7,3},{8,12},{9,13},{10,... | collective-permute-start | bytes 245768 | tf_op jit(solution)/shard_map/cond/branch_0_fun/ppermute | solution.py:372
  34.9 0.5 %collective-permute-done.6.refs_7_ = f32[160,128]{1,0:T(8,128)S(1)} collective-permute-done((f32[160,128]{1,0:T(8,128)S(1)}, f32[160,128]{1,0:T(8,128)S(1)}, u32[]{:S(2)}, u32[]{:S(2)}) %collective-permute-start.6) | collective-permute-done | bytes 81952 | tf_op jit(solution)/shard_map/cond/branch_0_fun/ppermute | solution.py:372
  35.5 0.6 %collective-permute-start.8 = (f32[160,128]{1,0:T(8,128)S(1)}, f32[160,128]{1,0:T(8,128)S(1)}, u32[]{:S(2)}, u32[]{:S(2)}) collective-permute-start(f32[160,128]{1,0:T(8,128)S(1)} %get-tuple-element.422), channel_id=1, source_target_pairs={{0,5},{1,4},{2,7},{3,6},{4,1},{5,0},{6,3},{7,2},{8,13},{9,12},{10,... | collective-permute-start | bytes 245768 | tf_op jit(solution)/shard_map/cond/branch_0_fun/ppermute | solution.py:372
  36.1 3.5 %collective-permute-done.7.refs_8_ = f32[160,128]{1,0:T(8,128)S(1)} collective-permute-done((f32[160,128]{1,0:T(8,128)S(1)}, f32[160,128]{1,0:T(8,128)S(1)}, u32[]{:S(2)}, u32[]{:S(2)}) %collective-permute-start.7) | collective-permute-done | bytes 81952 | tf_op jit(solution)/shard_map/cond/branch_0_fun/ppermute | solution.py:372
  39.5 0.8 %collective-permute-done.8.refs_9_ = f32[160,128]{1,0:T(8,128)S(1)} collective-permute-done((f32[160,128]{1,0:T(8,128)S(1)}, f32[160,128]{1,0:T(8,128)S(1)}, u32[]{:S(2)}, u32[]{:S(2)}) %collective-permute-start.8) | collective-permute-done | bytes 81952 | tf_op jit(solution)/shard_map/cond/branch_0_fun/ppermute | solution.py:372
  40.4 4.5 %collective-permute-done.2.refs_5_ = f32[512,128]{1,0:T(8,128)S(1)} collective-permute-done((f32[512,128]{1,0:T(8,128)S(1)}, f32[512,128]{1,0:T(8,128)S(1)}, u32[]{:S(2)}, u32[]{:S(2)}) %collective-permute-start.2) | collective-permute-done | bytes 262176 | tf_op jit(solution)/shard_map/cond/branch_0_fun/ppermute | solution.py:372
  44.8 3.0 %products.2 = f32[1024,128]{1,0:T(8,128)} custom-call(s32[8,256]{1,0:T(8,128)S(1)} %get-tuple-element.405.refs_0_, f32[1024,128]{1,0:T(8,128)S(1)} %copy-done.1, f32[1024,128]{1,0:T(8,128)S(1)} %own.2.refs_2_, f32[512,128]{1,0:T(8,128)S(1)} %collective-permute-done.refs_3_, f32[512,128]{1,0:T(8,128)S(1)} %collective-permute-done.1.refs_4_, ...), custom_call_target="tpu_custom_call" | custom-call | tf_op jit(solution)/shard_map/cond/branch_0_fun/products/pallas_call | solution.py:445
  (12 shorter events, 0.3 us)
Async XLA Ops:
  1.7 18.7 %collective-permute-start.18 = (f32[256,128]{1,0:T(8,128)S(1)}, f32[256,128]{1,0:T(8,128)S(1)}, u32[]{:S(2)}, u32[]{:S(2)}) collective-permute-start(f32[256,128]{1,0:T(8,128)S(1)} %get-tuple-element.469), channel_id=1, source_target_pairs={{0,1},{1,0},{2,3},{3,2},{4,5},{5,4},{6,7},{7,6},{8,9},{9,8},{10,11... | collective-permute-start | bytes 393224 | tf_op jit(solution)/shard_map/ppermute | solution.py:372
  2.1 18.3 %collective-permute-start.19 = (f32[256,128]{1,0:T(8,128)S(1)}, f32[256,128]{1,0:T(8,128)S(1)}, u32[]{:S(2)}, u32[]{:S(2)}) collective-permute-start(f32[256,128]{1,0:T(8,128)S(1)} %get-tuple-element.470), channel_id=1, source_target_pairs={{0,4},{1,5},{2,6},{3,7},{4,0},{5,1},{6,2},{7,3},{8,12},{9,13},{10,... | collective-permute-start | bytes 393224 | tf_op jit(solution)/shard_map/ppermute | solution.py:372
  4.7 15.8 %collective-permute-start.20 = (f32[256,128]{1,0:T(8,128)S(1)}, f32[256,128]{1,0:T(8,128)S(1)}, u32[]{:S(2)}, u32[]{:S(2)}) collective-permute-start(f32[256,128]{1,0:T(8,128)S(1)} %get-tuple-element.471), channel_id=1, source_target_pairs={{0,5},{1,4},{2,7},{3,6},{4,1},{5,0},{6,3},{7,2},{8,13},{9,12},{10,... | collective-permute-start | bytes 393224 | tf_op jit(solution)/shard_map/ppermute | solution.py:372
  4.8 13.3 %all-to-all-start.6 = ((s32[32,2,8]{2,1,0:T(2,128)}), s32[32,2,8]{2,1,0:T(2,128)S(1)}, u32[]{:S(2)}, u32[]{:S(2)}) async-start(s32[32,2,8]{2,1,0:T(2,128)} %get-tuple-element.465), calls=%async_computation.6 | async-start | bytes 65536 | tf_op jit(solution)/shard_map/all_to_all | solution.py:413
  20.5 9.5 %copy-start.1 = (f32[1024,128]{1,0:T(8,128)S(1)}, f32[1024,128]{1,0:T(8,128)}, u32[]{:S(2)}) copy-start(f32[1024,128]{1,0:T(8,128)} %get-tuple-element.406.refs_1_) | copy-start | bytes 1572868 | tf_op jit(solution)/shard_map/cond
  21.9 9.1 %collective-permute-start.3 = (f32[192,128]{1,0:T(8,128)S(1)}, f32[192,128]{1,0:T(8,128)S(1)}, u32[]{:S(2)}, u32[]{:S(2)}) collective-permute-start(f32[192,128]{1,0:T(8,128)S(1)} %get-tuple-element.416), channel_id=1, source_target_pairs={{0,8},{8,0},{16,24},{24,16},{1,9},{9,1},{17,25},{25,17},{2,10},{10... | collective-permute-start | bytes 294920 | tf_op jit(solution)/shard_map/cond/branch_0_fun/ppermute | solution.py:372
  22.5 10.5 %collective-permute-start.4 = (f32[192,128]{1,0:T(8,128)S(1)}, f32[192,128]{1,0:T(8,128)S(1)}, u32[]{:S(2)}, u32[]{:S(2)}) collective-permute-start(f32[192,128]{1,0:T(8,128)S(1)} %get-tuple-element.417), channel_id=1, source_target_pairs={{0,16},{8,24},{16,0},{24,8},{1,17},{9,25},{17,1},{25,9},{2,18},{10... | collective-permute-start | bytes 294920 | tf_op jit(solution)/shard_map/cond/branch_0_fun/ppermute | solution.py:372
  23.0 10.0 %collective-permute-start.5 = (f32[192,128]{1,0:T(8,128)S(1)}, f32[192,128]{1,0:T(8,128)S(1)}, u32[]{:S(2)}, u32[]{:S(2)}) collective-permute-start(f32[192,128]{1,0:T(8,128)S(1)} %get-tuple-element.418), channel_id=1, source_target_pairs={{0,24},{8,16},{16,8},{24,0},{1,25},{9,17},{17,9},{25,1},{2,26},{10... | collective-permute-start | bytes 294920 | tf_op jit(solution)/shard_map/cond/branch_0_fun/ppermute | solution.py:372
  30.9 9.5 %collective-permute-start = (f32[512,128]{1,0:T(8,128)S(1)}, f32[512,128]{1,0:T(8,128)S(1)}, u32[]{:S(2)}, u32[]{:S(2)}) collective-permute-start(f32[512,128]{1,0:T(8,128)S(1)} %get-tuple-element.410), channel_id=1, source_target_pairs={{0,1},{1,0},{2,3},{3,2},{4,5},{5,4},{6,7},{7,6},{8,9},{9,8},{10,11... | collective-permute-start | bytes 786440 | tf_op jit(solution)/shard_map/cond/branch_0_fun/ppermute | solution.py:372
  30.9 9.4 %collective-permute-start.1 = (f32[512,128]{1,0:T(8,128)S(1)}, f32[512,128]{1,0:T(8,128)S(1)}, u32[]{:S(2)}, u32[]{:S(2)}) collective-permute-start(f32[512,128]{1,0:T(8,128)S(1)} %get-tuple-element.411), channel_id=1, source_target_pairs={{0,2},{1,3},{2,0},{3,1},{4,6},{5,7},{6,4},{7,5},{8,10},{9,11},{10,... | collective-permute-start | bytes 786440 | tf_op jit(solution)/shard_map/cond/branch_0_fun/ppermute | solution.py:372
  31.0 13.8 %collective-permute-start.2 = (f32[512,128]{1,0:T(8,128)S(1)}, f32[512,128]{1,0:T(8,128)S(1)}, u32[]{:S(2)}, u32[]{:S(2)}) collective-permute-start(f32[512,128]{1,0:T(8,128)S(1)} %get-tuple-element.412), channel_id=1, source_target_pairs={{0,3},{1,2},{2,1},{3,0},{4,7},{5,6},{6,5},{7,4},{8,11},{9,10},{10,... | collective-permute-start | bytes 786440 | tf_op jit(solution)/shard_map/cond/branch_0_fun/ppermute | solution.py:372
  34.1 1.3 %collective-permute-start.6 = (f32[160,128]{1,0:T(8,128)S(1)}, f32[160,128]{1,0:T(8,128)S(1)}, u32[]{:S(2)}, u32[]{:S(2)}) collective-permute-start(f32[160,128]{1,0:T(8,128)S(1)} %get-tuple-element.420), channel_id=1, source_target_pairs={{0,1},{1,0},{2,3},{3,2},{4,5},{5,4},{6,7},{7,6},{8,9},{9,8},{10,11... | collective-permute-start | bytes 245768 | tf_op jit(solution)/shard_map/cond/branch_0_fun/ppermute | solution.py:372
  34.3 5.2 %collective-permute-start.7 = (f32[160,128]{1,0:T(8,128)S(1)}, f32[160,128]{1,0:T(8,128)S(1)}, u32[]{:S(2)}, u32[]{:S(2)}) collective-permute-start(f32[160,128]{1,0:T(8,128)S(1)} %get-tuple-element.421), channel_id=1, source_target_pairs={{0,4},{1,5},{2,6},{3,7},{4,0},{5,1},{6,2},{7,3},{8,12},{9,13},{10,... | collective-permute-start | bytes 245768 | tf_op jit(solution)/shard_map/cond/branch_0_fun/ppermute | solution.py:372
  35.5 4.9 %collective-permute-start.8 = (f32[160,128]{1,0:T(8,128)S(1)}, f32[160,128]{1,0:T(8,128)S(1)}, u32[]{:S(2)}, u32[]{:S(2)}) collective-permute-start(f32[160,128]{1,0:T(8,128)S(1)} %get-tuple-element.422), channel_id=1, source_target_pairs={{0,5},{1,4},{2,7},{3,6},{4,1},{5,0},{6,3},{7,2},{8,13},{9,12},{10,... | collective-permute-start | bytes 245768 | tf_op jit(solution)/shard_map/cond/branch_0_fun/ppermute | solution.py:372
